TPU v7x, 128 devices: a whole 4x4x4 slice. The times are simulated.
128 devices in a mesh: grp: 2 (over y_hi), seq: 64 (over y_lo, x, z, core).
Axes of the slice: x: 4, y: 4 (y_hi: 2, y_lo: 2; y = y_hi * 2 + y_lo), z: 4, core: 2. Of those that a mesh axis runs over, the one named last changes fastest.
Arguments:
- tokens: bfloat16 [16384, 2048], P(('grp', 'seq')), may hold values from -6 to 6
- lengths: int32 [2, 9], P('grp'), may hold values from 2 to 8124, as said below
- norm_gain: bfloat16 [2048], P('seq'), may hold values from 0.099609375 to 1.8984375
- w_query: bfloat16 [2048, 2048], P('seq'), may hold values from -0.125 to 0.125
- w_key: bfloat16 [2048, 2048], P('seq'), may hold values from -0.125 to 0.125
- w_value: bfloat16 [2048, 2048], P('seq'), may hold values from -0.125 to 0.125
- w_out: bfloat16 [2048, 2048], P('seq'), may hold values from -0.375 to 0.375
- mlp_gain: bfloat16 [2048], P('seq'), may hold values from 0.099609375 to 1.8984375
- w_gate: bfloat16 [2048, 5504], P('seq'), may hold values from -0.125 to 0.125
- w_up: bfloat16 [2048, 5504], P('seq'), may hold values from -0.125 to 0.125
- w_down: bfloat16 [5504, 2048], P('seq'), may hold values from -0.078125 to 0.078125
- cotangent: bfloat16 [16384, 2048], P(('grp', 'seq')), may hold values from -6 to 6
Outputs:
- outputs: bfloat16 [16384, 2048], P(('grp', 'seq'))
- input_grad: float32 [16384, 2048], P(('grp', 'seq'))
- gain_grad: float32 [2048], P('seq')
- query_grad: float32 [2048, 2048], P('seq')
- key_grad: float32 [2048, 2048], P('seq')
- value_grad: float32 [2048, 2048], P('seq')
- out_grad: float32 [2048, 2048], P('seq')
- mlp_gain_grad: float32 [2048], P('seq')
- gate_grad: float32 [2048, 5504], P('seq')
- up_grad: float32 [2048, 5504], P('seq')
- down_grad: float32 [5504, 2048], P('seq')
Inputs may be any that keep to these rules, and one draw needn't show every extreme that they name: Each group's 9 lengths sum to 8192; exactly one of them is longer than 128, and that row starts among the first 128 positions and ends among the last 128; each other row has fewer than 16 tokens.
All inputs are finite; a program needn't handle non-finite values.
Results may differ from a plain program's by a relative error of at most 0.017.
Values may be sent and summed in bfloat16 or wider, within the bound.
No kernel may reach another device: no remote copies, remote signals or barrier semaphores. Data moves between devices by JAX's collectives and lax.ppermute only.
A program may use at most 640 MiB of HBM per device.

v0:
```python
import math

import jax
import jax.numpy as jnp
from jax import lax
from jax.sharding import PartitionSpec as P

HEAD = 128
WIN = 64


epsilon = 1e-06


def in_one_piece(arrays, axis, dim, along):
    columns = [a.reshape(*a.shape[:along], -1) for a in arrays]
    both = jnp.concatenate(columns, axis=along)
    filled, at, outs = (lax.all_gather(both, axis, axis=dim, tiled=True), 0, [])
    for a, column in zip(arrays, columns):
        section = filled[..., at : at + column.shape[along]]
        outs.append(section.reshape(*section.shape[:along], *a.shape[along:]))
        at += column.shape[along]
    return tuple(outs)


def from_behind(value, axis, by):
    peers = lax.axis_size(axis)
    pairs = [(i, i + by) for i in range(peers) if 0 <= i + by < peers]
    return lax.ppermute(value, axis, pairs)


def sent_together(arrays, axis, dim, along):
    widths = [math.prod(a.shape[along:]) for a in arrays]
    both = jnp.concatenate(
        [a.reshape(*a.shape[:along], w) for a, w in zip(arrays, widths)], axis=along
    )
    filled = lax.psum_scatter(both, axis, scatter_dimension=dim, tiled=True)
    blocks = jnp.split(filled, [sum(widths[:k]) for k in range(1, len(widths))], axis=along)
    return tuple(
        (b.reshape(*filled.shape[:along], *a.shape[along:]) for a, b in zip(arrays, blocks))
    )


def from_everyone(value, axis):
    peers = lax.axis_size(axis)
    return lax.all_to_all(
        jnp.broadcast_to(value[None], (peers, *value.shape)), axis, 0, 0, tiled=True
    )


def taken_together(value, axis):
    everything = from_everyone(value, axis)
    return jnp.sum(everything.astype(jnp.float32), axis=0)


def inverse_rms(values):
    return lax.rsqrt(jnp.mean(values * values, axis=-1, keepdims=True) + epsilon)


def segment_numbers(positions, lengths):
    row_ends = jnp.cumsum(lengths)
    return jnp.sum((positions[:, None] >= row_ends[None, :]).astype(jnp.int32), axis=1)


def matmul(left, right):
    return jnp.dot(left, right, preferred_element_type=jnp.float32)


def matmul_left_t(left, right):
    return lax.dot_general(
        left, right, (((0,), (0,)), ((), ())), preferred_element_type=jnp.float32
    )


def matmul_right_t(left, right):
    return lax.dot_general(
        left, right, (((1,), (1,)), ((), ())), preferred_element_type=jnp.float32
    )


def norm_backward(grad_normed, inputs, scale_rows, gain):
    weighted = grad_normed * gain
    gain_term = jnp.sum(grad_normed * inputs * scale_rows, axis=0)
    input_term = scale_rows * weighted - inputs * scale_rows**3 * jnp.mean(
        weighted * inputs, axis=-1, keepdims=True
    )
    return (gain_term, input_term)


def window_scores(query_heads, key_heads, allowed, scale_factor):
    scores = (
        jnp.einsum("qhd,khd->hqk", query_heads, key_heads, preferred_element_type=jnp.float32)
        * scale_factor
    )
    return jnp.where(allowed[None], scores, -1e30)


def body(
    tokens,
    lengths,
    norm_gain,
    w_query,
    w_key,
    w_value,
    w_out,
    mlp_gain,
    w_gate,
    w_up,
    w_down,
    cotangent,
):
    local_rows = tokens.shape[0]
    model_width = tokens.shape[1]
    head_count = model_width // HEAD
    scale_factor = HEAD ** (-0.5)
    attn_full = in_one_piece((norm_gain, w_query, w_key, w_value, w_out), "seq", 0, 1)
    mlp_full = (
        *in_one_piece((mlp_gain, w_gate, w_up), "seq", 0, 1),
        lax.all_gather(w_down, "seq", axis=0, tiled=True),
    )
    gain_one = attn_full[0].astype(jnp.float32)
    inputs = tokens.astype(jnp.float32)
    scale_one = inverse_rms(inputs)
    normed = (inputs * scale_one * gain_one).astype(jnp.bfloat16)
    queries = matmul(normed, attn_full[1]).astype(jnp.bfloat16)
    key_rows = matmul(normed, attn_full[2]).astype(jnp.bfloat16)
    value_rows = matmul(normed, attn_full[3]).astype(jnp.bfloat16)
    arrived = from_behind(
        jnp.stack([key_rows[local_rows - WIN :], value_rows[local_rows - WIN :]]), "seq", 1
    )
    all_keys = jnp.concatenate([arrived[0], key_rows], axis=0)
    all_values = jnp.concatenate([arrived[1], value_rows], axis=0)
    first_pos = lax.axis_index("seq") * local_rows
    query_pos = first_pos + jnp.arange(local_rows, dtype=jnp.int32)
    key_pos = first_pos - WIN + jnp.arange(local_rows + WIN, dtype=jnp.int32)
    row_lengths = lengths[0]
    query_segs = segment_numbers(query_pos, row_lengths)
    key_segs = jnp.where(key_pos >= 0, segment_numbers(key_pos, row_lengths), -1)
    distance = query_pos[:, None] - key_pos[None, :]
    allowed = (distance >= 0) & (distance < WIN) & (query_segs[:, None] == key_segs[None, :])
    query_heads = queries.reshape(local_rows, head_count, HEAD)
    key_heads = all_keys.reshape(local_rows + WIN, head_count, HEAD)
    value_heads = all_values.reshape(local_rows + WIN, head_count, HEAD)
    scores = window_scores(query_heads, key_heads, allowed, scale_factor)
    largest = jnp.max(scores, axis=-1, keepdims=True)
    exponents = jnp.exp(scores - largest)
    row_totals = jnp.sum(exponents, axis=-1, keepdims=True)
    log_total = largest + jnp.log(row_totals)
    probs_low = (exponents / row_totals).astype(jnp.bfloat16)
    mixed_heads = jnp.einsum(
        "hqk,khd->qhd", probs_low, value_heads, preferred_element_type=jnp.float32
    )
    mixed_heads = mixed_heads.reshape(local_rows, model_width).astype(jnp.bfloat16)
    hidden_state = inputs + matmul(mixed_heads, attn_full[4])
    gain_two = mlp_full[0].astype(jnp.float32)
    scale_two = inverse_rms(hidden_state)
    normed_again = (hidden_state * scale_two * gain_two).astype(jnp.bfloat16)
    gate_proj = matmul(normed_again, mlp_full[1])
    up_proj = matmul(normed_again, mlp_full[2])
    sigmoid_gate = jax.nn.sigmoid(gate_proj)
    silu_gate = gate_proj * sigmoid_gate
    activated = (silu_gate * up_proj).astype(jnp.bfloat16)
    outputs = (hidden_state + matmul(activated, mlp_full[3])).astype(jnp.bfloat16)
    upstream = cotangent.astype(jnp.float32)
    down_term = matmul_left_t(activated, cotangent)
    grad_act = matmul_right_t(cotangent, mlp_full[3])
    grad_gate = (
        grad_act * up_proj * sigmoid_gate * (1.0 + gate_proj * (1.0 - sigmoid_gate))
    ).astype(jnp.bfloat16)
    grad_up = (grad_act * silu_gate).astype(jnp.bfloat16)
    gate_term = matmul_left_t(normed_again, grad_gate)
    up_term = matmul_left_t(normed_again, grad_up)
    grad_norm_two = matmul_right_t(grad_gate, mlp_full[1]) + matmul_right_t(grad_up, mlp_full[2])
    gain_two_term, through_second = norm_backward(grad_norm_two, hidden_state, scale_two, gain_two)
    grad_hidden = upstream + through_second
    mlp_shards = (
        lax.psum_scatter(gain_two_term, "seq", scatter_dimension=0, tiled=True),
        lax.psum_scatter(gate_term, "seq", scatter_dimension=0, tiled=True),
        lax.psum_scatter(up_term, "seq", scatter_dimension=0, tiled=True),
        lax.psum_scatter(down_term, "seq", scatter_dimension=0, tiled=True),
    )
    hidden_low = grad_hidden.astype(jnp.bfloat16)
    out_term = matmul_left_t(mixed_heads, hidden_low)
    grad_mixed = (
        matmul_right_t(hidden_low, attn_full[4])
        .astype(jnp.bfloat16)
        .reshape(local_rows, head_count, HEAD)
    )
    scores_again = window_scores(query_heads, key_heads, allowed, scale_factor)
    probabilities = jnp.exp(scores_again - log_total)
    grad_probs = jnp.einsum(
        "qhd,khd->hqk", grad_mixed, value_heads, preferred_element_type=jnp.float32
    )
    row_inner = jnp.sum(probabilities * grad_probs, axis=-1, keepdims=True)
    grad_scores = (probabilities * (grad_probs - row_inner)).astype(jnp.bfloat16)
    grad_queries = (
        jnp.einsum("hqk,khd->qhd", grad_scores, key_heads, preferred_element_type=jnp.float32)
        * scale_factor
    )
    grad_queries = grad_queries.reshape(local_rows, model_width).astype(jnp.bfloat16)
    grad_keys_all = (
        jnp.einsum("hqk,qhd->khd", grad_scores, query_heads, preferred_element_type=jnp.float32)
        * scale_factor
    )
    grad_keys_all = grad_keys_all.reshape(local_rows + WIN, model_width)
    grad_values_all = jnp.einsum(
        "hqk,qhd->khd", probs_low, grad_mixed, preferred_element_type=jnp.float32
    )
    grad_values_all = grad_values_all.reshape(local_rows + WIN, model_width)
    returned = from_behind(
        jnp.stack([grad_keys_all[:WIN], grad_values_all[:WIN]]).astype(jnp.bfloat16), "seq", -1
    ).astype(jnp.float32)
    grad_keys = jnp.concatenate(
        [grad_keys_all[WIN:local_rows], grad_keys_all[local_rows:] + returned[0]], axis=0
    ).astype(jnp.bfloat16)
    grad_values = jnp.concatenate(
        [grad_values_all[WIN:local_rows], grad_values_all[local_rows:] + returned[1]], axis=0
    ).astype(jnp.bfloat16)
    query_term = matmul_left_t(normed, grad_queries)
    key_term = matmul_left_t(normed, grad_keys)
    value_term = matmul_left_t(normed, grad_values)
    grad_norm_one = (
        matmul_right_t(grad_queries, attn_full[1])
        + matmul_right_t(grad_keys, attn_full[2])
        + matmul_right_t(grad_values, attn_full[3])
    )
    gain_one_term, through_first = norm_backward(grad_norm_one, inputs, scale_one, gain_one)
    input_grad = grad_hidden + through_first
    attn_shards = sent_together(
        (gain_one_term, query_term, key_term, value_term, out_term), "seq", 0, 1
    )
    totals = (
        taken_together(attn_shards[0].astype(jnp.bfloat16), "grp").astype(jnp.float32),
        taken_together(attn_shards[1].astype(jnp.bfloat16), "grp").astype(jnp.float32),
        taken_together(attn_shards[2].astype(jnp.bfloat16), "grp").astype(jnp.float32),
        taken_together(attn_shards[3].astype(jnp.bfloat16), "grp").astype(jnp.float32),
        taken_together(attn_shards[4].astype(jnp.bfloat16), "grp").astype(jnp.float32),
        taken_together(mlp_shards[0].astype(jnp.bfloat16), "grp").astype(jnp.float32),
        taken_together(mlp_shards[1].astype(jnp.bfloat16), "grp").astype(jnp.float32),
        taken_together(mlp_shards[2].astype(jnp.bfloat16), "grp").astype(jnp.float32),
        taken_together(mlp_shards[3].astype(jnp.bfloat16), "grp").astype(jnp.float32),
    )
    return (
        outputs,
        input_grad,
        totals[0],
        totals[1],
        totals[2],
        totals[3],
        totals[4],
        totals[5],
        totals[6],
        totals[7],
        totals[8],
    )


def solution(mesh):
    placed = (
        P(("grp", "seq"), None),
        P("grp", None),
        P("seq"),
        P("seq", None),
        P("seq", None),
        P("seq", None),
        P("seq", None),
        P("seq"),
        P("seq", None),
        P("seq", None),
        P("seq", None),
        P(("grp", "seq"), None),
    )
    return jax.shard_map(
        body,
        mesh=mesh,
        in_specs=placed,
        out_specs=(
            P(("grp", "seq"), None),
            P(("grp", "seq"), None),
            P("seq"),
            P("seq", None),
            P("seq", None),
            P("seq", None),
            P("seq", None),
            P("seq"),
            P("seq", None),
            P("seq", None),
            P("seq", None),
        ),
        check_vma=False,
    )
```

profile of v0, /device:TPU:8, one launch (start us, length us, event | category | flops | bytes accessed | tf_op | source)
XLA Modules:
  0.0 1993.5 jit_solution(15787622799095960540)
XLA Ops:
  15.3 131.3 %all-gather.9.cloned.1.call-done = bf16[64,86,2048]{2,1,0:T(8,128)(2,1)} async-done(((bf16[1,86,2048]{2,1,0:T(8,128)(2,1)}), bf16[64,86,2048]{2,1,0:T(8,128)(2,1)}) %all-gather.9.cloned.1.call-update) | async-done | bytes 22544400 | tf_op jit(solution)/shard_map/all_gather | solution.py:119
  146.7 22.8 %reshape.261 = bf16[5504,2048]{1,0:T(8,128)(2,1)} reshape(bf16[64,86,2048]{2,1,0:T(8,128)(2,1)} %all-gather.9.cloned.1.call-done) | data formatting | bytes 45088768
  169.4 13.5 fusion.102
  182.9 155.4 %all-gather.5.cloned.1.call-done = bf16[2048,8193]{1,0:T(8,128)(2,1)} async-done(((bf16[32,8193]{1,0:T(8,128)(2,1)}), bf16[2048,8193]{1,0:T(8,128)(2,1)}) %all-gather.5.cloned.1.call-update) | async-done | bytes 33558544 | tf_op jit(solution)/shard_map/all_gather | solution.py:18
  354.6 6.5 fusion.56
  370.2 7.1 multiply_reduce_fusion.3
  377.4 215.9 %all-gather.7.cloned.1.call-done = bf16[2048,11009]{1,0:T(8,128)(2,1)} async-done(((bf16[32,11009]{1,0:T(8,128)(2,1)}), bf16[2048,11009]{1,0:T(8,128)(2,1)}) %all-gather.7.cloned.1.call-update) | async-done | bytes 45092880 | tf_op jit(solution)/shard_map/all_gather | solution.py:18
  594.7 16.6 fusion.3
  611.3 14.7 multiply_convert_fusion.1
  627.2 17.3 fusion.103
  644.8 19.4 fusion.104
  664.3 14.5 fusion.1
  678.8 14.8 multiply_reduce_fusion.1
  695.2 7.4 fusion.53
  715.9 10.4 collective-permute-start.1
  726.9 8.3 fusion.92
  735.2 8.1 fusion.81
  743.3 8.0 fusion.13
  752.8 8.3 fusion.79
  761.1 8.4 fusion.80
  769.5 7.1 fusion.29
  776.7 8.3 fusion.67
  784.9 173.4 %concatenate.43 = f32[2048,8193]{0,1:T(8,128)} concatenate(f32[2048,1]{0,1:T(1,128)S(1)} %bitcast.133, f32[2048,2048]{0,1:T(8,128)} %fusion.92, f32[2048,2048]{0,1:T(8,128)} %fusion.80, f32[2048,2048]{0,1:T(8,128)} %fusion.79, f32[2048,2048]{0,1:T(8,128)} %fusion.81), dimensions={1} | concatenate | bytes 134234112 | tf_op jit(solution)/shard_map/concatenate | solution.py:34
  958.3 65.1 %copy.143 = f32[2048,8193]{1,0:T(8,128)} copy(f32[2048,8193]{0,1:T(8,128)} %concatenate.43) | data formatting | bytes 134234112
  1024.8 18.2 fusion.105
  1043.0 484.2 %fusion = f32[88,2048]{1,0:T(8,128)S(1)} fusion(f32[5504,2048]{1,0:T(8,128)} %fusion.105), kind=kCustom, calls=%all-reduce-scatter | all-reduce-scatter fusion | flops 11534337 | bytes 45810176
  1535.7 149.3 %all-reduce = bf16[2048]{0:T(1024)(128)(2,1)S(1)} all-reduce(f32[2048]{0:T(1024)S(1)} %copy-done.28), channel_id=3, replica_groups=mesh['grp'=2,'seq'=64] {'seq'}, use_global_device_ids=true, to_apply=%region_18.19.clone | all-reduce | flops 2048 | bytes 12288
  1689.9 7.3 concatenate.44
  1704.0 11.7 fusion.50
  1729.2 186.2 %reduce-scatter.12.cloned.1.call-done = f32[32,8193]{1,0:T(8,128)} async-done(((f32[2048,8193]{1,0:T(8,128)}), f32[32,8193]{1,0:T(8,128)}) %reduce-scatter.12.cloned.1.call-update) | async-done | bytes 1048720
  1924.2 7.4 all-to-all-done.7
  1957.0 6.3 all-to-all-done.3
  (185 shorter events, 143.9 us)
Async XLA Ops:
  7.2 139.5 %all-gather.9.cloned.1.call-start = ((), (), s32[]{:S(2)}) async-start(), calls=%async_computation.16 | async-start | bytes 23429120 | tf_op jit(solution)/shard_map/all_gather | solution.py:119
  7.9 330.4 %all-gather.5.cloned.1.call-start = ((), (), s32[]{:S(2)}) async-start(), calls=%async_computation.12 | async-start | bytes 34611200 | tf_op jit(solution)/shard_map/all_gather | solution.py:18
  10.9 582.4 %all-gather.7.cloned.1.call-start = ((), (), s32[]{:S(2)}) async-start(), calls=%async_computation.13 | async-start | bytes 46325760 | tf_op jit(solution)/shard_map/all_gather | solution.py:18
  14.0 1702.2 %reduce-scatter.8.cloned.1.call-start = ((), (), s32[]{:S(2)}) async-start(), calls=%async_computation.14 | async-start | bytes 45793280 | tf_op jit(solution)/shard_map/reduce_scatter | solution.py:178
  15.3 154.1 %copy-start.9 = (bf16[128,2048]{1,0:T(8,128)(2,1)S(1)}, bf16[128,2048]{1,0:T(8,128)(2,1)}, u32[]{:S(2)}) copy-start(bf16[128,2048]{1,0:T(8,128)(2,1)} %param.23) | copy-start | bytes 1572868
  352.3 14.7 collective-permute-start
  377.3 301.4 %copy-start.3 = (f32[128,2048]{1,0:T(8,128)}, f32[128,2048]{1,0:T(8,128)S(1)}, u32[]{:S(2)}) copy-start(f32[128,2048]{1,0:T(8,128)S(1)} %get-tuple-element.39) | copy-start | bytes 3145732
  594.7 31.4 %copy-start.12 = (bf16[128,2048]{1,0:T(8,128)(2,1)}, bf16[128,2048]{1,0:T(8,128)(2,1)S(1)}, u32[]{:S(2)}) copy-start(bf16[128,2048]{1,0:T(8,128)(2,1)S(1)} %multiply_convert_fusion.4) | copy-start | bytes 1572868
  594.7 16.6 copy-start.15
  644.6 1083.4 %reduce-scatter.10.cloned.1.call-start = ((), (), s32[]{:S(2)}) async-start(), calls=%async_computation.15 | async-start | bytes 45793280 | tf_op jit(solution)/shard_map/reduce_scatter | solution.py:179
  664.2 1251.1 %reduce-scatter.12.cloned.1.call-start = ((), (), s32[]{:S(2)}) async-start(), calls=%async_computation.17 | async-start | bytes 69222400
  695.2 40.1 %copy-start.1 = (f32[128,2048]{1,0:T(8,128)}, f32[128,2048]{1,0:T(8,128)S(1)}, u32[]{:S(2)}) copy-start(f32[128,2048]{1,0:T(8,128)S(1)} %subtract_add_fusion) | copy-start | bytes 3145732
  709.9 16.5 copy-start.14
  711.4 15.0 copy-start.8
  715.9 35.4 %collective-permute-start.1 = (bf16[2,64,2048]{2,1,0:T(8,128)(2,1)S(1)}, bf16[2,64,2048]{2,1,0:T(8,128)(2,1)S(1)}, u32[]{:S(2)}, u32[]{:S(2)}) collective-permute-start(bf16[2,64,2048]{2,1,0:T(8,128)(2,1)S(1)} %pad_maximum_fusion.1), channel_id=1, source_target_pairs={{1,0},{2,1},{3,2},{4,3},{5,4},{6,5},{7,6},{8,7},{9,8},{10,9},{11,1... | collective-permute-start | bytes 1572872 | tf_op jit(solution)/shard_map/ppermute | solution.py:29
  1043.0 490.8 %copy-start.29 = (u32[128]{0:T(128)S(1)}, u32[128]{0:T(128)}, u32[]{:S(2)}) copy-start(u32[128]{0:T(128)} %constant.53) | copy-start | bytes 1540
  1043.0 492.7 %copy-start.28 = (f32[2048]{0:T(1024)S(1)}, f32[2048]{0:T(1024)}, u32[]{:S(2)}) copy-start(f32[2048]{0:T(1024)} %get-tuple-element.11) | copy-start | bytes 24580
  1528.1 175.9 %copy-start.4 = (f32[128,2048]{1,0:T(8,128)S(1)}, f32[128,2048]{1,0:T(8,128)}, u32[]{:S(2)}) copy-start(f32[128,2048]{1,0:T(8,128)} %copy-done.3) | copy-start | bytes 3145732
  1528.1 161.8 %collective-permute-start.2 = (bf16[88,2048]{1,0:T(8,128)(2,1)S(1)}, bf16[88,2048]{1,0:T(8,128)(2,1)}, u32[]{:S(2)}, u32[]{:S(2)}) collective-permute-start(bf16[88,2048]{1,0:T(8,128)(2,1)S(1)} %convert.38), channel_id=1, source_target_pairs={{0,1},{1,2},{2,3},{3,4},{4,5},{5,6},{6,7},{7,8},{8,9},{9,10},{10,1... | collective-permute-start | bytes 1081352
  1531.9 158.0 %collective-permute-start.3 = (bf16[38,2048]{1,0:T(8,128)(2,1)}, bf16[38,2048]{1,0:T(8,128)(2,1)S(1)}, u32[]{:S(2)}, u32[]{:S(2)}) collective-permute-start(bf16[38,2048]{1,0:T(8,128)(2,1)} %slice.122), channel_id=1, source_target_pairs={{0,2},{1,3},{2,4},{3,5},{4,6},{5,7},{6,8},{7,9},{8,10},{9,11},{10,... | collective-permute-start | bytes 466952
  1685.6 12.7 all-to-all-start.5
  1699.2 18.2 all-to-all-start.8
  1718.3 199.6 %all-to-all-start.6 = ((bf16[2,32,5504]{2,1,0:T(8,128)(2,1)}), bf16[2,32,5504]{2,1,0:T(8,128)(2,1)S(1)}, u32[]{:S(2)}, u32[]{:S(2)}) async-start(bf16[2,32,5504]{2,1,0:T(8,128)(2,1)} %broadcast_in_dim.47), calls=%async_computation.7 | async-start | bytes 1409024 | tf_op jit(solution)/shard_map/all_to_all | solution.py:46
  1918.8 12.8 all-to-all-start.7
  1924.2 21.6 %copy-start.20 = (bf16[32,2048]{0,1:T(8,128)(2,1)S(1)}, bf16[32,2048]{0,1:T(8,128)(2,1)}, u32[]{:S(2)}) copy-start(bf16[32,2048]{0,1:T(8,128)(2,1)} %get-tuple-element.19) | copy-start | bytes 393220
  1932.2 8.4 all-to-all-start
  1936.6 20.0 %copy-start.19 = (bf16[32,2048]{0,1:T(8,128)(2,1)S(1)}, bf16[32,2048]{0,1:T(8,128)(2,1)}, u32[]{:S(2)}) copy-start(bf16[32,2048]{0,1:T(8,128)(2,1)} %get-tuple-element.20) | copy-start | bytes 393220
  1941.3 15.6 copy-start.18
  1941.3 10.2 all-to-all-start.4
  1952.2 11.1 all-to-all-start.3
  1964.1 10.8 all-to-all-start.2
  1975.6 10.1 all-to-all-start.1
  (19 other events, 100.1 us)
Sparse Core Ops, SparseCore 0:
  9.7 136.8 all-gather.8
  148.9 189.3 all-gather.4
  340.6 252.6 all-gather.6
  644.7 365.1 reduce-scatter.7
  1012.3 477.1 reduce-scatter.9
  1491.8 423.4 reduce-scatter.11
where the time goes:
time: 2010 us; the launch traced here: 1990 us
  waiting for transfers between devices  730 us (36%)
  blocking collectives  633 us (31%)
  local copies, waits for them, and re-layouts  303 us (15%)
  matrix products  237 us (12%)
  starting transfers between devices  51.8 us (3%)
  other arithmetic  21.7 us (1%)
    unnamed x2, blocking collectives  633 us
    all_gather x2, waiting for transfers between devices, in_one_piece(): filled, at, outs = (lax.all_gather(both, axis, axis=dim, tiled=True), 0, [])  371 us
    unnamed x9, waiting for transfers between devices  187 us
    concatenate x1, local copies, waits for them, and re-layouts, sent_together(): jnp.concatenate([a.reshape(*a.shape[:along], w) for a, w in zip(arrays, w...  173 us
    all_gather x1, waiting for transfers between devices, body(): lax.all_gather(w_down, 'seq', axis=0, tiled=True)  131 us
    unnamed x78, local copies, waits for them, and re-layouts  106 us
    dot_general x7, matrix products, matmul_left_t(): lax.dot_general(left, right, (((0,), (0,)), ((), ())), preferred_element_...  88.1 us
    dot_general x7, matrix products, matmul_right_t(): lax.dot_general(left, right, (((1,), (1,)), ((), ())), preferred_element_...  73.5 us
  transfers between devices with their start and end apart: 19, of which 11 were waited for; matrix products, arithmetic and copies ran while one was open for 49% of the time, Pallas kernels for 0%

commit v1 on v0

v1 whole, which is shorter than its diff:
```python
import functools

import jax
import jax.numpy as jnp
from jax import lax
from jax.experimental import pallas as pl
from jax.experimental.pallas import tpu as pltpu
from jax.sharding import Mesh
from jax.sharding import PartitionSpec as P

HEAD = 128
WIN = 64
BLOCK = 128
epsilon = 1e-06

TEAM = ("z", "c")
FLEET = ("yl", "x")
SEQ = ("yl", "x", "z", "c")
ALL = ("g", "yl", "x", "z", "c")
N_Z, N_C, N_TEAM, N_FLEET = 4, 2, 8, 8
SCALE = HEAD ** (-0.5)
low = jnp.bfloat16
full = jnp.float32


def from_ahead(value, axis, by):
    n = lax.axis_size(axis)
    return lax.ppermute(value, axis, [((i + by) % n, i) for i in range(n)])


def along_line(value, by):
    return lax.ppermute(
        value, FLEET, [(i, i + by) for i in range(N_FLEET) if 0 <= i + by < N_FLEET]
    )


def swapped(value):
    return lax.ppermute(
        value, SEQ, [(N_TEAM * f + t, N_TEAM * t + f) for f in range(N_FLEET) for t in range(N_TEAM)]
    )


def team_gather(value):
    mine = jnp.concatenate([value] + [from_ahead(value, "z", k) for k in range(1, N_Z)], axis=0)
    return jnp.concatenate([mine, from_ahead(mine, "c", 1)], axis=0)


def team_scatter(parts):
    rows = parts.shape[0] // N_TEAM
    half = N_Z * rows
    there = from_ahead(parts[half:].astype(low), "c", 1)
    pair = parts[:half].astype(full) + there.astype(full)
    total = pair[:rows]
    for k in range(1, N_Z):
        total = total + from_ahead(pair[k * rows : (k + 1) * rows].astype(low), "z", -k).astype(full)
    return total


def inverse_rms(values):
    return lax.rsqrt(jnp.mean(values * values, axis=-1, keepdims=True) + epsilon)


def matmul(left, right):
    return jnp.dot(left, right, preferred_element_type=full)


def matmul_left_t(left, right):
    return lax.dot_general(left, right, (((0,), (0,)), ((), ())), preferred_element_type=full)


def matmul_right_t(left, right):
    return lax.dot_general(left, right, (((1,), (1,)), ((), ())), preferred_element_type=full)


def segment_numbers(positions, lengths):
    row_ends = jnp.cumsum(lengths)
    return jnp.sum((positions[..., None] >= row_ends).astype(jnp.int32), axis=-1)


def probabilities(query, keys, mask):
    scores = matmul_right_t(query, keys) * SCALE
    scores = jnp.where(mask > 0, scores, -1e30)
    weights = jnp.exp(scores - jnp.max(scores, axis=-1, keepdims=True))
    return weights / jnp.sum(weights, axis=-1, keepdims=True)


def attend_kernel(place, q_ref, k_ref, v_ref, kp_ref, vp_ref, mask_ref, out_ref):
    mask = mask_ref[0]
    for head in range(q_ref.shape[1] // HEAD):
        at = slice(head * HEAD, (head + 1) * HEAD)
        keys = jnp.concatenate([kp_ref[:, at], k_ref[:, at]], axis=0)
        values = jnp.concatenate([vp_ref[:, at], v_ref[:, at]], axis=0)
        probs = probabilities(q_ref[:, at], keys, mask)
        out_ref[:, at] = matmul(probs.astype(low), values).astype(low)


def attend_back_kernel(
    place, q_ref, k_ref, v_ref, kp_ref, vp_ref, mask_ref, gm_ref, grads_ref, tail_ref, halo_ref, carry
):
    step = pl.program_id(0)
    mask = mask_ref[0]
    wide = q_ref.shape[1]

    @pl.when(step == 0)
    def _():
        carry[...] = jnp.zeros_like(carry)

    for head in range(wide // HEAD):
        at = slice(head * HEAD, (head + 1) * HEAD)
        query = q_ref[:, at]
        keys = jnp.concatenate([kp_ref[:, at], k_ref[:, at]], axis=0)
        values = jnp.concatenate([vp_ref[:, at], v_ref[:, at]], axis=0)
        grad_mixed = gm_ref[:, at]
        probs = probabilities(query, keys, mask)
        grad_probs = matmul_right_t(grad_mixed, values)
        inner = jnp.sum(probs * grad_probs, axis=-1, keepdims=True)
        grad_scores = (probs * (grad_probs - inner)).astype(low)
        grads_ref[:, at] = (matmul(grad_scores, keys) * SCALE).astype(low)
        grad_keys = matmul_left_t(grad_scores, query) * SCALE
        grad_values = matmul_left_t(probs.astype(low), grad_mixed)
        for which, grad in ((0, grad_keys), (1, grad_values)):
            col = which * wide + head * HEAD
            here = slice(col, col + HEAD)
            there = slice(wide + col, wide + col + HEAD)
            last = grad[BLOCK:] + carry[:, here]
            grads_ref[: BLOCK - WIN, there] = grad[WIN:BLOCK].astype(low)
            grads_ref[BLOCK - WIN :, there] = last.astype(low)

            @pl.when(step == 0)
            def _(last=last, here=here):
                tail_ref[:, here] = last

            carry[:, here] = grad[:WIN]

    @pl.when(step == N_TEAM - 1)
    def _():
        halo_ref[...] = carry[...].astype(low)


def attention_specs(wide):
    def block(rows, column, first):
        return pl.BlockSpec((rows, wide), lambda s, place: (place[first + s], column))

    return [
        block(BLOCK, 0, 0),
        block(BLOCK, 1, 0),
        block(BLOCK, 2, 0),
        block(WIN, 1, N_TEAM),
        block(WIN, 2, N_TEAM),
        pl.BlockSpec((1, BLOCK, BLOCK + WIN), lambda s, place: (place[s], 0, 0)),
    ]


def attend(place, qkv, mask):
    wide = qkv.shape[1] // 3
    return pl.pallas_call(
        attend_kernel,
        grid_spec=pltpu.PrefetchScalarGridSpec(
            num_scalar_prefetch=1,
            grid=(N_TEAM,),
            in_specs=attention_specs(wide),
            out_specs=pl.BlockSpec((BLOCK, wide), lambda s, place: (place[s], 0)),
        ),
        out_shape=jax.ShapeDtypeStruct((N_TEAM * BLOCK, wide), low),
        compiler_params=pltpu.CompilerParams(vmem_limit_bytes=16 << 20),
    )(place, qkv, qkv, qkv, qkv, qkv, mask)


def attend_back(place, qkv, mask, grad_mixed):
    wide = qkv.shape[1] // 3
    flip = lambda spec: pl.BlockSpec(
        spec.block_shape, lambda s, place: spec.index_map(N_TEAM - 1 - s, place)
    )
    by_block = lambda width: pl.BlockSpec((BLOCK, width), lambda s, place: (place[N_TEAM - 1 - s], 0))
    once = pl.BlockSpec((WIN, 2 * wide), lambda s, place: (0, 0))
    return pl.pallas_call(
        attend_back_kernel,
        grid_spec=pltpu.PrefetchScalarGridSpec(
            num_scalar_prefetch=1,
            grid=(N_TEAM,),
            in_specs=[flip(spec) for spec in attention_specs(wide)] + [by_block(wide)],
            out_specs=[by_block(3 * wide), once, once],
            scratch_shapes=[pltpu.VMEM((WIN, 2 * wide), full)],
        ),
        out_shape=[
            jax.ShapeDtypeStruct((N_TEAM * BLOCK, 3 * wide), low),
            jax.ShapeDtypeStruct((WIN, 2 * wide), full),
            jax.ShapeDtypeStruct((WIN, 2 * wide), low),
        ],
        compiler_params=pltpu.CompilerParams(vmem_limit_bytes=16 << 20),
    )(place, qkv, qkv, qkv, qkv, qkv, mask, grad_mixed)


def norm_backward(grad_normed, inputs, scale_rows, gain):
    weighted = grad_normed * gain
    gain_term = jnp.sum(grad_normed * inputs * scale_rows, axis=0)
    input_term = scale_rows * weighted - inputs * scale_rows**3 * jnp.mean(
        weighted * inputs, axis=-1, keepdims=True
    )
    return (gain_term, input_term)


def fleet_reduce(terms):
    return lax.psum_scatter(terms.astype(low), (*FLEET, "g"), scatter_dimension=0, tiled=True)


def body(
    tokens, lengths, norm_gain, w_query, w_key, w_value, w_out, mlp_gain, w_gate, w_up, w_down, cotangent
):
    rows, width = tokens.shape
    shard = w_query.shape[0]
    team_wide = width // N_TEAM
    unit_rows = w_down.shape[0]
    unit_pad = -(-unit_rows // 32) * 32
    units = N_FLEET * unit_pad
    z, c = lax.axis_index("z"), lax.axis_index("c")
    fleet = lax.axis_index(FLEET)

    gains = lax.all_gather(jnp.concatenate([norm_gain, mlp_gain])[None], SEQ, axis=0, tiled=True)
    gain_one = gains[:, :shard].reshape(width).astype(full)
    gain_two = gains[:, shard:].reshape(width).astype(full)
    out_there = swapped(w_out)
    qkv_cut = jnp.stack([w_query, w_key, w_value], axis=1).reshape(shard, 3, N_TEAM, team_wide)
    qkv_cut = qkv_cut.transpose(2, 0, 1, 3).reshape(N_TEAM, shard, 3 * team_wide)
    qkv_cut = lax.all_to_all(qkv_cut, TEAM, 0, 0, tiled=True).reshape(N_TEAM * shard, 3 * team_wide)
    out_cut = out_there.reshape(shard, N_TEAM, team_wide).transpose(1, 0, 2)
    out_cut = out_cut.reshape(N_TEAM * shard, team_wide)
    attn = lax.all_gather(jnp.concatenate([qkv_cut, out_cut], axis=1), FLEET, axis=0, tiled=True)
    w_qkv = attn[:, : 3 * team_wide]
    w_out_team = attn[:, 3 * team_wide :].reshape(N_FLEET, N_TEAM, shard, team_wide)
    w_out_team = w_out_team.transpose(0, 2, 1, 3).reshape(N_FLEET * shard, width)

    def units_cut(weight):
        cut = weight.reshape(shard, N_FLEET, N_TEAM, unit_rows)
        cut = jnp.pad(cut, ((0, 0), (0, 0), (0, 0), (0, unit_pad - unit_rows)))
        return cut.transpose(2, 0, 1, 3).reshape(N_TEAM, shard, units)

    gate_up_cut = jnp.concatenate([units_cut(w_gate), units_cut(w_up)], axis=2)
    gate_up_cut = lax.all_to_all(gate_up_cut, TEAM, 0, 0, tiled=True)
    w_gate_up = lax.all_gather(
        gate_up_cut.reshape(N_TEAM * shard, 2 * units), FLEET, axis=0, tiled=True
    )
    down_cut = jnp.pad(w_down, ((0, unit_pad - unit_rows), (0, 0)))
    w_down_team = lax.all_gather(down_cut, FLEET, axis=0, tiled=True)

    order = jnp.arange(N_TEAM, dtype=jnp.int32)
    spot = (jnp.bitwise_xor(order % N_C, c) * N_Z + (order // N_C - z) % N_Z).astype(jnp.int32)
    before = jnp.concatenate([jnp.full((1,), 2 * N_TEAM, jnp.int32), 2 * spot[:-1] + 1])
    place = jnp.concatenate([spot, before])
    last_at = spot[N_TEAM - 1] * BLOCK + BLOCK - WIN
    kept = jnp.arange(N_TEAM, dtype=jnp.int32)
    kept_block = N_C * ((kept % N_Z + z) % N_Z) + jnp.bitwise_xor(kept // N_Z, c)
    first_pos = (fleet * N_TEAM + kept_block) * BLOCK
    query_pos = first_pos[:, None] + jnp.arange(BLOCK, dtype=jnp.int32)
    key_pos = first_pos[:, None] - WIN + jnp.arange(BLOCK + WIN, dtype=jnp.int32)
    query_segs = segment_numbers(query_pos, lengths[0])
    key_segs = jnp.where(key_pos >= 0, segment_numbers(key_pos, lengths[0]), -1)
    distance = query_pos[:, :, None] - key_pos[:, None, :]
    mask = (distance >= 0) & (distance < WIN) & (query_segs[:, :, None] == key_segs[:, None, :])
    mask = mask.astype(full)

    token_rows = team_gather(tokens)
    halo = along_line(lax.dynamic_slice_in_dim(token_rows, last_at, WIN, 0), 1)
    token_rows = jnp.concatenate([token_rows, halo], axis=0).astype(full)
    normed = (token_rows * inverse_rms(token_rows) * gain_one).astype(low)
    qkv = matmul(normed, w_qkv).astype(low)
    mixed = attend(place, qkv, mask)
    inputs = tokens.astype(full)
    hidden = inputs + team_scatter(matmul(mixed, w_out_team))

    cotangents = team_gather(cotangent)
    scale_two = inverse_rms(hidden)
    again = team_gather((hidden * scale_two * gain_two).astype(low))
    both = matmul(again, w_gate_up)
    gate, up = both[:, :units], both[:, units:]
    sigmoid = jax.nn.sigmoid(gate)
    silu = gate * sigmoid
    activated = (silu * up).astype(low)
    grad_act = matmul_right_t(cotangents, w_down_team)
    grad_gate = (grad_act * up * sigmoid * (1.0 + gate * (1.0 - sigmoid))).astype(low)
    grad_up = (grad_act * silu).astype(low)
    grad_both = jnp.concatenate([grad_gate, grad_up], axis=1)
    grad_again = team_scatter(matmul_right_t(grad_both, w_gate_up))
    down_sum = fleet_reduce(matmul_left_t(activated, cotangents))
    pair_rows = shard // 2
    gate_up_term = matmul_left_t(again, grad_both).astype(low)
    gate_up_term = gate_up_term.reshape(N_FLEET, N_TEAM, 2, pair_rows, 2 * units)
    gate_up_term = gate_up_term.transpose(0, 2, 1, 3, 4).reshape(width, 2 * units)
    gate_up_sum = fleet_reduce(gate_up_term)

    gain_two_term, through_second = norm_backward(grad_again, hidden, scale_two, gain_two)
    grad_hidden = cotangent.astype(full) + through_second
    hidden_low = team_gather(grad_hidden.astype(low))
    outputs = (hidden + team_scatter(matmul(activated, w_down_team))).astype(low)

    grad_mixed = matmul_right_t(hidden_low, w_out_team).astype(low)
    grad_qkv, tail, halo_grads = attend_back(place, qkv, mask, grad_mixed)
    tail = tail + along_line(halo_grads, -1).astype(full)
    grad_qkv = lax.dynamic_update_slice(grad_qkv, tail.astype(low), (last_at, team_wide))
    out_term = matmul_left_t(mixed, hidden_low)
    grad_normed = team_scatter(matmul_right_t(grad_qkv, w_qkv))
    qkv_term = matmul_left_t(normed[: N_TEAM * BLOCK], grad_qkv).astype(low)
    qkv_term = qkv_term.reshape(N_FLEET, N_TEAM, 2, pair_rows, 3 * team_wide)
    qkv_term = qkv_term.transpose(0, 2, 1, 3, 4).reshape(width, 3 * team_wide)
    out_term = out_term.astype(low).reshape(N_FLEET, 2, pair_rows, N_TEAM, team_wide)
    out_term = out_term.transpose(0, 1, 3, 2, 4).reshape(width, team_wide)
    attn_sum = fleet_reduce(jnp.concatenate([qkv_term, out_term], axis=1))
    gain_one_term, through_first = norm_backward(grad_normed, inputs, inverse_rms(inputs), gain_one)
    input_grad = grad_hidden + through_first

    mine = lax.axis_index("g") == 0

    def both_halves(value):
        other = from_ahead(value, "g", 1)
        return jnp.concatenate(
            [jnp.where(mine, value, other), jnp.where(mine, other, value)], axis=-2
        )

    def to_owners(sums, blocks):
        sums = lax.all_to_all(sums.reshape(N_TEAM, pair_rows, sums.shape[1]), TEAM, 0, 0, tiled=True)
        sums = both_halves(sums)
        return jnp.split(sums, blocks, axis=2)

    def columns(block):
        return block.transpose(1, 0, 2).reshape(shard, width).astype(full)

    def unit_columns(block):
        block = block.reshape(N_TEAM, shard, N_FLEET, unit_pad)[..., :unit_rows]
        return block.transpose(1, 2, 0, 3).reshape(shard, N_FLEET * N_TEAM * unit_rows).astype(full)

    gate_cols, up_cols = to_owners(gate_up_sum, 2)
    down_grad = both_halves(down_sum)[:unit_rows].astype(full)
    query_cols, key_cols, value_cols = to_owners(attn_sum[:, : 3 * team_wide], 3)
    out_grad = swapped(attn_sum[:, 3 * team_wide :])
    out_grad = both_halves(out_grad.reshape(N_TEAM, pair_rows, team_wide))
    gain_terms = jnp.concatenate(
        [gain_one_term.reshape(-1, shard), gain_two_term.reshape(-1, shard)], axis=1
    )
    gain_sum = jnp.sum(lax.all_to_all(gain_terms, SEQ, 0, 0, tiled=True), axis=0)
    gain_sum = gain_sum + from_ahead(gain_sum, "g", 1)
    return (
        outputs,
        input_grad,
        gain_sum[:shard],
        columns(query_cols),
        columns(key_cols),
        columns(value_cols),
        columns(out_grad),
        gain_sum[shard:],
        unit_columns(gate_cols),
        unit_columns(up_cols),
        down_grad,
    )


def solution(mesh):
    fine = Mesh(mesh.devices.reshape(2, 2, 4, 4, 2), ALL)
    return jax.shard_map(
        body,
        mesh=fine,
        in_specs=(
            P(ALL, None),
            P("g", None),
            P(SEQ),
            P(SEQ, None),
            P(SEQ, None),
            P(SEQ, None),
            P(SEQ, None),
            P(SEQ),
            P(SEQ, None),
            P(SEQ, None),
            P(SEQ, None),
            P(ALL, None),
        ),
        out_specs=(
            P(ALL, None),
            P(ALL, None),
            P(SEQ),
            P(SEQ, None),
            P(SEQ, None),
            P(SEQ, None),
            P(SEQ, None),
            P(SEQ),
            P(SEQ, None),
            P(SEQ, None),
            P(SEQ, None),
        ),
        check_vma=False,
    )
```

time: 2010 us -> 763 us (0.38)
  blocking collectives: 633 us -> 150 us
  waiting for transfers between devices: 730 us -> 326 us
  local copies, waits for them, and re-layouts: 303 us -> 53.5 us
  matrix products: 237 us -> 70.7 us
  starting transfers between devices: 51.8 us -> 76.3 us
  Pallas kernels: 0 us -> 20.3 us
    all_gather x3, waiting for transfers between devices: 503 us -> 0.01 us  [the longest x1 0.01 us: body(): lax.all_gather(jnp.concatenate([qkv_cut, out_cut], axis=1), FLEET, axis=0...]
    unnamed x2 -> x1, blocking collectives: 633 us -> 150 us
    ppermute x2 -> x41, waiting for transfers between devices: 5.85 us -> 215 us  [the longest x37 194 us: from_ahead(): return lax.ppermute(value, axis, [((i + by) % n, i) for i in range(n)])]
    unnamed x9 -> x6, waiting for transfers between devices: 187 us -> 0.1 us
    concatenate x5, local copies, waits for them, and re-layouts: 178 us -> 3.03 us  [the longest x4 2.32 us: team_gather(): return jnp.concatenate([mine, from_ahead(mine, 'c', 1)], axis=0)]
    reduce_scatter x2 -> x3, waiting for transfers between devices: 0.01 us -> 88.1 us  [fleet_reduce(): lax.psum_scatter(terms.astype(low), (*FLEET, 'g'), scatter_dimension=0, t...]
    unnamed x78 -> x83, local copies, waits for them, and re-layouts: 106 us -> 21 us
    dot_general x7 -> x4, matrix products: 88.1 us -> 19.5 us  [matmul_left_t(): lax.dot_general(left, right, (((0,), (0,)), ((), ())), preferred_element_...]
  transfers between devices with their start and end apart: 19 -> 52, of which waited for: 11 -> 31; matrix products, arithmetic and copies ran while one was open for 49% -> 17% of each run, Pallas kernels for 0% -> 3%
where the time goes in v1:
time: 763 us; the launch traced here: 755 us
  waiting for transfers between devices  326 us (43%)
  blocking collectives  150 us (20%)
  starting transfers between devices  76.3 us (10%)
  matrix products  70.7 us (9%)
  local copies, waits for them, and re-layouts  53.5 us (7%)
  other arithmetic  40.7 us (5%)
  Pallas kernels  20.3 us (3%)
  between operations  16.9 us (2%)
    ppermute x37, waiting for transfers between devices, from_ahead(): return lax.ppermute(value, axis, [((i + by) % n, i) for i in range(n)])  194 us
    unnamed x1, blocking collectives  150 us
    reduce_scatter x3, waiting for transfers between devices, fleet_reduce(): lax.psum_scatter(terms.astype(low), (*FLEET, 'g'), scatter_dimension=0, t...  88.1 us
    ppermute x37, starting transfers between devices, from_ahead(): return lax.ppermute(value, axis, [((i + by) % n, i) for i in range(n)])  36.3 us
    dot_general x4, matrix products, matmul_right_t(): lax.dot_general(left, right, (((1,), (1,)), ((), ())), preferred_element_...  26.6 us
    dot_general x4, matrix products, matmul(): return jnp.dot(left, right, preferred_element_type=full)  24.7 us
    unnamed x83, local copies, waits for them, and re-layouts  21 us
    dot_general x4, matrix products, matmul_left_t(): lax.dot_general(left, right, (((0,), (0,)), ((), ())), preferred_element_...  19.5 us
  transfers between devices with their start and end apart: 52, of which 31 were waited for; matrix products, arithmetic and copies ran while one was open for 17% of the time, Pallas kernels for 3%

profile of v1, /device:TPU:8, one launch (start us, length us, event | category | flops | bytes accessed | tf_op | source)
XLA Modules:
  0.0 754.7 jit_solution(17244743210140762580)
XLA Ops:
  12.8 5.3 all-to-all-start
  18.2 5.3 collective-permute-start.5
  23.5 8.3 %collective-permute-done.5 = bf16[32,2048]{1,0:T(8,128)(2,1)S(1)} collective-permute-done((bf16[32,2048]{1,0:T(8,128)(2,1)S(1)}, bf16[32,2048]{1,0:T(8,128)(2,1)S(1)}, u32[]{:S(2)}, u32[]{:S(2)}) %collective-permute-start.5) | collective-permute-done | bytes 131104 | tf_op jit(solution)/shard_map/ppermute | solution.py:38
  48.3 8.7 %all-to-all-done.1 = bf16[8,32,1536]{2,1,0:T(8,128)(2,1)S(1)} async-done(((bf16[8,32,1536]{2,1,0:T(8,128)(2,1)}), bf16[8,32,1536]{2,1,0:T(8,128)(2,1)S(1)}, u32[]{:S(2)}, u32[]{:S(2)}) %all-to-all-start.1) | async-done | bytes 786464 | tf_op jit(solution)/shard_map/all_to_all | solution.py:239
  60.8 150.2 %all-reduce.3 = bf16[4096]{0:T(1024)(128)(2,1)S(1)} all-reduce(bf16[4096]{0:T(1024)(128)(2,1)S(1)} %dynamic-update-slice), channel_id=2, replica_groups=mesh['g'=2,'yl'=2,'x'=4,'z'=4,'c'=2] {'yl','x','z','c'}, use_global_device_ids=true, to_apply=%add.3 | all-reduce | flops 4096 | bytes 16384
  221.1 9.7 %collective-permute-done.4 = bf16[64,2048]{1,0:T(8,128)(2,1)S(1)} collective-permute-done((bf16[64,2048]{1,0:T(8,128)(2,1)S(1)}, bf16[64,2048]{1,0:T(8,128)(2,1)S(1)}, u32[]{:S(2)}, u32[]{:S(2)}) %collective-permute-start.4) | collective-permute-done | bytes 262176 | tf_op jit(solution)/shard_map/ppermute | solution.py:32
  240.9 5.9 convolution_convert_fusion.2.q_ref.k_ref.v_ref.kp_ref.vp_ref
  246.8 8.0 %shard_map.203 = bf16[1024,256]{1,0:T(8,128)(2,1)S(1)} custom-call(s32[16]{0:T(128)S(1)} %pad_add_fusion.place, bf16[1088,768]{1,0:T(8,128)(2,1)S(1)} %convolution_convert_fusion.2.q_ref.k_ref.v_ref.kp_ref.vp_ref, bf16[1088,768]{1,0:T(8,128)(2,1)S(1)} %convolution_convert_fusion.2.q_ref.k_ref.v_ref.kp_ref.vp_ref, ...), custom_call_target="tpu_custom_call" | custom-call | tf_op jit(solution)/shard_map/pallas_call | solution.py:156
  273.6 10.4 %collective-permute-done.20 = bf16[128,2048]{1,0:T(8,128)(2,1)} collective-permute-done((bf16[128,2048]{1,0:T(8,128)(2,1)}, bf16[128,2048]{1,0:T(8,128)(2,1)}, u32[]{:S(2)}, u32[]{:S(2)}) %collective-permute-start.20) | collective-permute-done | bytes 524320 | tf_op jit(solution)/shard_map/ppermute | solution.py:28
  286.2 9.4 %collective-permute-done.7 = bf16[128,2048]{1,0:T(8,128)(2,1)} collective-permute-done((bf16[128,2048]{1,0:T(8,128)(2,1)}, bf16[128,2048]{1,0:T(8,128)(2,1)}, u32[]{:S(2)}, u32[]{:S(2)}) %collective-permute-start.7) | collective-permute-done | bytes 524320 | tf_op jit(solution)/shard_map/ppermute | solution.py:28
  295.7 10.7 %collective-permute-done.8 = bf16[128,2048]{1,0:T(8,128)(2,1)} collective-permute-done((bf16[128,2048]{1,0:T(8,128)(2,1)}, bf16[128,2048]{1,0:T(8,128)(2,1)}, u32[]{:S(2)}, u32[]{:S(2)}) %collective-permute-start.8) | collective-permute-done | bytes 524320 | tf_op jit(solution)/shard_map/ppermute | solution.py:28
  312.6 12.8 %collective-permute-done.10 = bf16[128,2048]{1,0:T(8,128)(2,1)S(1)} collective-permute-done((bf16[128,2048]{1,0:T(8,128)(2,1)S(1)}, bf16[128,2048]{1,0:T(8,128)(2,1)S(1)}, u32[]{:S(2)}, u32[]{:S(2)}) %collective-permute-start.10) | collective-permute-done | bytes 524320 | tf_op jit(solution)/shard_map/ppermute | solution.py:28
  328.0 9.7 %collective-permute-done.12 = bf16[128,2048]{1,0:T(8,128)(2,1)S(1)} collective-permute-done((bf16[128,2048]{1,0:T(8,128)(2,1)S(1)}, bf16[128,2048]{1,0:T(8,128)(2,1)S(1)}, u32[]{:S(2)}, u32[]{:S(2)}) %collective-permute-start.12) | collective-permute-done | bytes 524320 | tf_op jit(solution)/shard_map/ppermute | solution.py:28
  347.2 11.7 %fusion.61 = f32[1024,1536]{1,0:T(8,128)} fusion(bf16[1024,2048]{1,0:T(8,128)(2,1)} %constant_dynamic-update-slice_fusion.11, bf16[2048,1536]{1,0:T(8,128)(2,1)} %all-gather.7.cloned.1.call-done), kind=kOutput, calls=%fused_computation.186 | convolution fusion | flops 6442450944 | bytes 16777216 | tf_op jit(solution)/shard_map/dot_general | solution.py:64
  358.9 11.1 %multiply_convert_fusion.1 = (bf16[1024,768]{1,0:T(8,128)(2,1)}, bf16[1024,768]{1,0:T(8,128)(2,1)}, bf16[1024,768]{1,0:T(8,128)(2,1)S(1)}) fusion(f32[1024,1536]{1,0:T(8,128)} %fusion.61, bf16[1024,2048]{1,0:T(8,128)(2,1)} %copy-done.18, bf16[768,2048]{1,0:T(8,128)(2,1)} %all-gather.9.cloned.1.call-done), kind=kOutput, calls=%fused_computation.22 | convolution fusion | flops 3233021952 | bytes 18350080 | tf_op jit(solution)/shard_map/dot_general | solution.py:72
  376.4 9.5 %convolution_convert_fusion = bf16[2048,1536]{1,0:T(8,128)(2,1)S(1)} fusion(bf16[1024,2048]{1,0:T(8,128)(2,1)} %constant_dynamic-update-slice_fusion.11, bf16[1024,768]{1,0:T(8,128)(2,1)} %get-tuple-element.41, bf16[1024,768]{1,0:T(8,128)(2,1)} %get-tuple-element.40), kind=kOutput, calls=%fused_computation.5 | convolution fusion | flops 6451888128 | bytes 13631488 | tf_op jit(solution)/shard_map/dot_general | solution.py:68
  389.2 5.8 fusion.62
  396.9 8.8 %fusion.12 = f32[1024,2048]{1,0:T(8,128)S(1)} fusion(bf16[2048,1536]{1,0:T(8,128)(2,1)} %all-gather.7.cloned.1.call-done, bf16[1024,768]{1,0:T(8,128)(2,1)S(1)} %copy-done.27, bf16[1024,768]{1,0:T(8,128)(2,1)S(1)} %copy-done.26), kind=kOutput, calls=%fused_computation.39 | convolution fusion | flops 6448742400 | bytes 17825792 | tf_op jit(solution)/shard_map/dot_general | solution.py:72
  419.0 17.9 %collective-permute-done.15 = bf16[128,2048]{1,0:T(8,128)(2,1)S(1)} collective-permute-done((bf16[128,2048]{1,0:T(8,128)(2,1)S(1)}, bf16[128,2048]{1,0:T(8,128)(2,1)S(1)}, u32[]{:S(2)}, u32[]{:S(2)}) %collective-permute-start.15) | collective-permute-done | bytes 524320 | tf_op jit(solution)/shard_map/ppermute | solution.py:28
  437.7 20.6 %collective-permute-done.23 = bf16[128,2048]{1,0:T(8,128)(2,1)S(1)} collective-permute-done((bf16[128,2048]{1,0:T(8,128)(2,1)S(1)}, bf16[128,2048]{1,0:T(8,128)(2,1)S(1)}, u32[]{:S(2)}, u32[]{:S(2)}) %collective-permute-start.23) | collective-permute-done | bytes 524320 | tf_op jit(solution)/shard_map/ppermute | solution.py:28
  466.2 21.3 %collective-permute-done.26 = bf16[128,2048]{1,0:T(8,128)(2,1)S(1)} collective-permute-done((bf16[128,2048]{1,0:T(8,128)(2,1)S(1)}, bf16[128,2048]{1,0:T(8,128)(2,1)S(1)}, u32[]{:S(2)}, u32[]{:S(2)}) %collective-permute-start.26) | collective-permute-done | bytes 524320 | tf_op jit(solution)/shard_map/ppermute | solution.py:28
  497.0 12.3 %shard_map.204 = (bf16[1024,768]{1,0:T(8,128)(2,1)S(1)}, f32[64,512]{1,0:T(8,128)S(1)}, bf16[64,512]{1,0:T(8,128)(2,1)S(1)}) custom-call(s32[16]{0:T(128)S(1)} %pad_add_fusion.place, bf16[1088,768]{1,0:T(8,128)(2,1)S(1)} %convolution_convert_fusion.2.q_ref.k_ref.v_ref.kp_ref.vp_ref, ...), custom_call_target="tpu_custom_call" | custom-call | tf_op jit(solution)/shard_map/pallas_call | solution.py:176
  524.6 5.3 fusion.9
  543.6 21.6 %collective-permute-done.32 = bf16[128,2048]{1,0:T(8,128)(2,1)S(1)} collective-permute-done((bf16[128,2048]{1,0:T(8,128)(2,1)}, bf16[128,2048]{1,0:T(8,128)(2,1)S(1)}, u32[]{:S(2)}, u32[]{:S(2)}) %collective-permute-start.32) | collective-permute-done | bytes 524320 | tf_op jit(solution)/shard_map/ppermute | solution.py:28
  569.5 6.5 all-to-all-start.2
  577.1 6.0 all-to-all-done.2
  583.2 21.7 %reduce-scatter.6.cloned.1.call-done = bf16[128,1536]{1,0:T(8,128)(2,1)} async-done(((bf16[2048,1536]{1,0:T(8,128)(2,1)}), bf16[128,1536]{1,0:T(8,128)(2,1)}) %reduce-scatter.6.cloned.1.call-update) | async-done | bytes 393232 | tf_op jit(solution)/shard_map/reduce_scatter | solution.py:204
  612.6 5.6 all-to-all-done.4
  622.8 26.9 %collective-permute-done.39 = bf16[8,16,1536]{2,1,0:T(8,128)(2,1)S(1)} collective-permute-done((bf16[8,16,1536]{2,1,0:T(8,128)(2,1)S(1)}, bf16[8,16,1536]{2,1,0:T(8,128)(2,1)S(1)}, u32[]{:S(2)}, u32[]{:S(2)}) %collective-permute-start.39) | collective-permute-done | bytes 393248 | tf_op jit(solution)/shard_map/ppermute | solution.py:28
  650.4 66.4 %reduce-scatter.4.cloned.1.call-done = bf16[128,1024]{1,0:T(8,128)(2,1)} async-done(((bf16[2048,1024]{1,0:T(8,128)(2,1)}), bf16[128,1024]{1,0:T(8,128)(2,1)}) %reduce-scatter.4.cloned.1.call-update) | async-done | bytes 262160 | tf_op jit(solution)/shard_map/reduce_scatter | solution.py:204
  717.7 5.4 collective-permute-start.37
  738.9 6.3 collective-permute-done.36
  (281 shorter events, 192.6 us)
Async XLA Ops:
  12.8 19.9 %all-to-all-start = ((bf16[8,32,768]{2,1,0:T(8,128)(2,1)}), bf16[8,32,768]{2,1,0:T(8,128)(2,1)S(1)}, u32[]{:S(2)}, u32[]{:S(2)}) async-start(bf16[8,32,768]{2,1,0:T(8,128)(2,1)} %reshape.334), calls=%async_computation | async-start | bytes 786432 | tf_op jit(solution)/shard_map/all_to_all | solution.py:225
  18.1 220.1 %all-gather.5.cloned.1.call-start = ((), (), s32[]{:S(2)}) async-start(), calls=%async_computation.8 | async-start | bytes 4718592 | tf_op jit(solution)/shard_map/all_gather | solution.py:228
  39.8 17.2 %all-to-all-start.1 = ((bf16[8,32,1536]{2,1,0:T(8,128)(2,1)}), bf16[8,32,1536]{2,1,0:T(8,128)(2,1)S(1)}, u32[]{:S(2)}, u32[]{:S(2)}) async-start(bf16[8,32,1536]{2,1,0:T(8,128)(2,1)} %pad_maximum_fusion.8), calls=%async_computation.1 | async-start | bytes 1572864 | tf_op jit(solution)/shard_map/all_to_all | solution.py:239
  43.3 303.9 %all-gather.7.cloned.1.call-start = ((), (), s32[]{:S(2)}) async-start(), calls=%async_computation.9 | async-start | bytes 7077888 | tf_op jit(solution)/shard_map/all_gather | solution.py:240
  43.4 168.0 %collective-permute-start = (bf16[128,2048]{1,0:T(8,128)(2,1)S(1)}, bf16[128,2048]{1,0:T(8,128)(2,1)S(1)}, u32[]{:S(2)}, u32[]{:S(2)}) collective-permute-start(bf16[128,2048]{1,0:T(8,128)(2,1)S(1)} %copy-done.6), channel_id=1, source_target_pairs={{2,0},{4,2},{6,4},{0,6},{3,1},{5,3},{7,5},{1,7},{10,8},{12,10},{14... | collective-permute-start | bytes 1572872 | tf_op jit(solution)/shard_map/ppermute | solution.py:28
  46.6 164.8 %collective-permute-start.1 = (bf16[128,2048]{1,0:T(8,128)(2,1)S(1)}, bf16[128,2048]{1,0:T(8,128)(2,1)S(1)}, u32[]{:S(2)}, u32[]{:S(2)}) collective-permute-start(bf16[128,2048]{1,0:T(8,128)(2,1)S(1)} %copy-done.6), channel_id=1, source_target_pairs={{4,0},{6,2},{0,4},{2,6},{5,1},{7,3},{1,5},{3,7},{12,8},{14,10},{8,... | collective-permute-start | bytes 1572872 | tf_op jit(solution)/shard_map/ppermute | solution.py:28
  47.4 164.0 %collective-permute-start.2 = (bf16[128,2048]{1,0:T(8,128)(2,1)S(1)}, bf16[128,2048]{1,0:T(8,128)(2,1)S(1)}, u32[]{:S(2)}, u32[]{:S(2)}) collective-permute-start(bf16[128,2048]{1,0:T(8,128)(2,1)S(1)} %copy-done.6), channel_id=1, source_target_pairs={{6,0},{0,2},{2,4},{4,6},{7,1},{1,3},{3,5},{5,7},{14,8},{8,10},{10,... | collective-permute-start | bytes 1572872 | tf_op jit(solution)/shard_map/ppermute | solution.py:28
  57.9 301.0 %all-gather.9.cloned.1.call-start = ((), (), s32[]{:S(2)}) async-start(), calls=%async_computation.10 | async-start | bytes 3538944 | tf_op jit(solution)/shard_map/all_gather | solution.py:244
  256.6 17.0 %collective-permute-start.19 = (bf16[128,2048]{1,0:T(8,128)(2,1)}, bf16[128,2048]{1,0:T(8,128)(2,1)}, u32[]{:S(2)}, u32[]{:S(2)}) collective-permute-start(bf16[128,2048]{1,0:T(8,128)(2,1)} %param.23), channel_id=1, source_target_pairs={{4,0},{6,2},{0,4},{2,6},{5,1},{7,3},{1,5},{3,7},{12,8},{14,10},{8,... | collective-permute-start | bytes 1572872 | tf_op jit(solution)/shard_map/ppermute | solution.py:28
  256.7 27.3 %collective-permute-start.20 = (bf16[128,2048]{1,0:T(8,128)(2,1)}, bf16[128,2048]{1,0:T(8,128)(2,1)}, u32[]{:S(2)}, u32[]{:S(2)}) collective-permute-start(bf16[128,2048]{1,0:T(8,128)(2,1)} %param.23), channel_id=1, source_target_pairs={{6,0},{0,2},{2,4},{4,6},{7,1},{1,3},{3,5},{5,7},{14,8},{8,10},{10,... | collective-permute-start | bytes 1572872 | tf_op jit(solution)/shard_map/ppermute | solution.py:28
  264.8 30.9 %collective-permute-start.7 = (bf16[128,2048]{1,0:T(8,128)(2,1)}, bf16[128,2048]{1,0:T(8,128)(2,1)}, u32[]{:S(2)}, u32[]{:S(2)}) collective-permute-start(bf16[128,2048]{1,0:T(8,128)(2,1)} %get-tuple-element.52), channel_id=1, source_target_pairs={{6,0},{0,2},{2,4},{4,6},{7,1},{1,3},{3,5},{5,7},{14,8},{8,10},{10,... | collective-permute-start | bytes 1572872 | tf_op jit(solution)/shard_map/ppermute | solution.py:28
  264.8 41.6 %collective-permute-start.8 = (bf16[128,2048]{1,0:T(8,128)(2,1)}, bf16[128,2048]{1,0:T(8,128)(2,1)}, u32[]{:S(2)}, u32[]{:S(2)}) collective-permute-start(bf16[128,2048]{1,0:T(8,128)(2,1)} %get-tuple-element.54), channel_id=1, source_target_pairs={{4,0},{6,2},{0,4},{2,6},{5,1},{7,3},{1,5},{3,7},{12,8},{14,10},{8,... | collective-permute-start | bytes 1572872 | tf_op jit(solution)/shard_map/ppermute | solution.py:28
  271.6 34.8 %collective-permute-start.9 = (bf16[128,2048]{1,0:T(8,128)(2,1)}, bf16[128,2048]{1,0:T(8,128)(2,1)}, u32[]{:S(2)}, u32[]{:S(2)}) collective-permute-start(bf16[128,2048]{1,0:T(8,128)(2,1)} %get-tuple-element.53), channel_id=1, source_target_pairs={{2,0},{4,2},{6,4},{0,6},{3,1},{5,3},{7,5},{1,7},{10,8},{12,10},{14... | collective-permute-start | bytes 1572872 | tf_op jit(solution)/shard_map/ppermute | solution.py:28
  273.5 268.6 %reduce-scatter.8.cloned.1.call-start = ((), (), s32[]{:S(2)}) async-start(), calls=%async_computation.13 | async-start | bytes 3342336 | tf_op jit(solution)/shard_map/reduce_scatter | solution.py:204
  285.7 56.7 %collective-permute-start.21 = (bf16[512,2048]{1,0:T(8,128)(2,1)S(1)}, bf16[512,2048]{1,0:T(8,128)(2,1)S(1)}, u32[]{:S(2)}, u32[]{:S(2)}) collective-permute-start(bf16[512,2048]{1,0:T(8,128)(2,1)S(1)} %pad_maximum_fusion.4), channel_id=1, source_target_pairs={{1,0},{0,1},{3,2},{2,3},{5,4},{4,5},{7,6},{6,7},{9,8},{8,9},{11,10... | collective-permute-start | bytes 6291464 | tf_op jit(solution)/shard_map/ppermute | solution.py:28
  311.7 26.0 %collective-permute-start.12 = (bf16[128,2048]{1,0:T(8,128)(2,1)S(1)}, bf16[128,2048]{1,0:T(8,128)(2,1)S(1)}, u32[]{:S(2)}, u32[]{:S(2)}) collective-permute-start(bf16[128,2048]{1,0:T(8,128)(2,1)S(1)} %get-tuple-element.33), channel_id=1, source_target_pairs={{6,0},{0,2},{2,4},{4,6},{7,1},{1,3},{3,5},{5,7},{14,8},{8,10},{10,... | collective-permute-start | bytes 1572872 | tf_op jit(solution)/shard_map/ppermute | solution.py:28
  376.1 228.7 %reduce-scatter.6.cloned.1.call-start = ((), (), s32[]{:S(2)}) async-start(), calls=%async_computation.12 | async-start | bytes 6684672 | tf_op jit(solution)/shard_map/reduce_scatter | solution.py:204
  389.2 327.7 %reduce-scatter.4.cloned.1.call-start = ((), (), s32[]{:S(2)}) async-start(), calls=%async_computation.11 | async-start | bytes 4456448 | tf_op jit(solution)/shard_map/reduce_scatter | solution.py:204
  409.5 27.3 %collective-permute-start.15 = (bf16[128,2048]{1,0:T(8,128)(2,1)S(1)}, bf16[128,2048]{1,0:T(8,128)(2,1)S(1)}, u32[]{:S(2)}, u32[]{:S(2)}) collective-permute-start(bf16[128,2048]{1,0:T(8,128)(2,1)S(1)} %get-tuple-element.49), channel_id=1, source_target_pairs={{6,0},{0,2},{2,4},{4,6},{7,1},{1,3},{3,5},{5,7},{14,8},{8,10},{10,... | collective-permute-start | bytes 1572872 | tf_op jit(solution)/shard_map/ppermute | solution.py:28
  409.6 27.2 %collective-permute-start.16 = (bf16[128,2048]{1,0:T(8,128)(2,1)S(1)}, bf16[128,2048]{1,0:T(8,128)(2,1)S(1)}, u32[]{:S(2)}, u32[]{:S(2)}) collective-permute-start(bf16[128,2048]{1,0:T(8,128)(2,1)S(1)} %get-tuple-element.51), channel_id=1, source_target_pairs={{4,0},{6,2},{0,4},{2,6},{5,1},{7,3},{1,5},{3,7},{12,8},{14,10},{8,... | collective-permute-start | bytes 1572872 | tf_op jit(solution)/shard_map/ppermute | solution.py:28
  412.0 25.7 %collective-permute-start.17 = (bf16[128,2048]{1,0:T(8,128)(2,1)S(1)}, bf16[128,2048]{1,0:T(8,128)(2,1)S(1)}, u32[]{:S(2)}, u32[]{:S(2)}) collective-permute-start(bf16[128,2048]{1,0:T(8,128)(2,1)S(1)} %get-tuple-element.50), channel_id=1, source_target_pairs={{2,0},{4,2},{6,4},{0,6},{3,1},{5,3},{7,5},{1,7},{10,8},{12,10},{14... | collective-permute-start | bytes 1572872 | tf_op jit(solution)/shard_map/ppermute | solution.py:28
  415.7 42.7 %collective-permute-start.23 = (bf16[128,2048]{1,0:T(8,128)(2,1)S(1)}, bf16[128,2048]{1,0:T(8,128)(2,1)S(1)}, u32[]{:S(2)}, u32[]{:S(2)}) collective-permute-start(bf16[128,2048]{1,0:T(8,128)(2,1)S(1)} %get-tuple-element.46), channel_id=1, source_target_pairs={{6,0},{0,2},{2,4},{4,6},{7,1},{1,3},{3,5},{5,7},{14,8},{8,10},{10,... | collective-permute-start | bytes 1572872 | tf_op jit(solution)/shard_map/ppermute | solution.py:28
  417.1 41.2 %collective-permute-start.24 = (bf16[128,2048]{1,0:T(8,128)(2,1)S(1)}, bf16[128,2048]{1,0:T(8,128)(2,1)S(1)}, u32[]{:S(2)}, u32[]{:S(2)}) collective-permute-start(bf16[128,2048]{1,0:T(8,128)(2,1)S(1)} %get-tuple-element.48), channel_id=1, source_target_pairs={{4,0},{6,2},{0,4},{2,6},{5,1},{7,3},{1,5},{3,7},{12,8},{14,10},{8,... | collective-permute-start | bytes 1572872 | tf_op jit(solution)/shard_map/ppermute | solution.py:28
  436.8 22.2 %collective-permute-start.25 = (bf16[128,2048]{1,0:T(8,128)(2,1)S(1)}, bf16[128,2048]{1,0:T(8,128)(2,1)S(1)}, u32[]{:S(2)}, u32[]{:S(2)}) collective-permute-start(bf16[128,2048]{1,0:T(8,128)(2,1)S(1)} %get-tuple-element.47), channel_id=1, source_target_pairs={{2,0},{4,2},{6,4},{0,6},{3,1},{5,3},{7,5},{1,7},{10,8},{12,10},{14... | collective-permute-start | bytes 1572872 | tf_op jit(solution)/shard_map/ppermute | solution.py:28
  463.1 24.5 %collective-permute-start.26 = (bf16[128,2048]{1,0:T(8,128)(2,1)S(1)}, bf16[128,2048]{1,0:T(8,128)(2,1)S(1)}, u32[]{:S(2)}, u32[]{:S(2)}) collective-permute-start(bf16[128,2048]{1,0:T(8,128)(2,1)S(1)} %get-tuple-element.25), channel_id=1, source_target_pairs={{2,0},{4,2},{6,4},{0,6},{3,1},{5,3},{7,5},{1,7},{10,8},{12,10},{14... | collective-permute-start | bytes 1572872 | tf_op jit(solution)/shard_map/ppermute | solution.py:28
  465.4 22.2 %collective-permute-start.27 = (bf16[128,2048]{1,0:T(8,128)(2,1)S(1)}, bf16[128,2048]{1,0:T(8,128)(2,1)S(1)}, u32[]{:S(2)}, u32[]{:S(2)}) collective-permute-start(bf16[128,2048]{1,0:T(8,128)(2,1)S(1)} %get-tuple-element.25), channel_id=1, source_target_pairs={{4,0},{6,2},{0,4},{2,6},{5,1},{7,3},{1,5},{3,7},{12,8},{14,10},{8,... | collective-permute-start | bytes 1572872 | tf_op jit(solution)/shard_map/ppermute | solution.py:28
  465.4 25.7 %collective-permute-start.28 = (bf16[128,2048]{1,0:T(8,128)(2,1)S(1)}, bf16[128,2048]{1,0:T(8,128)(2,1)S(1)}, u32[]{:S(2)}, u32[]{:S(2)}) collective-permute-start(bf16[128,2048]{1,0:T(8,128)(2,1)S(1)} %get-tuple-element.25), channel_id=1, source_target_pairs={{6,0},{0,2},{2,4},{4,6},{7,1},{1,3},{3,5},{5,7},{14,8},{8,10},{10,... | collective-permute-start | bytes 1572872 | tf_op jit(solution)/shard_map/ppermute | solution.py:28
  538.5 26.6 %collective-permute-start.32 = (bf16[128,2048]{1,0:T(8,128)(2,1)}, bf16[128,2048]{1,0:T(8,128)(2,1)S(1)}, u32[]{:S(2)}, u32[]{:S(2)}) collective-permute-start(bf16[128,2048]{1,0:T(8,128)(2,1)} %get-tuple-element.43), channel_id=1, source_target_pairs={{6,0},{0,2},{2,4},{4,6},{7,1},{1,3},{3,5},{5,7},{14,8},{8,10},{10,... | collective-permute-start | bytes 1572872 | tf_op jit(solution)/shard_map/ppermute | solution.py:28
  538.5 26.6 %collective-permute-start.33 = (bf16[128,2048]{1,0:T(8,128)(2,1)}, bf16[128,2048]{1,0:T(8,128)(2,1)}, u32[]{:S(2)}, u32[]{:S(2)}) collective-permute-start(bf16[128,2048]{1,0:T(8,128)(2,1)} %get-tuple-element.45), channel_id=1, source_target_pairs={{4,0},{6,2},{0,4},{2,6},{5,1},{7,3},{1,5},{3,7},{12,8},{14,10},{8,... | collective-permute-start | bytes 1572872 | tf_op jit(solution)/shard_map/ppermute | solution.py:28
  540.7 25.0 %collective-permute-start.34 = (bf16[128,2048]{1,0:T(8,128)(2,1)S(1)}, bf16[128,2048]{1,0:T(8,128)(2,1)S(1)}, u32[]{:S(2)}, u32[]{:S(2)}) collective-permute-start(bf16[128,2048]{1,0:T(8,128)(2,1)S(1)} %get-tuple-element.44), channel_id=1, source_target_pairs={{2,0},{4,2},{6,4},{0,6},{3,1},{5,3},{7,5},{1,7},{10,8},{12,10},{14... | collective-permute-start | bytes 1572872 | tf_op jit(solution)/shard_map/ppermute | solution.py:28
  542.1 34.0 %collective-permute-start.40 = (bf16[48,2048]{1,0:T(8,128)(2,1)}, bf16[48,2048]{1,0:T(8,128)(2,1)}, u32[]{:S(2)}, u32[]{:S(2)}) collective-permute-start(bf16[48,2048]{1,0:T(8,128)(2,1)} %reduce-scatter.8.cloned.1.call-done), channel_id=1, source_target_pairs={{64,0},{0,64},{65,1},{1,65},{66,2},{2,66},{67,3},{3,67},{68,4},{4,... | collective-permute-start | bytes 589832 | tf_op jit(solution)/shard_map/ppermute | solution.py:28
  618.2 31.4 %collective-permute-start.39 = (bf16[8,16,1536]{2,1,0:T(8,128)(2,1)S(1)}, bf16[8,16,1536]{2,1,0:T(8,128)(2,1)S(1)}, u32[]{:S(2)}, u32[]{:S(2)}) collective-permute-start(bf16[8,16,1536]{2,1,0:T(8,128)(2,1)S(1)} %all-to-all-done.4), channel_id=1, source_target_pairs={{64,0},{0,64},{65,1},{1,65},{66,2},{2,66},{67,3},{3,67},{68,4},{4,... | collective-permute-start | bytes 1179656 | tf_op jit(solution)/shard_map/ppermute | solution.py:28
  (50 other events, 803.0 us)
Sparse Core Ops, SparseCore 0:
  33.7 52.0 all-gather.4
  87.5 71.2 all-gather.6
  273.6 59.1 all-gather.8
  376.3 82.6 reduce-scatter.7
  461.2 143.5 reduce-scatter.5
  607.1 109.6 reduce-scatter.3

commit v2 on v1

--- a/solution.py
+++ b/solution.py
@@ -17,7 +17,7 @@
 FLEET = ("yl", "x")
 SEQ = ("yl", "x", "z", "c")
 ALL = ("g", "yl", "x", "z", "c")
-N_Z, N_C, N_TEAM, N_FLEET = 4, 2, 8, 8
+N_X, N_Z, N_C, N_TEAM, N_FLEET = 4, 4, 2, 8, 8
 SCALE = HEAD ** (-0.5)
 low = jnp.bfloat16
 full = jnp.float32
@@ -34,26 +34,36 @@
     )
 
 
-def swapped(value):
-    return lax.ppermute(
-        value, SEQ, [(N_TEAM * f + t, N_TEAM * t + f) for f in range(N_FLEET) for t in range(N_TEAM)]
-    )
-
-
-def team_gather(value):
-    mine = jnp.concatenate([value] + [from_ahead(value, "z", k) for k in range(1, N_Z)], axis=0)
-    return jnp.concatenate([mine, from_ahead(mine, "c", 1)], axis=0)
-
-
-def team_scatter(parts):
-    rows = parts.shape[0] // N_TEAM
-    half = N_Z * rows
-    there = from_ahead(parts[half:].astype(low), "c", 1)
-    pair = parts[:half].astype(full) + there.astype(full)
-    total = pair[:rows]
-    for k in range(1, N_Z):
-        total = total + from_ahead(pair[k * rows : (k + 1) * rows].astype(low), "z", -k).astype(full)
-    return total
+def swapped(value, across=0):
+    n = N_FLEET * N_TEAM
+    pairs = [(N_TEAM * f + t, N_TEAM * t + f) for f in range(N_FLEET) for t in range(N_TEAM)]
+    return lax.ppermute(value, ALL, [(g * n + a, (g ^ across) * n + b) for g in range(2) for a, b in pairs])
+
+
+def z_gather(value):
+    return [value] + [from_ahead(value, "z", k) for k in (1, 2, 3)]
+
+
+def z_sum(blocks):
+    return blocks[0] + sum(from_ahead(blocks[k].astype(low), "z", -k).astype(full) for k in (1, 2, 3))
+
+
+def core_sum(left, right):
+    there = from_ahead(right(left[1]).astype(low), "c", 1)
+    pair = right(left[0]) + there.astype(full)
+    rows = pair.shape[0] // N_Z
+    return [pair[k * rows : (k + 1) * rows] for k in range(N_Z)]
+
+
+def in_order(pieces):
+    rows = pieces[0][0].shape[0]
+    x, yl = lax.axis_index("x"), lax.axis_index("yl")
+    whole = jnp.zeros((N_FLEET * rows, pieces[0][0].shape[1]), low)
+    for side in range(2):
+        for k in (0, 1, 3, 2):
+            place = ((yl ^ side) * N_X + (x + k) % N_X) * rows
+            whole = lax.dynamic_update_slice(whole, pieces[side][k], (place, 0))
+    return whole
 
 
 def inverse_rms(values):
@@ -70,6 +80,122 @@
 
 def matmul_right_t(left, right):
     return lax.dot_general(left, right, (((1,), (1,)), ((), ())), preferred_element_type=full)
+
+
+def cut_kernel(unit_rows, q_ref, k_ref, v_ref, gate_ref, up_ref, gain_ref, out_ref):
+    wide = q_ref.shape[1] // N_TEAM
+    lanes = gain_ref.shape[1]
+    units = (out_ref.shape[2] - 3 * wide - lanes) // 2
+    pad = units // N_FLEET
+    at_gate = 3 * wide + lanes
+    out_ref[:, :, at_gate:] = jnp.zeros((N_TEAM, q_ref.shape[0], 2 * units), low)
+    for t in range(N_TEAM):
+        for i, ref in enumerate((q_ref, k_ref, v_ref)):
+            out_ref[t, :, i * wide : (i + 1) * wide] = ref[:, t * wide : (t + 1) * wide]
+        out_ref[t, :, 3 * wide : at_gate] = gain_ref[...]
+        for i, ref in enumerate((gate_ref, up_ref)):
+            for f in range(N_FLEET):
+                at = at_gate + i * units + f * pad
+                first = (f * N_TEAM + t) * unit_rows
+                out_ref[t, :, at : at + unit_rows] = ref[:, first : first + unit_rows]
+
+
+def cut_for_team(w_query, w_key, w_value, w_gate, w_up, gains, unit_rows, units):
+    shard, width = w_query.shape
+    columns = 3 * width // N_TEAM + gains.shape[1] + 2 * units
+    return pl.pallas_call(
+        functools.partial(cut_kernel, unit_rows),
+        out_shape=jax.ShapeDtypeStruct((N_TEAM, shard, columns), low),
+        compiler_params=pltpu.CompilerParams(vmem_limit_bytes=16 << 20),
+    )(w_query, w_key, w_value, w_gate, w_up, gains)
+
+
+def norm_kernel(mine_ref, other_ref, halo_ref, gain_ref, out_ref):
+    gain = gain_ref[...].astype(full).T[:1]
+    at = 0
+    for ref in (mine_ref, other_ref, halo_ref):
+        for first in range(0, ref.shape[0], 16):
+            values = ref[first : first + 16].astype(full)
+            out_ref[at + first : at + first + 16] = (values * inverse_rms(values) * gain).astype(low)
+        at += ref.shape[0]
+
+
+def normalised(mine, other, halo, gain_columns):
+    rows = mine.shape[0] + other.shape[0] + halo.shape[0]
+    return pl.pallas_call(
+        norm_kernel,
+        out_shape=jax.ShapeDtypeStruct((rows, mine.shape[1]), low),
+        compiler_params=pltpu.CompilerParams(vmem_limit_bytes=32 << 20),
+    )(mine, other, halo, gain_columns)
+
+
+TILE = 256
+
+
+def terms_kernel(x0_ref, x1_ref, dy0_ref, dy1_ref, act0_ref, act1_ref, grad0_ref, grad1_ref, out_ref, down):
+    step = pl.program_id(0)
+    units = act0_ref.shape[1]
+    pad = units // N_FLEET
+    block = x0_ref.shape[1]
+
+    @pl.when(step == 0)
+    def _():
+        for first in range(0, units, TILE):
+            at = slice(first, first + TILE)
+            down[at] = (
+                matmul_left_t(act0_ref[:, at], dy0_ref[...]) + matmul_left_t(act1_ref[:, at], dy1_ref[...])
+            ).astype(low)
+
+    for i in range(2):
+        at = slice(i * units, (i + 1) * units)
+        term = matmul_left_t(x0_ref[...], grad0_ref[:, at]) + matmul_left_t(x1_ref[...], grad1_ref[:, at])
+        term = term.astype(low)
+        for row in range(0, block, 32):
+            for g in range(2):
+                out_ref[g, 0, row // 2 : row // 2 + 16, at] = term[row + 16 * g : row + 16 * g + 16]
+    rows = down[pl.ds(pl.multiple_of(step * pad, 16), pad)]
+    for g in range(2):
+        for (row, col), (to, lane) in down_chunks(pad // 2, rows.shape[1], 2 * units):
+            first = g * (pad // 2) + row
+            out_ref[g, 0, block // 2 + to : block // 2 + to + 16, lane : lane + 512] = rows[
+                first : first + 16, col : col + 512
+            ]
+
+
+def down_chunks(rows, width, wide):
+    packed = rows * width // wide
+    places = [(row, col) for col in range(0, width, 512) for row in range(0, rows, 16)]
+    return [(place, (16 * i % packed, 16 * i // packed * 512)) for i, place in enumerate(places)]
+
+
+def unpack_down(packed, rows, width):
+    parts = {
+        place: packed[to : to + 16, lane : lane + 512]
+        for place, (to, lane) in down_chunks(rows, width, packed.shape[1])
+    }
+    return jnp.concatenate(
+        [jnp.concatenate([parts[row, col] for col in range(0, width, 512)], axis=1) for row in range(0, rows, 16)],
+        axis=0,
+    )
+
+
+def feed_terms(rows, dy_rows, activated, grad_both):
+    half, width = rows[0].shape
+    units = activated[0].shape[1]
+    block = width // N_FLEET
+    tall = block // 2 + units // N_FLEET // 2 * width // (2 * units)
+    whole = lambda wide: pl.BlockSpec((half, wide), lambda s: (0, 0))
+    cut = pl.BlockSpec((half, block), lambda s: (0, s))
+    return pl.pallas_call(
+        terms_kernel,
+        grid=(N_FLEET,),
+        in_specs=[cut] * 2 + [whole(width)] * 2 + [whole(units)] * 2 + [whole(2 * units)] * 2,
+        out_specs=pl.BlockSpec((2, 1, tall, 2 * units), lambda s: (0, s, 0, 0)),
+        out_shape=jax.ShapeDtypeStruct((2, N_FLEET, tall, 2 * units), low),
+        scratch_shapes=[pltpu.VMEM((units, width), low)],
+        compiler_params=pltpu.CompilerParams(vmem_limit_bytes=56 << 20),
+        cost_estimate=pl.CostEstimate(flops=1, bytes_accessed=1, transcendentals=0),
+    )(*rows, *dy_rows, *activated, *grad_both)
 
 
 def segment_numbers(positions, lengths):
@@ -200,10 +326,6 @@
     return (gain_term, input_term)
 
 
-def fleet_reduce(terms):
-    return lax.psum_scatter(terms.astype(low), (*FLEET, "g"), scatter_dimension=0, tiled=True)
-
-
 def body(
     tokens, lengths, norm_gain, w_query, w_key, w_value, w_out, mlp_gain, w_gate, w_up, w_down, cotangent
 ):
@@ -213,35 +335,49 @@
     unit_rows = w_down.shape[0]
     unit_pad = -(-unit_rows // 32) * 32
     units = N_FLEET * unit_pad
-    z, c = lax.axis_index("z"), lax.axis_index("c")
+    x, yl, z, c = [lax.axis_index(axis) for axis in ("x", "yl", "z", "c")]
     fleet = lax.axis_index(FLEET)
 
-    gains = lax.all_gather(jnp.concatenate([norm_gain, mlp_gain])[None], SEQ, axis=0, tiled=True)
-    gain_one = gains[:, :shard].reshape(width).astype(full)
-    gain_two = gains[:, shard:].reshape(width).astype(full)
+    inputs = tokens.astype(full)
+    down_cut = jnp.pad(w_down, ((0, unit_pad - unit_rows), (0, 0)))
+    w_down_team = lax.all_gather(down_cut, FLEET, axis=0, tiled=True)
+    gains = jnp.concatenate([norm_gain[:, None], mlp_gain[:, None], jnp.zeros((shard, 126), low)], axis=1)
+    cut = cut_for_team(w_query, w_key, w_value, w_gate, w_up, gains, unit_rows, units)
+    cut = lax.all_to_all(cut, TEAM, 0, 0, tiled=True).reshape(N_TEAM * shard, -1)
     out_there = swapped(w_out)
-    qkv_cut = jnp.stack([w_query, w_key, w_value], axis=1).reshape(shard, 3, N_TEAM, team_wide)
-    qkv_cut = qkv_cut.transpose(2, 0, 1, 3).reshape(N_TEAM, shard, 3 * team_wide)
-    qkv_cut = lax.all_to_all(qkv_cut, TEAM, 0, 0, tiled=True).reshape(N_TEAM * shard, 3 * team_wide)
+    cut, out_there, tokens_later, cotangent_later = lax.optimization_barrier((cut, out_there, tokens, cotangent))
+    at_gate = 3 * team_wide + gains.shape[1]
     out_cut = out_there.reshape(shard, N_TEAM, team_wide).transpose(1, 0, 2)
     out_cut = out_cut.reshape(N_TEAM * shard, team_wide)
-    attn = lax.all_gather(jnp.concatenate([qkv_cut, out_cut], axis=1), FLEET, axis=0, tiled=True)
+    attn = jnp.concatenate([cut[:, :at_gate], out_cut], axis=1)
+    along_y = lambda value, by: from_ahead(value, ("g", "yl"), by)
+    attn_x = [attn, from_ahead(attn, "x", 1), None, from_ahead(attn, "x", 3)]
+    attn_y = [along_y(attn, 1)]
+    x_mine = [tokens_later, from_ahead(tokens_later, "z", 1), None, from_ahead(tokens_later, "z", 3)]
+    attn_x, attn_y, x_mine = lax.optimization_barrier((attn_x, attn_y, x_mine))
+    attn_y += [along_y(attn_x[1], -1), None, along_y(attn_x[3], 1)]
+    attn_x[2] = from_ahead(attn_x[0], "x", 2)
+    x_mine[2] = from_ahead(x_mine[0], "z", 2)
+    attn_x, attn_y, x_mine, cotangent_later = lax.optimization_barrier((attn_x, attn_y, x_mine, cotangent_later))
+    low_half = shard * N_TEAM // 2
+    attn_y[2] = jnp.concatenate(
+        [along_y(attn_x[2][:low_half], 1), along_y(attn_x[2][low_half:], -1)], axis=0
+    )
+    x_mine = jnp.concatenate(x_mine, axis=0)
+    x_other = from_ahead(x_mine, "c", 1)
+    dy_mine = [cotangent_later, from_ahead(cotangent_later, "z", 1), None, from_ahead(cotangent_later, "z", 3)]
+    attn_x, attn_y, x_other, dy_mine, gate_up = lax.optimization_barrier(
+        (attn_x, attn_y, x_other, dy_mine, cut[:, at_gate:])
+    )
+    w_gate_up = lax.all_gather(gate_up, FLEET, axis=0, tiled=True)
+    dy_mine[2] = from_ahead(dy_mine[0], "z", 2)
+    attn = in_order([attn_x, attn_y])
     w_qkv = attn[:, : 3 * team_wide]
-    w_out_team = attn[:, 3 * team_wide :].reshape(N_FLEET, N_TEAM, shard, team_wide)
+    gain_columns = attn[:, 3 * team_wide : at_gate]
+    gain_one = gain_columns[:, 0].reshape(1, width).astype(full)
+    gain_two = gain_columns[:, 1].reshape(1, width).astype(full)
+    w_out_team = attn[:, at_gate:].reshape(N_FLEET, N_TEAM, shard, team_wide)
     w_out_team = w_out_team.transpose(0, 2, 1, 3).reshape(N_FLEET * shard, width)
-
-    def units_cut(weight):
-        cut = weight.reshape(shard, N_FLEET, N_TEAM, unit_rows)
-        cut = jnp.pad(cut, ((0, 0), (0, 0), (0, 0), (0, unit_pad - unit_rows)))
-        return cut.transpose(2, 0, 1, 3).reshape(N_TEAM, shard, units)
-
-    gate_up_cut = jnp.concatenate([units_cut(w_gate), units_cut(w_up)], axis=2)
-    gate_up_cut = lax.all_to_all(gate_up_cut, TEAM, 0, 0, tiled=True)
-    w_gate_up = lax.all_gather(
-        gate_up_cut.reshape(N_TEAM * shard, 2 * units), FLEET, axis=0, tiled=True
-    )
-    down_cut = jnp.pad(w_down, ((0, unit_pad - unit_rows), (0, 0)))
-    w_down_team = lax.all_gather(down_cut, FLEET, axis=0, tiled=True)
 
     order = jnp.arange(N_TEAM, dtype=jnp.int32)
     spot = (jnp.bitwise_xor(order % N_C, c) * N_Z + (order // N_C - z) % N_Z).astype(jnp.int32)
@@ -259,67 +395,86 @@
     mask = (distance >= 0) & (distance < WIN) & (query_segs[:, :, None] == key_segs[:, None, :])
     mask = mask.astype(full)
 
-    token_rows = team_gather(tokens)
-    halo = along_line(lax.dynamic_slice_in_dim(token_rows, last_at, WIN, 0), 1)
-    token_rows = jnp.concatenate([token_rows, halo], axis=0).astype(full)
-    normed = (token_rows * inverse_rms(token_rows) * gain_one).astype(low)
+    half = N_Z * BLOCK
+    last_of = lambda rows: lax.dynamic_slice_in_dim(rows, last_at % half, WIN, 0)
+    halo = along_line(jnp.where(last_at < half, last_of(x_mine), last_of(x_other)), 1)
+    normed = normalised(x_mine, x_other, halo, gain_columns)
     qkv = matmul(normed, w_qkv).astype(low)
+    qkv, dy_mine = lax.optimization_barrier((qkv, dy_mine))
+    dy_mine = jnp.concatenate(dy_mine, axis=0)
+    dy_other = from_ahead(dy_mine, "c", 1)
     mixed = attend(place, qkv, mask)
-    inputs = tokens.astype(full)
-    hidden = inputs + team_scatter(matmul(mixed, w_out_team))
-
-    cotangents = team_gather(cotangent)
+    mixed, dy_other = lax.optimization_barrier((mixed, dy_other))
+    halves = lambda rows: (rows[:half], rows[half : 2 * half])
+    hidden = inputs + z_sum(core_sum(halves(mixed), lambda rows: matmul(rows, w_out_team)))
+
     scale_two = inverse_rms(hidden)
-    again = team_gather((hidden * scale_two * gain_two).astype(low))
-    both = matmul(again, w_gate_up)
-    gate, up = both[:, :units], both[:, units:]
-    sigmoid = jax.nn.sigmoid(gate)
-    silu = gate * sigmoid
-    activated = (silu * up).astype(low)
-    grad_act = matmul_right_t(cotangents, w_down_team)
-    grad_gate = (grad_act * up * sigmoid * (1.0 + gate * (1.0 - sigmoid))).astype(low)
-    grad_up = (grad_act * silu).astype(low)
-    grad_both = jnp.concatenate([grad_gate, grad_up], axis=1)
-    grad_again = team_scatter(matmul_right_t(grad_both, w_gate_up))
-    down_sum = fleet_reduce(matmul_left_t(activated, cotangents))
-    pair_rows = shard // 2
-    gate_up_term = matmul_left_t(again, grad_both).astype(low)
-    gate_up_term = gate_up_term.reshape(N_FLEET, N_TEAM, 2, pair_rows, 2 * units)
-    gate_up_term = gate_up_term.transpose(0, 2, 1, 3, 4).reshape(width, 2 * units)
-    gate_up_sum = fleet_reduce(gate_up_term)
+    again = [jnp.concatenate(z_gather((hidden * scale_two * gain_two).astype(low)), axis=0)]
+    again.append(from_ahead(again[0], "c", 1))
+    dy_rows, activated, grad_both = [dy_mine, dy_other], [], []
+    for rows, dy in zip(again, dy_rows):
+        both = matmul(rows, w_gate_up)
+        gate, up = both[:, :units], both[:, units:]
+        sigmoid = jax.nn.sigmoid(gate)
+        silu = gate * sigmoid
+        activated.append((silu * up).astype(low))
+        grad_act = matmul_right_t(dy, w_down_team)
+        grad_gate = (grad_act * up * sigmoid * (1.0 + gate * (1.0 - sigmoid))).astype(low)
+        grad_up = (grad_act * silu).astype(low)
+        grad_both.append(jnp.concatenate([grad_gate, grad_up], axis=1))
+    again_blocks = core_sum(grad_both, lambda rows: matmul_right_t(rows, w_gate_up))
+    again_blocks, activated, grad_both = lax.optimization_barrier((again_blocks, activated, grad_both))
+    grad_again = z_sum(again_blocks)
+    mlp_term = feed_terms(again, dy_rows, activated, grad_both)
+    grad_again, mlp_term = lax.optimization_barrier((grad_again, mlp_term))
+    mlp_sum = lax.psum_scatter(
+        mlp_term.reshape(-1, 2 * units), ("g", *FLEET), scatter_dimension=0, tiled=True
+    )
 
     gain_two_term, through_second = norm_backward(grad_again, hidden, scale_two, gain_two)
     grad_hidden = cotangent.astype(full) + through_second
-    hidden_low = team_gather(grad_hidden.astype(low))
-    outputs = (hidden + team_scatter(matmul(activated, w_down_team))).astype(low)
-
+    hidden_low = [jnp.concatenate(z_gather(grad_hidden.astype(low)), axis=0)]
+    hidden_low.append(from_ahead(hidden_low[0], "c", 1))
+    activated, hidden_low = lax.optimization_barrier((activated, hidden_low))
+    output_blocks = core_sum(activated, lambda rows: matmul(rows, w_down_team))
+
+    hidden_low = jnp.concatenate(hidden_low, axis=0)
     grad_mixed = matmul_right_t(hidden_low, w_out_team).astype(low)
     grad_qkv, tail, halo_grads = attend_back(place, qkv, mask, grad_mixed)
     tail = tail + along_line(halo_grads, -1).astype(full)
     grad_qkv = lax.dynamic_update_slice(grad_qkv, tail.astype(low), (last_at, team_wide))
-    out_term = matmul_left_t(mixed, hidden_low)
-    grad_normed = team_scatter(matmul_right_t(grad_qkv, w_qkv))
-    qkv_term = matmul_left_t(normed[: N_TEAM * BLOCK], grad_qkv).astype(low)
-    qkv_term = qkv_term.reshape(N_FLEET, N_TEAM, 2, pair_rows, 3 * team_wide)
-    qkv_term = qkv_term.transpose(0, 2, 1, 3, 4).reshape(width, 3 * team_wide)
-    out_term = out_term.astype(low).reshape(N_FLEET, 2, pair_rows, N_TEAM, team_wide)
-    out_term = out_term.transpose(0, 1, 3, 2, 4).reshape(width, team_wide)
-    attn_sum = fleet_reduce(jnp.concatenate([qkv_term, out_term], axis=1))
+    grad_qkv, output_blocks = lax.optimization_barrier((grad_qkv, output_blocks))
+    outputs = (hidden + z_sum(output_blocks)).astype(low)
+    qkv_term = matmul_left_t(normed[: 2 * half], grad_qkv).astype(low)
+    out_term = matmul_left_t(mixed, hidden_low).astype(low).reshape(N_FLEET, shard, N_TEAM, team_wide)
+    out_term = out_term.transpose(0, 2, 1, 3).reshape(width, team_wide)
+    attn_term = jnp.concatenate([qkv_term, out_term], axis=1)
+    attn_term, grad_qkv = lax.optimization_barrier((attn_term, grad_qkv))
+    attn_sum = lax.psum_scatter(attn_term, FLEET, scatter_dimension=0, tiled=True)
+    normed_blocks = core_sum(halves(grad_qkv), lambda rows: matmul_right_t(rows, w_qkv))
+    normed_blocks, outputs = lax.optimization_barrier((normed_blocks, outputs))
+    grad_normed = z_sum(normed_blocks)
+
+    twice = lambda value: jnp.concatenate([value, value], axis=0)
+    gate_up_sum = mlp_sum[: N_TEAM * shard // 2].reshape(N_TEAM, shard // 2, 2 * units)
+    gate_up_sum = lax.all_to_all(twice(gate_up_sum), ("g", *TEAM), 0, 0, tiled=True)
+    gate_up_sum = jnp.concatenate([gate_up_sum[:N_TEAM], gate_up_sum[N_TEAM:]], axis=1)
+    down_sum = unpack_down(mlp_sum[N_TEAM * shard // 2 :], unit_pad // 2, width)
+    down_there = from_ahead(down_sum, "g", 1)
+    mine = lax.axis_index("g") == 0
+    down_grad = jnp.concatenate(
+        [jnp.where(mine, down_sum, down_there), jnp.where(mine, down_there, down_sum)], axis=0
+    )
+    down_grad = down_grad[:unit_rows].astype(full)
+    grad_normed, gate_up_sum, down_grad = lax.optimization_barrier((grad_normed, gate_up_sum, down_grad))
     gain_one_term, through_first = norm_backward(grad_normed, inputs, inverse_rms(inputs), gain_one)
     input_grad = grad_hidden + through_first
-
-    mine = lax.axis_index("g") == 0
-
-    def both_halves(value):
-        other = from_ahead(value, "g", 1)
-        return jnp.concatenate(
-            [jnp.where(mine, value, other), jnp.where(mine, other, value)], axis=-2
-        )
-
-    def to_owners(sums, blocks):
-        sums = lax.all_to_all(sums.reshape(N_TEAM, pair_rows, sums.shape[1]), TEAM, 0, 0, tiled=True)
-        sums = both_halves(sums)
-        return jnp.split(sums, blocks, axis=2)
+    gain_terms = jnp.concatenate(
+        [gain_one_term.reshape(-1, shard), gain_two_term.reshape(-1, shard)], axis=1
+    )
+    gain_sum = jnp.sum(lax.all_to_all(gain_terms, SEQ, 0, 0, tiled=True), axis=0)
+    gain_sum = gain_sum + from_ahead(gain_sum, "g", 1)
+    gain_sum, attn_sum, input_grad = lax.optimization_barrier((gain_sum, attn_sum, input_grad))
 
     def columns(block):
         return block.transpose(1, 0, 2).reshape(shard, width).astype(full)
@@ -328,16 +483,13 @@
         block = block.reshape(N_TEAM, shard, N_FLEET, unit_pad)[..., :unit_rows]
         return block.transpose(1, 2, 0, 3).reshape(shard, N_FLEET * N_TEAM * unit_rows).astype(full)
 
-    gate_cols, up_cols = to_owners(gate_up_sum, 2)
-    down_grad = both_halves(down_sum)[:unit_rows].astype(full)
-    query_cols, key_cols, value_cols = to_owners(attn_sum[:, : 3 * team_wide], 3)
-    out_grad = swapped(attn_sum[:, 3 * team_wide :])
-    out_grad = both_halves(out_grad.reshape(N_TEAM, pair_rows, team_wide))
-    gain_terms = jnp.concatenate(
-        [gain_one_term.reshape(-1, shard), gain_two_term.reshape(-1, shard)], axis=1
-    )
-    gain_sum = jnp.sum(lax.all_to_all(gain_terms, SEQ, 0, 0, tiled=True), axis=0)
-    gain_sum = gain_sum + from_ahead(gain_sum, "g", 1)
+    gate_cols, up_cols = jnp.split(gate_up_sum, 2, axis=2)
+    qkv_sum = attn_sum[:, : 3 * team_wide].reshape(N_TEAM, shard, 3 * team_wide)
+    qkv_sum = lax.all_to_all(twice(qkv_sum), ("g", *TEAM), 0, 0, tiled=True)
+    qkv_sum = qkv_sum[:N_TEAM].astype(full) + qkv_sum[N_TEAM:].astype(full)
+    query_cols, key_cols, value_cols = jnp.split(qkv_sum, 3, axis=2)
+    out_sum = attn_sum[:, 3 * team_wide :].reshape(N_TEAM, shard, team_wide)
+    out_grad = swapped(out_sum).astype(full) + swapped(out_sum, 1).astype(full)
     return (
         outputs,
         input_grad,

time: 763 us -> 511 us (0.67)
  blocking collectives: 150 us -> 0 us
  waiting for transfers between devices: 326 us -> 219 us
  Pallas kernels: 20.3 us -> 43.2 us
  other arithmetic: 40.7 us -> 30.4 us
  starting transfers between devices: 76.3 us -> 84.5 us
    unnamed x1 -> x0, blocking collectives: 150 us -> none
    reduce_scatter x3 -> x2, waiting for transfers between devices: 88.1 us -> 0.01 us  [the longest x1 0.01 us: body(): lax.psum_scatter(mlp_term.reshape(-1, 2 * units), ('g', *FLEET), scatter_...]
    ppermute x37 -> x42, waiting for transfers between devices: 194 us -> 171 us  [from_ahead(): return lax.ppermute(value, axis, [((i + by) % n, i) for i in range(n)])]
    pallas_call x0 -> x3, Pallas kernels: none -> 22.9 us  [the longest x1 17.9 us: feed_terms(): pl.pallas_call(terms_kernel, grid=(N_FLEET,), in_specs=[cut] * 2 + [whole...]
    dot_general x4 -> x2, matrix products: 19.5 us -> 4.99 us  [matmul_left_t(): lax.dot_general(left, right, (((0,), (0,)), ((), ())), preferred_element_...]
    ppermute x2 -> x3, waiting for transfers between devices: 8.3 us -> 22.5 us  [swapped(): lax.ppermute(value, ALL, [(g * n + a, (g ^ across) * n + b) for g in rang...]
    another operation x5 -> x1, other arithmetic: 11.5 us -> 0.18 us
    all_to_all x4 -> x3, waiting for transfers between devices: 16.6 us -> 10.3 us  [the longest x1 9.95 us: body(): lax.all_to_all(cut, TEAM, 0, 0, tiled=True).reshape(N_TEAM * shard, -1)]
  transfers between devices with their start and end apart: 52 -> 55, of which waited for: 31 -> 31; matrix products, arithmetic and copies ran while one was open for 17% -> 22% of each run, Pallas kernels for 3% -> 8%
where the time goes in v2:
time: 511 us; the launch traced here: 504 us
  waiting for transfers between devices  219 us (43%)
  starting transfers between devices  84.5 us (17%)
  matrix products  63.1 us (12%)
  local copies, waits for them, and re-layouts  47.9 us (9%)
  Pallas kernels  43.2 us (8%)
  other arithmetic  30.4 us (6%)
  between operations  15.9 us (3%)
    ppermute x42, waiting for transfers between devices, from_ahead(): return lax.ppermute(value, axis, [((i + by) % n, i) for i in range(n)])  171 us
    ppermute x42, starting transfers between devices, from_ahead(): return lax.ppermute(value, axis, [((i + by) % n, i) for i in range(n)])  39.7 us
    dot_general x7, matrix products, matmul_right_t(): lax.dot_general(left, right, (((1,), (1,)), ((), ())), preferred_element_...  29.8 us
    dot_general x7, matrix products, matmul(): return jnp.dot(left, right, preferred_element_type=full)  28.4 us
    ppermute x3, waiting for transfers between devices, swapped(): lax.ppermute(value, ALL, [(g * n + a, (g ^ across) * n + b) for g in rang...  22.5 us
    pallas_call x1, Pallas kernels, feed_terms(): pl.pallas_call(terms_kernel, grid=(N_FLEET,), in_specs=[cut] * 2 + [whole...  17.9 us
    unnamed x110, local copies, waits for them, and re-layouts  17.2 us
    ppermute x3, starting transfers between devices, swapped(): lax.ppermute(value, ALL, [(g * n + a, (g ^ across) * n + b) for g in rang...  14.2 us
  transfers between devices with their start and end apart: 55, of which 31 were waited for; matrix products, arithmetic and copies ran while one was open for 22% of the time, Pallas kernels for 8%

profile of v2, /device:TPU:8, one launch (start us, length us, event | category | flops | bytes accessed | tf_op | source)
XLA Modules:
  0.0 503.8 jit_solution(12952624400986372379)
XLA Ops:
  15.2 5.3 %all-to-all-start = ((bf16[8,32,2432]{2,1,0:T(8,128)(2,1)}), bf16[8,32,2432]{2,1,0:T(8,128)(2,1)S(1)}, u32[]{:S(2)}, u32[]{:S(2)}) async-start(bf16[8,32,2432]{2,1,0:T(8,128)(2,1)} %shard_map.203), calls=%async_computation | async-start | bytes 2490368 | tf_op jit(solution)/shard_map/all_to_all | solution.py:346
  20.6 5.3 %collective-permute-start = (bf16[32,2048]{1,0:T(8,128)(2,1)S(1)}, bf16[32,2048]{1,0:T(8,128)(2,1)S(1)}, u32[]{:S(2)}, u32[]{:S(2)}) collective-permute-start(bf16[32,2048]{1,0:T(8,128)(2,1)S(1)} %copy-done.46), channel_id=1, source_target_pairs={{0,0},{1,8},{2,16},{3,24},{4,32},{5,40},{6,48},{7,56},{8,1},{9,9},... | collective-permute-start | bytes 393224 | tf_op jit(solution)/shard_map/ppermute | solution.py:40
  25.9 8.4 %collective-permute-done = bf16[32,2048]{1,0:T(8,128)(2,1)S(1)} collective-permute-done((bf16[32,2048]{1,0:T(8,128)(2,1)S(1)}, bf16[32,2048]{1,0:T(8,128)(2,1)S(1)}, u32[]{:S(2)}, u32[]{:S(2)}) %collective-permute-start) | collective-permute-done | bytes 131104 | tf_op jit(solution)/shard_map/ppermute | solution.py:40
  34.3 9.9 %all-to-all-done = bf16[8,32,2432]{2,1,0:T(8,128)(2,1)S(1)} async-done(((bf16[8,32,2432]{2,1,0:T(8,128)(2,1)}), bf16[8,32,2432]{2,1,0:T(8,128)(2,1)S(1)}, u32[]{:S(2)}, u32[]{:S(2)}) %all-to-all-start) | async-done | bytes 1245216 | tf_op jit(solution)/shard_map/all_to_all | solution.py:346
  48.8 10.6 %collective-permute-done.4 = bf16[128,2048]{1,0:T(8,128)(2,1)S(1)} collective-permute-done((bf16[128,2048]{1,0:T(8,128)(2,1)S(1)}, bf16[128,2048]{1,0:T(8,128)(2,1)S(1)}, u32[]{:S(2)}, u32[]{:S(2)}) %collective-permute-start.4) | collective-permute-done | bytes 524320 | tf_op jit(solution)/shard_map/ppermute | solution.py:28
  68.0 10.8 %collective-permute-done.9 = bf16[128,2048]{1,0:T(8,128)(2,1)S(1)} collective-permute-done((bf16[128,2048]{1,0:T(8,128)(2,1)S(1)}, bf16[128,2048]{1,0:T(8,128)(2,1)S(1)}, u32[]{:S(2)}, u32[]{:S(2)}) %collective-permute-start.9) | collective-permute-done | bytes 524320 | tf_op jit(solution)/shard_map/ppermute | solution.py:28
  86.4 4.9 collective-permute-done.11
  109.8 9.5 %collective-permute-done.15.halo_ref = bf16[64,2048]{1,0:T(8,128)(2,1)S(1)} collective-permute-done((bf16[64,2048]{1,0:T(8,128)(2,1)S(1)}, bf16[64,2048]{1,0:T(8,128)(2,1)S(1)}, u32[]{:S(2)}, u32[]{:S(2)}) %collective-permute-start.15) | collective-permute-done | bytes 262176 | tf_op jit(solution)/shard_map/ppermute | solution.py:32
  135.1 8.0 %shard_map.205 = bf16[1024,256]{1,0:T(8,128)(2,1)S(1)} custom-call(s32[16]{0:T(128)S(1)} %pad_add_fusion.place, bf16[1088,768]{1,0:T(8,128)(2,1)S(1)} %convolution_convert_fusion.q_ref.k_ref.v_ref.kp_ref.vp_ref, bf16[1088,768]{1,0:T(8,128)(2,1)S(1)} %convolution_convert_fusion.q_ref.k_ref.v_ref.kp_ref.vp_ref, ...), custom_call_target="tpu_custom_call" | custom-call | tf_op jit(solution)/shard_map/pallas_call | solution.py:282
  156.8 10.9 %collective-permute-done.21 = bf16[128,2048]{1,0:T(8,128)(2,1)S(1)} collective-permute-done((bf16[128,2048]{1,0:T(8,128)(2,1)S(1)}, bf16[128,2048]{1,0:T(8,128)(2,1)S(1)}, u32[]{:S(2)}, u32[]{:S(2)}) %collective-permute-start.21) | collective-permute-done | bytes 524320 | tf_op jit(solution)/shard_map/ppermute | solution.py:28
  169.3 10.6 %collective-permute-done.19 = bf16[128,2048]{1,0:T(8,128)(2,1)S(1)} collective-permute-done((bf16[128,2048]{1,0:T(8,128)(2,1)S(1)}, bf16[128,2048]{1,0:T(8,128)(2,1)S(1)}, u32[]{:S(2)}, u32[]{:S(2)}) %collective-permute-start.19) | collective-permute-done | bytes 524320 | tf_op jit(solution)/shard_map/ppermute | solution.py:28
  187.3 21.8 %collective-permute-done.24 = bf16[128,2048]{1,0:T(8,128)(2,1)S(1)} collective-permute-done((bf16[128,2048]{1,0:T(8,128)(2,1)S(1)}, bf16[128,2048]{1,0:T(8,128)(2,1)S(1)}, u32[]{:S(2)}, u32[]{:S(2)}) %collective-permute-start.24) | collective-permute-done | bytes 524320 | tf_op jit(solution)/shard_map/ppermute | solution.py:28
  211.3 4.3 collective-permute-done.25.x1_ref
  215.6 8.6 %fusion.49 = f32[512,1536]{1,0:T(8,128)} fusion(bf16[512,2048]{1,0:T(8,128)(2,1)} %collective-permute-done.25.x1_ref, bf16[2048,1536]{1,0:T(8,128)(2,1)} %all-gather.5.cloned.1.call-done), kind=kOutput, calls=%fused_computation.153 | convolution fusion | flops 3221225472 | bytes 11534336 | tf_op jit(solution)/shard_map/dot_general | solution.py:74
  224.2 6.8 %multiply_convert_fusion.3 = (bf16[512,768]{1,0:T(8,128)(2,1)S(1)}, bf16[512,768]{1,0:T(8,128)(2,1)S(1)}, bf16[512,768]{1,0:T(8,128)(2,1)}) fusion(f32[512,1536]{1,0:T(8,128)} %fusion.49, bf16[512,2048]{1,0:T(8,128)(2,1)} %collective-permute-done.17.dy1_ref, bf16[768,2048]{1,0:T(8,128)(2,1)} %all-gather.3.cloned.1.call-done), kind=kOutput, calls=%fused_computation.30 | convolution fusion | flops 1616510976 | bytes 10747904 | tf_op jit(solution)/shard_map/dot_general | solution.py:82
  238.6 5.0 multiply_convert_fusion.5
  252.9 17.9 %shard_map.206 = bf16[2,8,192,1536]{3,2,1,0:T(8,128)(2,1)} custom-call(bf16[512,2048]{1,0:T(8,128)(2,1)} %copy-done.15, bf16[512,2048]{1,0:T(8,128)(2,1)} %collective-permute-done.25.x1_ref, bf16[512,2048]{1,0:T(8,128)(2,1)} %constant_dynamic-update-slice_fusion.4.dy0_ref, bf16[512,2048]{1,0:T(8,128)(2,1)} %collective-permute-done.17.dy1_ref, ...), custom_call_target="tpu_custom_call" | custom-call | flops 1 | bytes 1 | tf_op jit(solution)/shard_map/pallas_call | solution.py:189
  270.8 4.1 collective-permute-done.29
  288.0 22.7 %collective-permute-done.32 = bf16[128,2048]{1,0:T(8,128)(2,1)S(1)} collective-permute-done((bf16[128,2048]{1,0:T(8,128)(2,1)S(1)}, bf16[128,2048]{1,0:T(8,128)(2,1)S(1)}, u32[]{:S(2)}, u32[]{:S(2)}) %collective-permute-start.32) | collective-permute-done | bytes 524320 | tf_op jit(solution)/shard_map/ppermute | solution.py:28
  311.7 4.3 collective-permute-done.33
  324.5 12.3 %shard_map.207 = (bf16[1024,768]{1,0:T(8,128)(2,1)S(1)}, f32[64,512]{1,0:T(8,128)S(1)}, bf16[64,512]{1,0:T(8,128)(2,1)S(1)}) custom-call(s32[16]{0:T(128)S(1)} %pad_add_fusion.place, bf16[1088,768]{1,0:T(8,128)(2,1)S(1)} %convolution_convert_fusion.q_ref.k_ref.v_ref.kp_ref.vp_ref, ...), custom_call_target="tpu_custom_call" | custom-call | tf_op jit(solution)/shard_map/pallas_call | solution.py:302
  337.9 5.2 %collective-permute-start.34 = (bf16[64,512]{1,0:T(8,128)(2,1)S(1)}, bf16[64,512]{1,0:T(8,128)(2,1)S(1)}, u32[]{:S(2)}, u32[]{:S(2)}) collective-permute-start(bf16[64,512]{1,0:T(8,128)(2,1)S(1)} %get-tuple-element.145), channel_id=1, source_target_pairs={{8,0},{16,8},{24,16},{32,24},{40,32},{48,40},{56,48},{9,1},{17,9},... | collective-permute-start | bytes 196616 | tf_op jit(solution)/shard_map/ppermute | solution.py:32
  349.2 4.7 convert_add_fusion.1
  361.2 5.1 %convolution_convert_fusion.2 = bf16[512,2048]{1,0:T(8,128)(2,1)} fusion(bf16[2048,1152]{1,0:T(8,128)(2,1)} %copy-done.8, bf16[1024,768]{1,0:T(8,128)(2,1)S(1)} %dynamic_update_slice.35), kind=kOutput, calls=%fused_computation.10 | convolution fusion | flops 1611661312 | bytes 6029312 | tf_op jit(solution)/shard_map/dot_general | solution.py:82
  370.2 22.2 %collective-permute-done.39 = bf16[128,2048]{1,0:T(8,128)(2,1)} collective-permute-done((bf16[128,2048]{1,0:T(8,128)(2,1)}, bf16[128,2048]{1,0:T(8,128)(2,1)}, u32[]{:S(2)}, u32[]{:S(2)}) %collective-permute-start.39) | collective-permute-done | bytes 524320 | tf_op jit(solution)/shard_map/ppermute | solution.py:28
  398.4 4.4 convert_add_fusion
  408.3 5.4 %all-to-all-start.1 = ((bf16[16,16,1536]{2,1,0:T(8,128)(2,1)}), bf16[16,16,1536]{2,1,0:T(8,128)(2,1)S(1)}, u32[]{:S(2)}, u32[]{:S(2)}) async-start(bf16[16,16,1536]{2,1,0:T(8,128)(2,1)} %pad_maximum_fusion.5), calls=%async_computation.2 | async-start | bytes 1572864 | tf_op jit(solution)/shard_map/all_to_all | solution.py:460
  423.7 12.7 %collective-permute-done.40 = bf16[128,2048]{1,0:T(8,128)(2,1)} collective-permute-done((bf16[128,2048]{1,0:T(8,128)(2,1)S(1)}, bf16[128,2048]{1,0:T(8,128)(2,1)}, u32[]{:S(2)}, u32[]{:S(2)}) %collective-permute-start.40) | collective-permute-done | bytes 524320 | tf_op jit(solution)/shard_map/ppermute | solution.py:28
  440.4 7.0 %all-to-all-start.2 = ((f32[64,1,64]{2,1,0:T(1,128)}), f32[64,1,64]{2,1,0:T(1,128)S(1)}, u32[]{:S(2)}, u32[]{:S(2)}) async-start(f32[64,1,64]{2,1,0:T(1,128)} %bitcast.16), calls=%async_computation.3 | async-start | bytes 65536 | tf_op jit(solution)/shard_map/all_to_all | solution.py:475
  448.9 5.7 %all-to-all-done.2 = f32[64,1,64]{2,1,0:T(1,128)S(1)} async-done(((f32[64,1,64]{2,1,0:T(1,128)}), f32[64,1,64]{2,1,0:T(1,128)S(1)}, u32[]{:S(2)}, u32[]{:S(2)}) %all-to-all-start.2) | async-done | bytes 16416 | tf_op jit(solution)/shard_map/all_to_all | solution.py:475
  470.3 5.0 collective-permute-start.46
  479.8 14.1 %collective-permute-done.46 = bf16[8,32,256]{2,1,0:T(8,128)(2,1)S(1)} collective-permute-done((bf16[8,32,256]{2,1,0:T(8,128)(2,1)S(1)}, bf16[8,32,256]{2,1,0:T(8,128)(2,1)S(1)}, u32[]{:S(2)}, u32[]{:S(2)}) %collective-permute-start.46) | collective-permute-done | bytes 131104 | tf_op jit(solution)/shard_map/ppermute | solution.py:40
  (316 shorter events, 194.2 us)
Async XLA Ops:
  15.2 29.0 %all-to-all-start = ((bf16[8,32,2432]{2,1,0:T(8,128)(2,1)}), bf16[8,32,2432]{2,1,0:T(8,128)(2,1)S(1)}, u32[]{:S(2)}, u32[]{:S(2)}) async-start(bf16[8,32,2432]{2,1,0:T(8,128)(2,1)} %shard_map.203), calls=%async_computation | async-start | bytes 2490368 | tf_op jit(solution)/shard_map/all_to_all | solution.py:346
  20.5 195.1 %all-gather.5.cloned.1.call-start = ((), (), s32[]{:S(2)}) async-start(), calls=%async_computation.7 | async-start | bytes 7077888 | tf_op jit(solution)/shard_map/all_gather | solution.py:372
  44.3 18.3 %collective-permute-start.1 = (bf16[256,1152]{1,0:T(8,128)(2,1)S(1)}, bf16[256,1152]{1,0:T(8,128)(2,1)S(1)}, u32[]{:S(2)}, u32[]{:S(2)}) collective-permute-start(bf16[256,1152]{1,0:T(8,128)(2,1)S(1)} %pad_maximum_fusion.8), channel_id=1, source_target_pairs={{8,0},{16,8},{24,16},{0,24},{9,1},{17,9},{25,17},{1,25},{10,2},{18... | collective-permute-start | bytes 1769480 | tf_op jit(solution)/shard_map/ppermute | solution.py:28
  44.4 18.2 %collective-permute-start.2 = (bf16[256,1152]{1,0:T(8,128)(2,1)S(1)}, bf16[256,1152]{1,0:T(8,128)(2,1)S(1)}, u32[]{:S(2)}, u32[]{:S(2)}) collective-permute-start(bf16[256,1152]{1,0:T(8,128)(2,1)S(1)} %pad_maximum_fusion.8), channel_id=1, source_target_pairs={{24,0},{0,8},{8,16},{16,24},{25,1},{1,9},{9,17},{17,25},{26,2},{2,... | collective-permute-start | bytes 1769480 | tf_op jit(solution)/shard_map/ppermute | solution.py:28
  80.0 19.7 %collective-permute-start.12 = (bf16[512,2048]{1,0:T(8,128)(2,1)S(1)}, bf16[512,2048]{1,0:T(8,128)(2,1)}, u32[]{:S(2)}, u32[]{:S(2)}) collective-permute-start(bf16[512,2048]{1,0:T(8,128)(2,1)S(1)} %constant_dynamic-update-slice_fusion.mine_ref), channel_id=1, source_target_pairs={{1,0},{0,1},{3,2},{2,3},{5,4},{4,5},{7,6},{6,7},{9,8},{8,9},{11,10... | collective-permute-start | bytes 6291464 | tf_op jit(solution)/shard_map/ppermute | solution.py:28
  99.8 124.5 %all-gather.3.cloned.1.call-start = ((), (), s32[]{:S(2)}) async-start(), calls=%async_computation.6 | async-start | bytes 3538944 | tf_op jit(solution)/shard_map/all_gather | solution.py:343
  102.3 17.0 %collective-permute-start.15 = (bf16[64,2048]{1,0:T(8,128)(2,1)S(1)}, bf16[64,2048]{1,0:T(8,128)(2,1)S(1)}, u32[]{:S(2)}, u32[]{:S(2)}) collective-permute-start(bf16[64,2048]{1,0:T(8,128)(2,1)S(1)} %dynamic-slice_select_fusion), channel_id=1, source_target_pairs={{0,8},{8,16},{16,24},{24,32},{32,40},{40,48},{48,56},{1,9},{9,17},... | collective-permute-start | bytes 786440 | tf_op jit(solution)/shard_map/ppermute | solution.py:32
  109.1 17.2 %collective-permute-start.16 = (bf16[128,2048]{1,0:T(8,128)(2,1)}, bf16[128,2048]{1,0:T(8,128)(2,1)S(1)}, u32[]{:S(2)}, u32[]{:S(2)}) collective-permute-start(bf16[128,2048]{1,0:T(8,128)(2,1)} %param.23), channel_id=1, source_target_pairs={{4,0},{6,2},{0,4},{2,6},{5,1},{7,3},{1,5},{3,7},{12,8},{14,10},{8,... | collective-permute-start | bytes 1572872 | tf_op jit(solution)/shard_map/ppermute | solution.py:28
  146.7 259.7 %reduce-scatter.3.cloned.1.call-start = ((), (), s32[]{:S(2)}) async-start(), calls=%async_computation.8 | async-start | bytes 10027008 | tf_op jit(solution)/shard_map/reduce_scatter | solution.py:430
  154.6 25.4 %collective-permute-start.19 = (bf16[128,2048]{1,0:T(8,128)(2,1)S(1)}, bf16[128,2048]{1,0:T(8,128)(2,1)S(1)}, u32[]{:S(2)}, u32[]{:S(2)}) collective-permute-start(bf16[128,2048]{1,0:T(8,128)(2,1)S(1)} %get-tuple-element.194), channel_id=1, source_target_pairs={{6,0},{0,2},{2,4},{4,6},{7,1},{1,3},{3,5},{5,7},{14,8},{8,10},{10,... | collective-permute-start | bytes 1572872 | tf_op jit(solution)/shard_map/ppermute | solution.py:28
  182.7 26.4 %collective-permute-start.24 = (bf16[128,2048]{1,0:T(8,128)(2,1)S(1)}, bf16[128,2048]{1,0:T(8,128)(2,1)S(1)}, u32[]{:S(2)}, u32[]{:S(2)}) collective-permute-start(bf16[128,2048]{1,0:T(8,128)(2,1)S(1)} %multiply_convert_fusion.6), channel_id=1, source_target_pairs={{6,0},{0,2},{2,4},{4,6},{7,1},{1,3},{3,5},{5,7},{14,8},{8,10},{10,... | collective-permute-start | bytes 1572872 | tf_op jit(solution)/shard_map/ppermute | solution.py:28
  182.8 26.3 %collective-permute-start.23 = (bf16[128,2048]{1,0:T(8,128)(2,1)S(1)}, bf16[128,2048]{1,0:T(8,128)(2,1)S(1)}, u32[]{:S(2)}, u32[]{:S(2)}) collective-permute-start(bf16[128,2048]{1,0:T(8,128)(2,1)S(1)} %multiply_convert_fusion.6), channel_id=1, source_target_pairs={{4,0},{6,2},{0,4},{2,6},{5,1},{7,3},{1,5},{3,7},{12,8},{14,10},{8,... | collective-permute-start | bytes 1572872 | tf_op jit(solution)/shard_map/ppermute | solution.py:28
  185.4 24.3 %collective-permute-start.22 = (bf16[128,2048]{1,0:T(8,128)(2,1)S(1)}, bf16[128,2048]{1,0:T(8,128)(2,1)S(1)}, u32[]{:S(2)}, u32[]{:S(2)}) collective-permute-start(bf16[128,2048]{1,0:T(8,128)(2,1)S(1)} %multiply_convert_fusion.6), channel_id=1, source_target_pairs={{2,0},{4,2},{6,4},{0,6},{3,1},{5,3},{7,5},{1,7},{10,8},{12,10},{14... | collective-permute-start | bytes 1572872 | tf_op jit(solution)/shard_map/ppermute | solution.py:28
  249.2 25.7 %collective-permute-start.29 = (bf16[128,2048]{1,0:T(8,128)(2,1)S(1)}, bf16[128,2048]{1,0:T(8,128)(2,1)S(1)}, u32[]{:S(2)}, u32[]{:S(2)}) collective-permute-start(bf16[128,2048]{1,0:T(8,128)(2,1)S(1)} %get-tuple-element.137), channel_id=1, source_target_pairs={{2,0},{4,2},{6,4},{0,6},{3,1},{5,3},{7,5},{1,7},{10,8},{12,10},{14... | collective-permute-start | bytes 1572872 | tf_op jit(solution)/shard_map/ppermute | solution.py:28
  251.9 23.0 %collective-permute-start.28 = (bf16[128,2048]{1,0:T(8,128)(2,1)S(1)}, bf16[128,2048]{1,0:T(8,128)(2,1)S(1)}, u32[]{:S(2)}, u32[]{:S(2)}) collective-permute-start(bf16[128,2048]{1,0:T(8,128)(2,1)S(1)} %get-tuple-element.136), channel_id=1, source_target_pairs={{4,0},{6,2},{0,4},{2,6},{5,1},{7,3},{1,5},{3,7},{12,8},{14,10},{8,... | collective-permute-start | bytes 1572872 | tf_op jit(solution)/shard_map/ppermute | solution.py:28
  252.1 26.2 %collective-permute-start.27 = (bf16[128,2048]{1,0:T(8,128)(2,1)S(1)}, bf16[128,2048]{1,0:T(8,128)(2,1)S(1)}, u32[]{:S(2)}, u32[]{:S(2)}) collective-permute-start(bf16[128,2048]{1,0:T(8,128)(2,1)S(1)} %get-tuple-element.135), channel_id=1, source_target_pairs={{6,0},{0,2},{2,4},{4,6},{7,1},{1,3},{3,5},{5,7},{14,8},{8,10},{10,... | collective-permute-start | bytes 1572872 | tf_op jit(solution)/shard_map/ppermute | solution.py:28
  279.6 180.2 %reduce-scatter.5.cloned.1.call-start = ((), (), s32[]{:S(2)}) async-start(), calls=%async_computation.9 | async-start | bytes 4718592 | tf_op jit(solution)/shard_map/reduce_scatter | solution.py:453
  284.5 26.2 %collective-permute-start.32 = (bf16[128,2048]{1,0:T(8,128)(2,1)S(1)}, bf16[128,2048]{1,0:T(8,128)(2,1)S(1)}, u32[]{:S(2)}, u32[]{:S(2)}) collective-permute-start(bf16[128,2048]{1,0:T(8,128)(2,1)S(1)} %get-tuple-element.173), channel_id=1, source_target_pairs={{6,0},{0,2},{2,4},{4,6},{7,1},{1,3},{3,5},{5,7},{14,8},{8,10},{10,... | collective-permute-start | bytes 1572872 | tf_op jit(solution)/shard_map/ppermute | solution.py:28
  284.7 26.0 %collective-permute-start.31 = (bf16[128,2048]{1,0:T(8,128)(2,1)S(1)}, bf16[128,2048]{1,0:T(8,128)(2,1)S(1)}, u32[]{:S(2)}, u32[]{:S(2)}) collective-permute-start(bf16[128,2048]{1,0:T(8,128)(2,1)S(1)} %get-tuple-element.173), channel_id=1, source_target_pairs={{4,0},{6,2},{0,4},{2,6},{5,1},{7,3},{1,5},{3,7},{12,8},{14,10},{8,... | collective-permute-start | bytes 1572872 | tf_op jit(solution)/shard_map/ppermute | solution.py:28
  287.1 24.2 %collective-permute-start.30 = (bf16[128,2048]{1,0:T(8,128)(2,1)S(1)}, bf16[128,2048]{1,0:T(8,128)(2,1)S(1)}, u32[]{:S(2)}, u32[]{:S(2)}) collective-permute-start(bf16[128,2048]{1,0:T(8,128)(2,1)S(1)} %get-tuple-element.173), channel_id=1, source_target_pairs={{2,0},{4,2},{6,4},{0,6},{3,1},{5,3},{7,5},{1,7},{10,8},{12,10},{14... | collective-permute-start | bytes 1572872 | tf_op jit(solution)/shard_map/ppermute | solution.py:28
  319.1 30.1 %collective-permute-start.35 = (bf16[512,2048]{1,0:T(8,128)(2,1)}, bf16[512,2048]{1,0:T(8,128)(2,1)}, u32[]{:S(2)}, u32[]{:S(2)}) collective-permute-start(bf16[512,2048]{1,0:T(8,128)(2,1)} %convolution_convert_fusion.3), channel_id=1, source_target_pairs={{1,0},{0,1},{3,2},{2,3},{5,4},{4,5},{7,6},{6,7},{9,8},{8,9},{11,10... | collective-permute-start | bytes 6291464 | tf_op jit(solution)/shard_map/ppermute | solution.py:28
  366.4 32.0 %collective-permute-start.36 = (bf16[512,2048]{1,0:T(8,128)(2,1)}, bf16[512,2048]{1,0:T(8,128)(2,1)}, u32[]{:S(2)}, u32[]{:S(2)}) collective-permute-start(bf16[512,2048]{1,0:T(8,128)(2,1)} %convolution_convert_fusion.2), channel_id=1, source_target_pairs={{1,0},{0,1},{3,2},{2,3},{5,4},{4,5},{7,6},{6,7},{9,8},{8,9},{11,10... | collective-permute-start | bytes 6291464 | tf_op jit(solution)/shard_map/ppermute | solution.py:28
  367.0 25.5 %collective-permute-start.39 = (bf16[128,2048]{1,0:T(8,128)(2,1)}, bf16[128,2048]{1,0:T(8,128)(2,1)}, u32[]{:S(2)}, u32[]{:S(2)}) collective-permute-start(bf16[128,2048]{1,0:T(8,128)(2,1)} %get-tuple-element.153), channel_id=1, source_target_pairs={{2,0},{4,2},{6,4},{0,6},{3,1},{5,3},{7,5},{1,7},{10,8},{12,10},{14... | collective-permute-start | bytes 1572872 | tf_op jit(solution)/shard_map/ppermute | solution.py:28
  369.3 23.2 %collective-permute-start.38 = (bf16[128,2048]{1,0:T(8,128)(2,1)}, bf16[128,2048]{1,0:T(8,128)(2,1)}, u32[]{:S(2)}, u32[]{:S(2)}) collective-permute-start(bf16[128,2048]{1,0:T(8,128)(2,1)} %get-tuple-element.152), channel_id=1, source_target_pairs={{4,0},{6,2},{0,4},{2,6},{5,1},{7,3},{1,5},{3,7},{12,8},{14,10},{8,... | collective-permute-start | bytes 1572872 | tf_op jit(solution)/shard_map/ppermute | solution.py:28
  369.3 26.3 %collective-permute-start.37 = (bf16[128,2048]{1,0:T(8,128)(2,1)S(1)}, bf16[128,2048]{1,0:T(8,128)(2,1)}, u32[]{:S(2)}, u32[]{:S(2)}) collective-permute-start(bf16[128,2048]{1,0:T(8,128)(2,1)S(1)} %get-tuple-element.151), channel_id=1, source_target_pairs={{6,0},{0,2},{2,4},{4,6},{7,1},{1,3},{3,5},{5,7},{14,8},{8,10},{10,... | collective-permute-start | bytes 1572872 | tf_op jit(solution)/shard_map/ppermute | solution.py:28
  405.3 17.6 %collective-permute-start.41 = (bf16[128,2048]{1,0:T(8,128)(2,1)}, bf16[128,2048]{1,0:T(8,128)(2,1)S(1)}, u32[]{:S(2)}, u32[]{:S(2)}) collective-permute-start(bf16[128,2048]{1,0:T(8,128)(2,1)} %get-tuple-element.157), channel_id=1, source_target_pairs={{4,0},{6,2},{0,4},{2,6},{5,1},{7,3},{1,5},{3,7},{12,8},{14,10},{8,... | collective-permute-start | bytes 1572872 | tf_op jit(solution)/shard_map/ppermute | solution.py:28
  405.5 30.8 %collective-permute-start.40 = (bf16[128,2048]{1,0:T(8,128)(2,1)S(1)}, bf16[128,2048]{1,0:T(8,128)(2,1)}, u32[]{:S(2)}, u32[]{:S(2)}) collective-permute-start(bf16[128,2048]{1,0:T(8,128)(2,1)S(1)} %get-tuple-element.156), channel_id=1, source_target_pairs={{6,0},{0,2},{2,4},{4,6},{7,1},{1,3},{3,5},{5,7},{14,8},{8,10},{10,... | collective-permute-start | bytes 1572872 | tf_op jit(solution)/shard_map/ppermute | solution.py:28
  408.3 30.9 %all-to-all-start.1 = ((bf16[16,16,1536]{2,1,0:T(8,128)(2,1)}), bf16[16,16,1536]{2,1,0:T(8,128)(2,1)S(1)}, u32[]{:S(2)}, u32[]{:S(2)}) async-start(bf16[16,16,1536]{2,1,0:T(8,128)(2,1)} %pad_maximum_fusion.5), calls=%async_computation.2 | async-start | bytes 1572864 | tf_op jit(solution)/shard_map/all_to_all | solution.py:460
  414.6 23.2 %collective-permute-start.43 = (bf16[48,2048]{1,0:T(8,128)(2,1)S(1)}, bf16[48,2048]{1,0:T(8,128)(2,1)S(1)}, u32[]{:S(2)}, u32[]{:S(2)}) collective-permute-start(bf16[48,2048]{1,0:T(8,128)(2,1)S(1)} %maximum_maximum_fusion), channel_id=1, source_target_pairs={{64,0},{0,64},{65,1},{1,65},{66,2},{2,66},{67,3},{3,67},{68,4},{4,... | collective-permute-start | bytes 589832 | tf_op jit(solution)/shard_map/ppermute | solution.py:28
  461.9 32.8 %all-to-all-start.3 = ((bf16[16,32,768]{2,1,0:T(8,128)(2,1)}), bf16[16,32,768]{2,1,0:T(8,128)(2,1)S(1)}, u32[]{:S(2)}, u32[]{:S(2)}) async-start(bf16[16,32,768]{2,1,0:T(8,128)(2,1)} %pad_maximum_fusion.7), calls=%async_computation.5 | async-start | bytes 1572864 | tf_op jit(solution)/shard_map/all_to_all | solution.py:488
  470.3 23.6 %collective-permute-start.46 = (bf16[8,32,256]{2,1,0:T(8,128)(2,1)S(1)}, bf16[8,32,256]{2,1,0:T(8,128)(2,1)S(1)}, u32[]{:S(2)}, u32[]{:S(2)}) collective-permute-start(bf16[8,32,256]{2,1,0:T(8,128)(2,1)S(1)} %bitcast.101), channel_id=1, source_target_pairs={{0,64},{1,72},{2,80},{3,88},{4,96},{5,104},{6,112},{7,120},{8,65},... | collective-permute-start | bytes 393224 | tf_op jit(solution)/shard_map/ppermute | solution.py:40
  475.3 18.6 %collective-permute-start.45 = (bf16[8,32,256]{2,1,0:T(8,128)(2,1)S(1)}, bf16[8,32,256]{2,1,0:T(8,128)(2,1)S(1)}, u32[]{:S(2)}, u32[]{:S(2)}) collective-permute-start(bf16[8,32,256]{2,1,0:T(8,128)(2,1)S(1)} %bitcast.102), channel_id=1, source_target_pairs={{0,0},{1,8},{2,16},{3,24},{4,32},{5,40},{6,48},{7,56},{8,1},{9,9},... | collective-permute-start | bytes 393224 | tf_op jit(solution)/shard_map/ppermute | solution.py:40
  (74 other events, 674.8 us)
Sparse Core Ops, SparseCore 0:
  99.9 73.3 all-gather.4
  174.9 39.2 all-gather.2
  279.7 84.4 reduce-scatter.2
  366.6 51.8 reduce-scatter.4

commit v3 on v2

v3 whole, which is shorter than its diff:
```python
import functools

import jax
import jax.numpy as jnp
from jax import lax
from jax.experimental import pallas as pl
from jax.experimental.pallas import tpu as pltpu
from jax.sharding import Mesh
from jax.sharding import PartitionSpec as P

FILLS = pl.CostEstimate(flops=1, bytes_accessed=1, transcendentals=0)
HEAD = 128
WIN = 64
BLOCK = 128
epsilon = 1e-06

TEAM = ("z", "c")
FLEET = ("yl", "x")
SEQ = ("yl", "x", "z", "c")
ALL = ("g", "yl", "x", "z", "c")
N_X, N_Z, N_C, N_TEAM, N_FLEET = 4, 4, 2, 8, 8
SCALE = HEAD ** (-0.5)
low = jnp.bfloat16
full = jnp.float32


def from_ahead(value, axis, by):
    n = lax.axis_size(axis)
    return lax.ppermute(value, axis, [((i + by) % n, i) for i in range(n)])


def along_line(value, by):
    return lax.ppermute(
        value, FLEET, [(i, i + by) for i in range(N_FLEET) if 0 <= i + by < N_FLEET]
    )


def swapped(value, across=0):
    n = N_FLEET * N_TEAM
    pairs = [(N_TEAM * f + t, N_TEAM * t + f) for f in range(N_FLEET) for t in range(N_TEAM)]
    return lax.ppermute(value, ALL, [(g * n + a, (g ^ across) * n + b) for g in range(2) for a, b in pairs])


def z_gather(value):
    return [value] + [from_ahead(value, "z", k) for k in (1, 2, 3)]


def z_send(blocks):
    return [blocks[0]] + [from_ahead(blocks[k], "z", -k) for k in (1, 2, 3)]


def core_sum(left, right):
    there = right(left[1]).astype(low)
    return core_blocks(right(left[0]), there)


def inverse_rms(values):
    return lax.rsqrt(jnp.mean(values * values, axis=-1, keepdims=True) + epsilon)


def matmul(left, right):
    return jnp.dot(left, right, preferred_element_type=full)


def matmul_left_t(left, right):
    return lax.dot_general(left, right, (((0,), (0,)), ((), ())), preferred_element_type=full)


def matmul_right_t(left, right):
    return lax.dot_general(left, right, (((1,), (1,)), ((), ())), preferred_element_type=full)


def attn_cut_kernel(q_ref, k_ref, v_ref, gain_ref, out_ref):
    wide = q_ref.shape[1] // N_TEAM
    for t in range(N_TEAM):
        for i, ref in enumerate((q_ref, k_ref, v_ref)):
            out_ref[t, :, i * wide : (i + 1) * wide] = ref[:, t * wide : (t + 1) * wide]
        out_ref[t, :, 3 * wide :] = gain_ref[...]


def feed_cut_kernel(unit_rows, gate_ref, up_ref, out_ref):
    units = out_ref.shape[2] // 2
    pad = units // N_FLEET
    out_ref[...] = jnp.zeros(out_ref.shape, low)
    for t in range(N_TEAM):
        for i, ref in enumerate((gate_ref, up_ref)):
            for f in range(N_FLEET):
                at = i * units + f * pad
                first = (f * N_TEAM + t) * unit_rows
                out_ref[t, :, at : at + unit_rows] = ref[:, first : first + unit_rows]


def attn_cut(w_query, w_key, w_value, gains):
    shard, width = w_query.shape
    return pl.pallas_call(
        attn_cut_kernel,
        out_shape=jax.ShapeDtypeStruct((N_TEAM, shard, 3 * width // N_TEAM + gains.shape[1]), low),
        compiler_params=pltpu.CompilerParams(vmem_limit_bytes=8 << 20),
    )(w_query, w_key, w_value, gains)


def feed_cut(w_gate, w_up, unit_rows, units):
    return pl.pallas_call(
        functools.partial(feed_cut_kernel, unit_rows),
        out_shape=jax.ShapeDtypeStruct((N_TEAM, w_gate.shape[0], 2 * units), low),
        compiler_params=pltpu.CompilerParams(vmem_limit_bytes=8 << 20),
        cost_estimate=FILLS,
    )(w_gate, w_up)


def join_kernel(*refs):
    rows = refs[0].shape[0]
    for i, ref in enumerate(refs[:-1]):
        refs[-1][i * rows : (i + 1) * rows] = ref[...]


def join(blocks):
    rows, width = blocks[0].shape
    return pl.pallas_call(
        join_kernel,
        out_shape=jax.ShapeDtypeStruct((len(blocks) * rows, width), low),
        compiler_params=pltpu.CompilerParams(vmem_limit_bytes=8 << 20),
        cost_estimate=FILLS,
    )(*blocks)


def pair_kernel(here_ref, there_ref, own_ref, *block_refs):
    rows = own_ref.shape[0]
    for i, ref in enumerate((own_ref, *block_refs)):
        at = slice(i * rows, (i + 1) * rows)
        ref[...] = (here_ref[at] + there_ref[at].astype(full)).astype(ref.dtype)


def core_blocks(here, there):
    rows, width = here.shape[0] // N_Z, here.shape[1]
    return pl.pallas_call(
        pair_kernel,
        out_shape=[jax.ShapeDtypeStruct((rows, width), full)] + [jax.ShapeDtypeStruct((rows, width), low)] * 3,
        compiler_params=pltpu.CompilerParams(vmem_limit_bytes=12 << 20),
        cost_estimate=FILLS,
    )(here, from_ahead(there, "c", 1))


def norm_kernel(*refs):
    *block_refs, gain_ref, out_ref, rows_ref = refs
    rows_ref[...] = gain_ref[...].astype(full).T[: rows_ref.shape[0]]
    gain = rows_ref[:1]
    at = 0
    for ref in block_refs:
        for first in range(0, ref.shape[0], 16):
            values = ref[first : first + 16].astype(full)
            out_ref[at + first : at + first + 16] = (values * inverse_rms(values) * gain).astype(low)
        at += ref.shape[0]


def normalised(blocks, gain_columns):
    rows = sum(block.shape[0] for block in blocks)
    width = blocks[0].shape[1]
    return pl.pallas_call(
        norm_kernel,
        out_shape=[jax.ShapeDtypeStruct((rows, width), low), jax.ShapeDtypeStruct((8, width), full)],
        compiler_params=pltpu.CompilerParams(vmem_limit_bytes=14 << 20),
        cost_estimate=FILLS,
    )(*blocks, gain_columns)


TILE = 256


def feed_kernel(*refs):
    sources = refs[: 2 * N_Z]
    gate_ref, up_ref, down_ref, act_ref, grad_gate_ref, grad_up_ref, x_ref, dy_ref, arrived = refs[2 * N_Z :]
    rows = sources[0].shape[0]

    @pl.when(pl.program_id(0) == 0)
    def _():
        places = [ref.at[pl.ds(i * rows, rows)] for ref in (x_ref, dy_ref) for i in range(N_Z)]
        copies = [pltpu.make_async_copy(sources[i], places[i], arrived.at[i]) for i in range(2 * N_Z)]
        for copy in copies:
            copy.start()
        for copy in copies:
            copy.wait()

    gate = matmul(x_ref[...], gate_ref[...])
    up = matmul(x_ref[...], up_ref[...])
    grad_act = matmul_right_t(dy_ref[...], down_ref[...])
    sigmoid = jax.nn.sigmoid(gate)
    silu = gate * sigmoid
    act_ref[...] = (silu * up).astype(low)
    grad_gate_ref[...] = (grad_act * up * sigmoid * (1.0 + gate * (1.0 - sigmoid))).astype(low)
    grad_up_ref[...] = (grad_act * silu).astype(low)


def feed(rows, dy_rows, w_gate_up, w_down):
    block, width = rows[0].shape
    units = w_down.shape[0]
    tiles = units // TILE
    whole = pl.BlockSpec((N_Z * block, width), lambda j: (0, 0))
    tile = pl.BlockSpec((N_Z * block, TILE), lambda j: (0, j))
    return pl.pallas_call(
        feed_kernel,
        grid=(tiles,),
        in_specs=[pl.BlockSpec(memory_space=pl.ANY)] * (2 * N_Z)
        + [
            pl.BlockSpec((width, TILE), lambda j: (0, j)),
            pl.BlockSpec((width, TILE), lambda j: (0, tiles + j)),
            pl.BlockSpec((TILE, width), lambda j: (j, 0)),
        ],
        out_specs=[tile] * 3 + [whole] * 2,
        out_shape=[jax.ShapeDtypeStruct((N_Z * block, units), low)] * 3
        + [jax.ShapeDtypeStruct((N_Z * block, width), low)] * 2,
        scratch_shapes=[pltpu.SemaphoreType.DMA((2 * N_Z,))],
        compiler_params=pltpu.CompilerParams(vmem_limit_bytes=24 << 20),
        cost_estimate=FILLS,
    )(*rows, *dy_rows, w_gate_up, w_gate_up, w_down)


def unpack_kernel(packed_ref, gate_up_ref, down_ref):
    block = gate_up_ref.shape[0]
    gate_up_ref[...] = packed_ref[0, :block]
    rows, width = down_ref.shape
    for (row, col), (to, lane) in down_chunks(rows, width, gate_up_ref.shape[1]):
        down_ref[row : row + 16, col : col + 512] = packed_ref[
            0, block + to : block + to + 16, lane : lane + 512
        ]


def unpack(packed, block, rows, width):
    fleet, tall, wide = packed.shape
    return pl.pallas_call(
        unpack_kernel,
        grid=(fleet,),
        in_specs=[pl.BlockSpec((1, tall, wide), lambda s: (s, 0, 0))],
        out_specs=[pl.BlockSpec((block, wide), lambda s: (s, 0)), pl.BlockSpec((rows, width), lambda s: (s, 0))],
        out_shape=[
            jax.ShapeDtypeStruct((fleet * block, wide), low),
            jax.ShapeDtypeStruct((fleet * rows, width), low),
        ],
        compiler_params=pltpu.CompilerParams(vmem_limit_bytes=10 << 20),
        cost_estimate=FILLS,
    )(packed)


def feed_back_kernel(gate_ref, up_ref, right_ref, out_ref):
    units = gate_ref.shape[1]
    out_ref[...] = (
        matmul_right_t(gate_ref[...], right_ref[:, :units]) + matmul_right_t(up_ref[...], right_ref[:, units:])
    ).astype(out_ref.dtype)


def feed_back(grad_gate, grad_up, w_gate_up, dtype):
    rows, units = grad_gate.shape
    width = w_gate_up.shape[0]
    whole = pl.BlockSpec((rows, units), lambda j: (0, 0))
    return pl.pallas_call(
        feed_back_kernel,
        grid=(width // 512,),
        in_specs=[whole, whole, pl.BlockSpec((512, 2 * units), lambda j: (j, 0))],
        out_specs=pl.BlockSpec((rows, 512), lambda j: (0, j)),
        out_shape=jax.ShapeDtypeStruct((rows, width), dtype),
        compiler_params=pltpu.CompilerParams(vmem_limit_bytes=20 << 20),
        cost_estimate=FILLS,
    )(grad_gate, grad_up, w_gate_up)


def terms_kernel(
    x0_ref, x1_ref, dy0_ref, dy1_ref, act0_ref, act1_ref, gate0_ref, gate1_ref, up0_ref, up1_ref, out_ref, down
):
    step = pl.program_id(0)
    units = act0_ref.shape[1]
    pad = units // N_FLEET
    block = x0_ref.shape[1]

    @pl.when(step == 0)
    def _():
        for first in range(0, units, TILE):
            at = slice(first, first + TILE)
            down[at] = (
                matmul_left_t(act0_ref[:, at], dy0_ref[...]) + matmul_left_t(act1_ref[:, at], dy1_ref[...])
            ).astype(low)

    for i, (grad0_ref, grad1_ref) in enumerate(((gate0_ref, gate1_ref), (up0_ref, up1_ref))):
        at = slice(i * units, (i + 1) * units)
        term = matmul_left_t(x0_ref[...], grad0_ref[...]) + matmul_left_t(x1_ref[...], grad1_ref[...])
        term = term.astype(low)
        for row in range(0, block, 32):
            for g in range(2):
                out_ref[g, 0, row // 2 : row // 2 + 16, at] = term[row + 16 * g : row + 16 * g + 16]
    rows = down[pl.ds(pl.multiple_of(step * pad, 16), pad)]
    for g in range(2):
        for (row, col), (to, lane) in down_chunks(pad // 2, rows.shape[1], 2 * units):
            first = g * (pad // 2) + row
            out_ref[g, 0, block // 2 + to : block // 2 + to + 16, lane : lane + 512] = rows[
                first : first + 16, col : col + 512
            ]


def down_chunks(rows, width, wide):
    packed = rows * width // wide
    places = [(row, col) for col in range(0, width, 512) for row in range(0, rows, 16)]
    return [(place, (16 * i % packed, 16 * i // packed * 512)) for i, place in enumerate(places)]


def pack_kernel(down_ref, out_ref):
    rows, width = out_ref.shape[0] * out_ref.shape[1] // down_ref.shape[1], down_ref.shape[1]
    held = down_ref[...]
    held = jnp.concatenate([held, jnp.zeros((rows - held.shape[0], width), low)], axis=0)
    for (row, col), (to, lane) in down_chunks(rows, width, out_ref.shape[1]):
        out_ref[to : to + 16, lane : lane + 512] = held[row : row + 16, col : col + 512]


def pack(down, rows, wide):
    return pl.pallas_call(
        pack_kernel,
        out_shape=jax.ShapeDtypeStruct((rows * down.shape[1] // wide, wide), low),
        compiler_params=pltpu.CompilerParams(vmem_limit_bytes=8 << 20),
        cost_estimate=FILLS,
    )(down)


def unpack_down(packed, rows, width):
    parts = {
        place: packed[to : to + 16, lane : lane + 512]
        for place, (to, lane) in down_chunks(rows, width, packed.shape[1])
    }
    return jnp.concatenate(
        [jnp.concatenate([parts[row, col] for col in range(0, width, 512)], axis=1) for row in range(0, rows, 16)],
        axis=0,
    )


def feed_terms(rows, dy_rows, activated, grad_gate, grad_up):
    half, width = rows[0].shape
    units = activated[0].shape[1]
    block = width // N_FLEET
    tall = block // 2 + units // N_FLEET // 2 * width // (2 * units)
    whole = lambda wide: pl.BlockSpec((half, wide), lambda s: (0, 0))
    cut = pl.BlockSpec((half, block), lambda s: (0, s))
    return pl.pallas_call(
        terms_kernel,
        grid=(N_FLEET,),
        in_specs=[cut] * 2 + [whole(width)] * 2 + [whole(units)] * 6,
        out_specs=pl.BlockSpec((2, 1, tall, 2 * units), lambda s: (0, s, 0, 0)),
        out_shape=pltpu.HBM((2, N_FLEET, tall, 2 * units), low),
        scratch_shapes=[pltpu.VMEM((units, width), low)],
        compiler_params=pltpu.CompilerParams(vmem_limit_bytes=28 << 20),
        cost_estimate=pl.CostEstimate(flops=10**10, bytes_accessed=2 * 10**7, transcendentals=0),
    )(*rows, *dy_rows, *activated, *grad_gate, *grad_up)


def down_kernel(left0_ref, left1_ref, right_ref, here_ref, there_ref):
    here_ref[...] = matmul(left0_ref[...], right_ref[...])
    there_ref[...] = matmul(left1_ref[...], right_ref[...]).astype(low)


def down_parts(left, right):
    half, depth = left[0].shape
    width = right.shape[1]
    whole = pl.BlockSpec((half, depth), lambda j: (0, 0))
    tile = pl.BlockSpec((half, 512), lambda j: (0, j))
    return pl.pallas_call(
        down_kernel,
        grid=(width // 512,),
        in_specs=[whole, whole, pl.BlockSpec((depth, 512), lambda j: (0, j))],
        out_specs=[tile, tile],
        out_shape=[jax.ShapeDtypeStruct((half, width), full), jax.ShapeDtypeStruct((half, width), low)],
        compiler_params=pltpu.CompilerParams(vmem_limit_bytes=16 << 20),
        cost_estimate=FILLS,
    )(*left, right)


def segment_numbers(positions, lengths):
    row_ends = jnp.cumsum(lengths)
    return jnp.sum((positions[..., None] >= row_ends).astype(jnp.int32), axis=-1)


def probabilities(query, keys, mask):
    scores = matmul_right_t(query, keys) * SCALE
    scores = jnp.where(mask > 0, scores, -1e30)
    weights = jnp.exp(scores - jnp.max(scores, axis=-1, keepdims=True))
    return weights / jnp.sum(weights, axis=-1, keepdims=True)


def attend_kernel(place, q_ref, k_ref, v_ref, kp_ref, vp_ref, halo_ref, mask_ref, out_ref):
    mask = mask_ref[0]
    wide = q_ref.shape[1]
    at_start = pl.program_id(0) == 0
    for head in range(wide // HEAD):
        at = slice(head * HEAD, (head + 1) * HEAD)
        at_value = slice(wide + head * HEAD, wide + (head + 1) * HEAD)
        keys = jnp.concatenate([jnp.where(at_start, halo_ref[:, at], kp_ref[:, at]), k_ref[:, at]], axis=0)
        values = jnp.concatenate([jnp.where(at_start, halo_ref[:, at_value], vp_ref[:, at]), v_ref[:, at]], axis=0)
        probs = probabilities(q_ref[:, at], keys, mask)
        out_ref[:, at] = matmul(probs.astype(low), values).astype(low)


def block_gradients(query, keys, values, mask, grad_mixed):
    probs = probabilities(query, keys, mask)
    grad_probs = matmul_right_t(grad_mixed, values)
    inner = jnp.sum(probs * grad_probs, axis=-1, keepdims=True)
    return (probs * (grad_probs - inner)).astype(low), probs.astype(low)


def halo_back_kernel(place, q_ref, k_ref, v_ref, halo_ref, mask_ref, gm_ref, back_ref):
    wide = q_ref.shape[1]
    for head in range(wide // HEAD):
        at = slice(head * HEAD, (head + 1) * HEAD)
        at_value = slice(wide + head * HEAD, wide + (head + 1) * HEAD)
        keys = jnp.concatenate([halo_ref[:, at], k_ref[:, at]], axis=0)
        values = jnp.concatenate([halo_ref[:, at_value], v_ref[:, at]], axis=0)
        grad_scores, probs = block_gradients(q_ref[:, at], keys, values, mask_ref[0], gm_ref[:, at])
        back_ref[:, at] = (matmul_left_t(grad_scores, q_ref[:, at])[:WIN] * SCALE).astype(low)
        back_ref[:, at_value] = matmul_left_t(probs, gm_ref[:, at])[:WIN].astype(low)


def halo_back(place, qkv, halo, mask, grad_mixed):
    wide = qkv.shape[1] // 3
    block = lambda column: pl.BlockSpec((BLOCK, wide), lambda s, place: (place[0], column))
    once = pl.BlockSpec((WIN, 2 * wide), lambda s, place: (0, 0))
    return pl.pallas_call(
        halo_back_kernel,
        grid_spec=pltpu.PrefetchScalarGridSpec(
            num_scalar_prefetch=1,
            grid=(1,),
            in_specs=[block(0), block(1), block(2), once]
            + [pl.BlockSpec((1, BLOCK, BLOCK + WIN), lambda s, place: (place[0], 0, 0)), block(0)],
            out_specs=once,
        ),
        out_shape=jax.ShapeDtypeStruct((WIN, 2 * wide), low),
        compiler_params=pltpu.CompilerParams(vmem_limit_bytes=8 << 20),
        cost_estimate=FILLS,
    )(place, qkv, qkv, qkv, halo, mask, grad_mixed)


def attend_back_kernel(
    place, q_ref, k_ref, v_ref, kp_ref, vp_ref, halo_ref, mask_ref, gm_ref, grads_ref, tail_ref, carry
):
    step = pl.program_id(0)
    mask = mask_ref[0]
    wide = q_ref.shape[1]
    at_start = step == N_TEAM - 1

    @pl.when(step == 0)
    def _():
        carry[...] = jnp.zeros_like(carry)

    for head in range(wide // HEAD):
        at = slice(head * HEAD, (head + 1) * HEAD)
        at_value = slice(wide + head * HEAD, wide + (head + 1) * HEAD)
        query = q_ref[:, at]
        keys = jnp.concatenate([jnp.where(at_start, halo_ref[:, at], kp_ref[:, at]), k_ref[:, at]], axis=0)
        values = jnp.concatenate([jnp.where(at_start, halo_ref[:, at_value], vp_ref[:, at]), v_ref[:, at]], axis=0)
        grad_mixed = gm_ref[:, at]
        grad_scores, probs = block_gradients(query, keys, values, mask, grad_mixed)
        grads_ref[:, at] = (matmul(grad_scores, keys) * SCALE).astype(low)
        grad_keys = matmul_left_t(grad_scores, query) * SCALE
        grad_values = matmul_left_t(probs, grad_mixed)
        for here, grad in ((at, grad_keys), (at_value, grad_values)):
            there = slice(wide + here.start, wide + here.stop)
            last = grad[BLOCK:] + carry[:, here]
            grads_ref[: BLOCK - WIN, there] = grad[WIN:BLOCK].astype(low)
            grads_ref[BLOCK - WIN :, there] = last.astype(low)

            @pl.when(step == 0)
            def _(last=last, here=here):
                tail_ref[:, here] = last

            carry[:, here] = grad[:WIN]


def attention_specs(wide, step):
    def block(rows, column, first):
        return pl.BlockSpec((rows, wide), lambda s, place: (place[first + step(s)], column))

    return [
        block(BLOCK, 0, 0),
        block(BLOCK, 1, 0),
        block(BLOCK, 2, 0),
        block(WIN, 1, N_TEAM),
        block(WIN, 2, N_TEAM),
        pl.BlockSpec((WIN, 2 * wide), lambda s, place: (0, 0)),
        pl.BlockSpec((1, BLOCK, BLOCK + WIN), lambda s, place: (place[step(s)], 0, 0)),
    ]


def attend(place, qkv, halo, mask):
    wide = qkv.shape[1] // 3
    return pl.pallas_call(
        attend_kernel,
        grid_spec=pltpu.PrefetchScalarGridSpec(
            num_scalar_prefetch=1,
            grid=(N_TEAM,),
            in_specs=attention_specs(wide, lambda s: s),
            out_specs=pl.BlockSpec((BLOCK, wide), lambda s, place: (place[s], 0)),
        ),
        out_shape=jax.ShapeDtypeStruct((N_TEAM * BLOCK, wide), low),
        compiler_params=pltpu.CompilerParams(vmem_limit_bytes=8 << 20),
        cost_estimate=FILLS,
    )(place, qkv, qkv, qkv, qkv, qkv, halo, mask)


def attend_back(place, qkv, halo, mask, grad_mixed):
    wide = qkv.shape[1] // 3
    step = lambda s: N_TEAM - 1 - s
    by_block = lambda width: pl.BlockSpec((BLOCK, width), lambda s, place: (place[step(s)], 0))
    once = pl.BlockSpec((WIN, 2 * wide), lambda s, place: (0, 0))
    return pl.pallas_call(
        attend_back_kernel,
        grid_spec=pltpu.PrefetchScalarGridSpec(
            num_scalar_prefetch=1,
            grid=(N_TEAM,),
            in_specs=attention_specs(wide, step) + [by_block(wide)],
            out_specs=[by_block(3 * wide), once],
            scratch_shapes=[pltpu.VMEM((WIN, 2 * wide), full)],
        ),
        out_shape=[
            jax.ShapeDtypeStruct((N_TEAM * BLOCK, 3 * wide), low),
            jax.ShapeDtypeStruct((WIN, 2 * wide), full),
        ],
        compiler_params=pltpu.CompilerParams(vmem_limit_bytes=8 << 20),
        cost_estimate=FILLS,
    )(place, qkv, qkv, qkv, qkv, qkv, halo, mask, grad_mixed)


def attn_terms_kernel(normed_ref, grad_ref, mixed_ref, hidden0_ref, hidden1_ref, out_ref, out_term):
    step = pl.program_id(0)
    half = hidden0_ref.shape[0]
    wide, deep = mixed_ref.shape[1], grad_ref.shape[1]
    rows = wide // N_FLEET

    @pl.when(step == 0)
    def _():
        out_term[...] = (
            matmul_left_t(mixed_ref[:half], hidden0_ref[...]) + matmul_left_t(mixed_ref[half:], hidden1_ref[...])
        ).astype(low)

    out_ref[:, :deep] = matmul_left_t(normed_ref[...], grad_ref[...]).astype(low)
    part = out_term[pl.ds(pl.multiple_of(step * rows, 32), rows)]
    for t in range(N_TEAM):
        out_ref[rows * t : rows * (t + 1), deep:] = part[:, wide * t : wide * (t + 1)]


def attn_terms(normed, grad_qkv, mixed, hidden_low):
    rows, width = normed.shape
    half, wide, deep = rows // 2, mixed.shape[1], grad_qkv.shape[1]
    block = width // N_FLEET
    whole = lambda shape: pl.BlockSpec(shape, lambda s: (0, 0))
    return pl.pallas_call(
        attn_terms_kernel,
        grid=(N_FLEET,),
        in_specs=[pl.BlockSpec((rows, block), lambda s: (0, s)), whole((rows, deep)), whole((rows, wide))]
        + [whole((half, width))] * 2,
        out_specs=pl.BlockSpec((block, deep + wide), lambda s: (s, 0)),
        out_shape=pltpu.HBM((width, deep + wide), low),
        scratch_shapes=[pltpu.VMEM((wide, width), low)],
        compiler_params=pltpu.CompilerParams(vmem_limit_bytes=18 << 20),
        cost_estimate=FILLS,
    )(normed, grad_qkv, mixed, *hidden_low)


def summed(refs, at):
    return refs[0][at] + sum(ref[at].astype(full) for ref in refs[1:])


def own_rows(kernel, out_types, *operands):
    shape = operands[0].shape
    n = len(operands)

    def whole(*refs):
        sources, outs, held, arrived = refs[:n], refs[n:-n - 1], refs[-n - 1 : -1], refs[-1]
        copies = [pltpu.make_async_copy(sources[i], held[i], arrived.at[i]) for i in range(n)]
        for copy in copies:
            copy.start()
        for copy in copies:
            copy.wait()
        for first in range(0, shape[0], 16):
            kernel(slice(first, first + 16), (*held, *outs))

    return pl.pallas_call(
        whole,
        in_specs=[pl.BlockSpec(memory_space=pl.ANY)] * n,
        out_shape=[jax.ShapeDtypeStruct(shape, dtype) for dtype in out_types],
        scratch_shapes=[pltpu.VMEM(operand.shape, operand.dtype) for operand in operands]
        + [pltpu.SemaphoreType.DMA((n,))],
        compiler_params=pltpu.CompilerParams(vmem_limit_bytes=12 << 20),
        cost_estimate=FILLS,
    )(*operands)


def hidden_kernel(at, refs):
    *parts, x_ref, gain_ref, hidden_ref, again_ref = refs
    hidden = x_ref[at].astype(full) + summed(parts, at)
    hidden_ref[at] = hidden
    again_ref[at] = (hidden * inverse_rms(hidden) * gain_ref[...]).astype(low)


def norm_backward(grad_normed, inputs, gain):
    scale_rows = inverse_rms(inputs)
    weighted = grad_normed * gain
    return scale_rows * weighted - inputs * scale_rows**3 * jnp.mean(
        weighted * inputs, axis=-1, keepdims=True
    )


def grad_hidden_kernel(at, refs):
    *parts, hidden_ref, dy_ref, gain_ref, grad_ref, low_ref = refs
    grad = dy_ref[at].astype(full) + norm_backward(summed(parts, at), hidden_ref[at], gain_ref[...])
    grad_ref[at] = grad
    low_ref[at] = grad.astype(low)


def input_grad_kernel(at, refs):
    *parts, x_ref, grad_ref, gain_ref, out_ref = refs
    out_ref[at] = grad_ref[at] + norm_backward(summed(parts, at), x_ref[at].astype(full), gain_ref[...])


def outputs_kernel(at, refs):
    *parts, hidden_ref, out_ref = refs
    out_ref[at] = (hidden_ref[at] + summed(parts, at)).astype(low)


def feed_owner_kernel(unit_rows, group, here_ref, there_ref, w_gate_ref, w_up_ref, gain_ref, gate_ref, up_ref, grad_ref):
    rows = here_ref.shape[1]
    units = here_ref.shape[2] // 2
    pad = units // N_FLEET
    first = group[0] == 0
    for t in range(N_TEAM):
        here, there = here_ref[t], there_ref[t]
        block = jnp.concatenate([jnp.where(first, here, there), jnp.where(first, there, here)], axis=0).astype(full)
        for i, out_ref in enumerate((gate_ref, up_ref)):
            for f in range(N_FLEET):
                at = i * units + f * pad
                to = (f * N_TEAM + t) * unit_rows
                out_ref[:, to : to + unit_rows] = block[:, at : at + unit_rows]
    for row in range(0, 2 * rows, 16):
        at = slice(row, row + 16)
        total = w_gate_ref[at].astype(full) * gate_ref[at] + w_up_ref[at].astype(full) * up_ref[at]
        grad_ref[at] = jnp.sum(total, axis=1, keepdims=True) / gain_ref[at].astype(full)


def feed_owner(group, here, there, w_gate, w_up, gain):
    shard, wide = w_gate.shape
    vmem = pl.BlockSpec(memory_space=pltpu.VMEM)
    return pl.pallas_call(
        functools.partial(feed_owner_kernel, wide // (N_FLEET * N_TEAM)),
        in_specs=[pl.BlockSpec(memory_space=pltpu.SMEM)] + [vmem] * 5,
        out_specs=[vmem] * 3,
        out_shape=[jax.ShapeDtypeStruct((shard, wide), full)] * 2 + [jax.ShapeDtypeStruct((shard, 1), full)],
        compiler_params=pltpu.CompilerParams(vmem_limit_bytes=10 << 20),
        cost_estimate=FILLS,
    )(group, here, there, w_gate, w_up, gain[:, None])


def attn_owner_kernel(
    sums_ref, out0_ref, out1_ref, w_query_ref, w_key_ref, w_value_ref, gain_ref,
    query_ref, key_ref, value_ref, out_ref, grad_ref,
):
    wide = sums_ref.shape[2] // 3
    weights = (w_query_ref, w_key_ref, w_value_ref)
    total = jnp.zeros((query_ref.shape[0], wide), full)
    for t in range(N_TEAM):
        to = slice(t * wide, (t + 1) * wide)
        block = sums_ref[t].astype(full) + sums_ref[N_TEAM + t].astype(full)
        for i, grad in enumerate((query_ref, key_ref, value_ref)):
            part = block[:, i * wide : (i + 1) * wide]
            grad[:, to] = part
            total += part * weights[i][:, to].astype(full)
        out_ref[:, to] = out0_ref[t].astype(full) + out1_ref[t].astype(full)
    grad_ref[...] = jnp.sum(total, axis=1, keepdims=True) / gain_ref[...].astype(full)


def attn_owner(sums, out_sums, w_query, w_key, w_value, gain):
    grad = jax.ShapeDtypeStruct(w_query.shape, full)
    return pl.pallas_call(
        attn_owner_kernel,
        out_shape=[grad] * 4 + [jax.ShapeDtypeStruct((w_query.shape[0], 1), full)],
        compiler_params=pltpu.CompilerParams(vmem_limit_bytes=8 << 20),
        cost_estimate=FILLS,
    )(sums, *out_sums, w_query, w_key, w_value, gain[:, None])


def body(
    tokens, lengths, norm_gain, w_query, w_key, w_value, w_out, mlp_gain, w_gate, w_up, w_down, cotangent
):
    rows, width = tokens.shape
    shard = w_query.shape[0]
    team_wide = width // N_TEAM
    unit_rows = w_down.shape[0]
    unit_pad = -(-unit_rows // 32) * 32
    units = N_FLEET * unit_pad
    x, yl, z, c = [lax.axis_index(axis) for axis in ("x", "yl", "z", "c")]
    fleet = lax.axis_index(FLEET)

    order = jnp.arange(N_TEAM, dtype=jnp.int32)
    spot = (jnp.bitwise_xor(order % N_C, c) * N_Z + (order // N_C - z) % N_Z).astype(jnp.int32)
    before = jnp.concatenate([jnp.zeros((1,), jnp.int32), 2 * spot[:-1] + 1])
    place = jnp.concatenate([spot, before])
    last_spot = (1 - c) * N_Z + N_Z - 1 - z
    last_at = last_spot * BLOCK + BLOCK - WIN
    kept = jnp.arange(N_TEAM, dtype=jnp.int32)
    kept_block = N_C * ((kept % N_Z + z) % N_Z) + jnp.bitwise_xor(kept // N_Z, c)
    first_pos = (fleet * N_TEAM + kept_block) * BLOCK
    query_pos = first_pos[:, None] + jnp.arange(BLOCK, dtype=jnp.int32)
    key_pos = first_pos[:, None] - WIN + jnp.arange(BLOCK + WIN, dtype=jnp.int32)
    query_segs = segment_numbers(query_pos, lengths[0])
    key_segs = jnp.where(key_pos >= 0, segment_numbers(key_pos, lengths[0]), -1)
    distance = query_pos[:, :, None] - key_pos[:, None, :]
    mask = (distance >= 0) & (distance < WIN) & (query_segs[:, :, None] == key_segs[:, None, :])
    mask = mask.astype(full)

    gains = jnp.concatenate([norm_gain[:, None], mlp_gain[:, None], jnp.zeros((shard, 126), low)], axis=1)
    out_there = swapped(w_out)
    x_mine = [tokens, from_ahead(tokens, "z", 1), None, from_ahead(tokens, "z", 3)]
    cut = attn_cut(w_query, w_key, w_value, gains)
    cut = lax.all_to_all(cut, TEAM, 0, 0, tiled=True).reshape(N_TEAM * shard, -1)
    out_cut = out_there.reshape(shard, N_TEAM, team_wide).transpose(1, 0, 2)
    out_cut = out_cut.reshape(N_TEAM * shard, team_wide)
    cut, out_cut, x_mine, w_gate_later, dy = lax.optimization_barrier((cut, out_cut, x_mine, w_gate, cotangent))
    at_out = cut.shape[1]
    attn_piece = jnp.concatenate([cut, out_cut], axis=1)
    along_y = lambda value, by: from_ahead(value, ("g", "yl"), by)
    other = lambda block: from_ahead(block, "c", 1)
    attn = lax.all_to_all(jnp.broadcast_to(attn_piece, (N_X, *attn_piece.shape)), "x", 0, 0, tiled=True)
    attn = attn.reshape(N_X * N_TEAM * shard, -1)
    x_mine[2] = from_ahead(x_mine[0], "z", 2)
    x_other = [other(x_mine[0]), other(x_mine[1]), None, other(x_mine[3])]
    gate_up = feed_cut(w_gate_later, w_up, unit_rows, units)
    down_piece = pack(w_down, unit_pad, 2 * units)
    attn, x_mine, x_other, dy, gate_up, down_piece, place, mask = lax.optimization_barrier(
        (attn, x_mine, x_other, dy, gate_up, down_piece, place, mask)
    )
    x_other[2] = other(x_mine[2])
    x_blocks = x_mine + x_other
    halo = along_line(lax.select_n(last_spot, *[block[BLOCK - WIN :] for block in x_blocks]), 1)
    gate_up_piece = lax.all_to_all(gate_up, TEAM, 0, 0, tiled=True).reshape(N_TEAM * shard, -1)
    attn_there = along_y(attn[: width // 4], 1), along_y(attn[width // 4 :], -1)
    dy_mine = [dy, from_ahead(dy, "z", 1), None, from_ahead(dy, "z", 3)]
    attn, attn_there, x_blocks, halo, dy_mine, gate_up_piece = lax.optimization_barrier(
        (attn, attn_there, x_blocks, halo, dy_mine, gate_up_piece)
    )
    feed_piece = jnp.concatenate([gate_up_piece, down_piece], axis=0)
    w_feed = lax.all_gather(feed_piece, FLEET, axis=0, tiled=False)
    dy_mine[2] = from_ahead(dy_mine[0], "z", 2)

    half = N_Z * BLOCK
    whole = jnp.zeros((width, attn.shape[1]), low)
    whole = lax.dynamic_update_slice(whole, attn, (yl * (width // 2), 0))
    whole = lax.dynamic_update_slice(whole, attn_there[0], ((1 - yl) * (width // 2), 0))
    attn = lax.dynamic_update_slice(whole, attn_there[1], ((1 - yl) * (width // 2) + width // 4, 0))
    w_qkv = attn[:, : 3 * team_wide]
    w_out_team = attn[:, at_out:].reshape(N_FLEET, N_TEAM, shard, team_wide)
    w_out_team = w_out_team.transpose(0, 2, 1, 3).reshape(N_FLEET * shard, width)
    normed, gain_rows = normalised(x_blocks, attn[:, 3 * team_wide : at_out])
    gain_one, gain_two = gain_rows[:1], gain_rows[1:2]
    qkv = matmul(normed, w_qkv).astype(low)
    qkv, dy_mine = lax.optimization_barrier((qkv, dy_mine))
    halo = halo.astype(full)
    halo = matmul((halo * inverse_rms(halo) * gain_one).astype(low), w_qkv[:, team_wide:]).astype(low)
    mixed = attend(place, qkv, halo, mask)
    halves = lambda rows: (rows[:half], rows[half : 2 * half])
    hidden_blocks = core_sum(halves(mixed), lambda rows: matmul(rows, w_out_team))
    hidden_blocks, dy_mine = lax.optimization_barrier((hidden_blocks, dy_mine))
    dy_other = [other(block) for block in dy_mine]
    hidden_parts, dy_mine, dy_other = lax.optimization_barrier((z_send(hidden_blocks), dy_mine, dy_other))

    hidden, again = own_rows(hidden_kernel, (full, low), *hidden_parts, tokens, gain_two)
    again = z_gather(again)
    again_other = [other(block) for block in again[:2]] + [None, other(again[3])]
    again, again_other[:2], again_other[3] = lax.optimization_barrier((again, again_other[:2], again_other[3]))
    again_other[2] = other(again[2])
    w_gate_up, w_down_team = unpack(w_feed, N_TEAM * shard, unit_pad, width)
    act_mine, gate_mine, up_mine, x_mine, dy_mine = feed(again, dy_mine, w_gate_up, w_down_team)
    act_other, gate_other, up_other, x_other, dy_other = feed(again_other, dy_other, w_gate_up, w_down_team)
    there = feed_back(gate_other, up_other, w_gate_up, low)
    again_blocks = core_blocks(feed_back(gate_mine, up_mine, w_gate_up, full), there)
    activated, grad_gate, grad_up = (act_mine, act_other), (gate_mine, gate_other), (up_mine, up_other)
    again_blocks, activated, grad_gate, grad_up = lax.optimization_barrier(
        (again_blocks, activated, grad_gate, grad_up)
    )
    mlp_term = feed_terms((x_mine, x_other), (dy_mine, dy_other), activated, grad_gate, grad_up)
    again_parts = z_send(again_blocks)
    mlp_term, again_parts[1], again_parts[3] = lax.optimization_barrier((mlp_term, again_parts[1], again_parts[3]))
    mlp_sum = lax.psum_scatter(
        mlp_term.reshape(-1, 2 * units), ("g", *FLEET), scatter_dimension=0, tiled=True
    )

    grad_hidden, hidden_low = own_rows(grad_hidden_kernel, (full, low), *again_parts, hidden, cotangent, gain_two)
    output_parts = down_parts(activated, w_down_team)
    hidden_low, output_parts = lax.optimization_barrier((z_gather(hidden_low), output_parts))
    hidden_low = [join(hidden_low)]
    hidden_low.append(other(hidden_low[0]))
    output_blocks = core_blocks(*output_parts)

    grad_mixed = [matmul_right_t(rows, w_out_team).astype(low) for rows in hidden_low]
    grad_mixed = jnp.concatenate(grad_mixed, axis=0)
    back = halo_back(place, qkv, halo, mask, grad_mixed)
    grad_qkv, tail = attend_back(place, qkv, halo, mask, grad_mixed)
    tail = tail + along_line(back, -1).astype(full)
    grad_qkv = lax.dynamic_update_slice(grad_qkv, tail.astype(low), (last_at, team_wide))
    attn_term = attn_terms(normed, grad_qkv, mixed, hidden_low)
    attn_term, grad_qkv, output_parts = lax.optimization_barrier((attn_term, grad_qkv, z_send(output_blocks)))
    attn_sum = lax.psum_scatter(attn_term, FLEET, scatter_dimension=0, tiled=True)
    (outputs,) = own_rows(outputs_kernel, (low,), *output_parts, hidden)
    normed_blocks = core_sum(halves(grad_qkv), lambda rows: matmul_right_t(rows, w_qkv))

    down_sum = unpack_down(mlp_sum[N_TEAM * shard // 2 :], unit_pad // 2, width)
    gate_up_sum = mlp_sum[: N_TEAM * shard // 2].reshape(N_TEAM, shard // 2, 2 * units)
    gate_up_sum = lax.all_to_all(gate_up_sum, TEAM, 0, 0, tiled=True)
    normed_blocks, gate_up_sum, down_sum = lax.optimization_barrier((normed_blocks, gate_up_sum, down_sum))
    gate_up_there, down_there = from_ahead(gate_up_sum, "g", 1), from_ahead(down_sum, "g", 1)
    normed_parts, attn_sum, outputs, gate_up_there, down_there = lax.optimization_barrier(
        (z_send(normed_blocks), attn_sum, outputs, gate_up_there, down_there)
    )
    (input_grad,) = own_rows(input_grad_kernel, (full,), *normed_parts, tokens, grad_hidden, gain_one)
    qkv_sum = attn_sum[:, : 3 * team_wide].reshape(N_TEAM, shard, 3 * team_wide)
    qkv_sum = lax.all_to_all(jnp.concatenate([qkv_sum, qkv_sum], axis=0), ("g", *TEAM), 0, 0, tiled=True)
    out_sum = attn_sum[:, 3 * team_wide :].reshape(N_TEAM, shard, team_wide)
    group = lax.axis_index("g")
    gate_grad, up_grad, mlp_gain_grad = feed_owner(
        group[None].astype(jnp.int32), gate_up_sum, gate_up_there, w_gate, w_up, mlp_gain
    )
    qkv_sum, out_sums, input_grad, gate_grad = lax.optimization_barrier(
        (qkv_sum, (swapped(out_sum), swapped(out_sum, 1)), input_grad, gate_grad)
    )
    query_grad, key_grad, value_grad, out_grad, gain_grad = attn_owner(
        qkv_sum, out_sums, w_query, w_key, w_value, norm_gain
    )
    first, second = jnp.where(group == 0, down_sum, down_there), jnp.where(group == 0, down_there, down_sum)
    down_grad = jnp.concatenate([first, second], axis=0)[:unit_rows].astype(full)
    return (
        outputs,
        input_grad,
        gain_grad[:, 0],
        query_grad,
        key_grad,
        value_grad,
        out_grad,
        mlp_gain_grad[:, 0],
        gate_grad,
        up_grad,
        down_grad,
    )


def solution(mesh):
    fine = Mesh(mesh.devices.reshape(2, 2, 4, 4, 2), ALL)
    return jax.shard_map(
        body,
        mesh=fine,
        in_specs=(
            P(ALL, None),
            P("g", None),
            P(SEQ),
            P(SEQ, None),
            P(SEQ, None),
            P(SEQ, None),
            P(SEQ, None),
            P(SEQ),
            P(SEQ, None),
            P(SEQ, None),
            P(SEQ, None),
            P(ALL, None),
        ),
        out_specs=(
            P(ALL, None),
            P(ALL, None),
            P(SEQ),
            P(SEQ, None),
            P(SEQ, None),
            P(SEQ, None),
            P(SEQ, None),
            P(SEQ),
            P(SEQ, None),
            P(SEQ, None),
            P(SEQ, None),
        ),
        check_vma=False,
    )
```

time: 511 us -> 464 us (0.908)
  Pallas kernels: 43.2 us -> 96.1 us
  matrix products: 63.1 us -> 15.7 us
  waiting for transfers between devices: 219 us -> 178 us
  other arithmetic: 30.4 us -> 10.7 us
  local copies, waits for them, and re-layouts: 47.9 us -> 54.9 us
    pallas_call x2 -> x23, Pallas kernels: 5.03 us -> 63 us  [the longest x2 15.4 us: feed(): pl.pallas_call(feed_kernel, grid=(tiles,), in_specs=[pl.BlockSpec(memory_...]
    ppermute x42 -> x45, waiting for transfers between devices: 171 us -> 120 us  [from_ahead(): return lax.ppermute(value, axis, [((i + by) % n, i) for i in range(n)])]
    dot_general x7 -> x4, matrix products: 28.4 us -> 6.53 us  [matmul(): return jnp.dot(left, right, preferred_element_type=full)]
    all_to_all x3 -> x4, waiting for transfers between devices: 6.05 us -> 26.9 us  [the longest x1 12.7 us: body(): lax.all_to_all(jnp.broadcast_to(attn_piece, (N_X, *attn_piece.shape)), 'x...]
    dot_general x7 -> x4, matrix products: 29.8 us -> 9.18 us  [matmul_right_t(): lax.dot_general(left, right, (((1,), (1,)), ((), ())), preferred_element_...]
    unnamed x110 -> x164, local copies, waits for them, and re-layouts: 17.2 us -> 37 us
    reduce_scatter x1, waiting for transfers between devices: 0.01 us -> 13.8 us  [body(): lax.psum_scatter(attn_term, FLEET, scatter_dimension=0, tiled=True)]
    convert_element_type x8 -> x1, other arithmetic: 11.3 us -> 0.92 us  [body(): jnp.concatenate([first, second], axis=0)[:unit_rows].astype(full)]
  transfers between devices with their start and end apart: 55 -> 58, of which waited for: 31 -> 24; matrix products, arithmetic and copies ran while one was open for 22% -> 8% of each run, Pallas kernels for 8% -> 18%
where the time goes in v3:
time: 464 us; the launch traced here: 456 us
  waiting for transfers between devices  178 us (38%)
  Pallas kernels  96.1 us (21%)
  starting transfers between devices  85.2 us (18%)
  local copies, waits for them, and re-layouts  54.9 us (12%)
  matrix products  15.7 us (3%)
  between operations  15.3 us (3%)
  other arithmetic  10.7 us (2%)
    ppermute x45, waiting for transfers between devices, from_ahead(): return lax.ppermute(value, axis, [((i + by) % n, i) for i in range(n)])  120 us
    ppermute x45, starting transfers between devices, from_ahead(): return lax.ppermute(value, axis, [((i + by) % n, i) for i in range(n)])  43.7 us
    unnamed x164, local copies, waits for them, and re-layouts  37 us
    pallas_call x2, Pallas kernels, feed(): pl.pallas_call(feed_kernel, grid=(tiles,), in_specs=[pl.BlockSpec(memory_...  15.4 us
    ppermute x3, starting transfers between devices, swapped(): lax.ppermute(value, ALL, [(g * n + a, (g ^ across) * n + b) for g in rang...  14.1 us
    reduce_scatter x1, waiting for transfers between devices, body(): lax.psum_scatter(attn_term, FLEET, scatter_dimension=0, tiled=True)  13.8 us
    pallas_call x1, Pallas kernels, feed_terms(): pl.pallas_call(terms_kernel, grid=(N_FLEET,), in_specs=[cut] * 2 + [whole...  13.5 us
    all_to_all x1, waiting for transfers between devices, body(): lax.all_to_all(jnp.broadcast_to(attn_piece, (N_X, *attn_piece.shape)), 'x...  12.7 us
  transfers between devices with their start and end apart: 58, of which 24 were waited for; matrix products, arithmetic and copies ran while one was open for 8% of the time, Pallas kernels for 18%

profile of v3, /device:TPU:8, one launch (start us, length us, event | category | flops | bytes accessed | tf_op | source)
XLA Modules:
  0.0 455.6 jit_solution(10360841227216301856)
XLA Ops:
  20.0 5.2 %collective-permute-start = (bf16[32,2048]{1,0:T(8,128)(2,1)}, bf16[32,2048]{1,0:T(8,128)(2,1)S(1)}, u32[]{:S(2)}, u32[]{:S(2)}) collective-permute-start(bf16[32,2048]{1,0:T(8,128)(2,1)} %param.18), channel_id=1, source_target_pairs={{0,0},{1,8},{2,16},{3,24},{4,32},{5,40},{6,48},{7,56},{8,1},{9,9},... | collective-permute-start | bytes 393224 | tf_op jit(solution)/shard_map/ppermute | solution.py:41
  25.3 8.6 %collective-permute-done = bf16[32,2048]{1,0:T(8,128)(2,1)S(1)} collective-permute-done((bf16[32,2048]{1,0:T(8,128)(2,1)}, bf16[32,2048]{1,0:T(8,128)(2,1)S(1)}, u32[]{:S(2)}, u32[]{:S(2)}) %collective-permute-start) | collective-permute-done | bytes 131104 | tf_op jit(solution)/shard_map/ppermute | solution.py:41
  36.9 4.6 %all-to-all-start.1 = ((bf16[4,256,1152]{2,1,0:T(8,128)(2,1)}), bf16[4,256,1152]{2,1,0:T(8,128)(2,1)}, u32[]{:S(2)}, u32[]{:S(2)}) async-start(bf16[4,256,1152]{2,1,0:T(8,128)(2,1)} %broadcast_in_dim.19), calls=%async_computation.1 | async-start | bytes 4718592 | tf_op jit(solution)/shard_map/all_to_all | solution.py:723
  47.5 10.6 %collective-permute-done.3.refs_2_ = bf16[128,2048]{1,0:T(8,128)(2,1)} collective-permute-done((bf16[128,2048]{1,0:T(8,128)(2,1)S(1)}, bf16[128,2048]{1,0:T(8,128)(2,1)}, u32[]{:S(2)}, u32[]{:S(2)}) %collective-permute-start.3) | collective-permute-done | bytes 524320 | tf_op jit(solution)/shard_map/ppermute | solution.py:29
  58.1 12.7 %all-to-all-done.1 = bf16[4,256,1152]{2,1,0:T(8,128)(2,1)} async-done(((bf16[4,256,1152]{2,1,0:T(8,128)(2,1)}), bf16[4,256,1152]{2,1,0:T(8,128)(2,1)}, u32[]{:S(2)}, u32[]{:S(2)}) %all-to-all-start.1) | async-done | bytes 2359328 | tf_op jit(solution)/shard_map/all_to_all | solution.py:723
  79.3 4.2 all-to-all-start.2
  88.2 5.3 %collective-permute-done.12.refs_7_ = bf16[128,2048]{1,0:T(8,128)(2,1)} collective-permute-done((bf16[128,2048]{1,0:T(8,128)(2,1)}, bf16[128,2048]{1,0:T(8,128)(2,1)}, u32[]{:S(2)}, u32[]{:S(2)}) %collective-permute-start.12) | collective-permute-done | bytes 524320 | tf_op jit(solution)/shard_map/ppermute | solution.py:29
  93.5 6.3 %all-to-all-done.2 = bf16[8,32,1536]{2,1,0:T(8,128)(2,1)} async-done(((bf16[8,32,1536]{2,1,0:T(8,128)(2,1)}), bf16[8,32,1536]{2,1,0:T(8,128)(2,1)}, u32[]{:S(2)}, u32[]{:S(2)}) %all-to-all-start.2) | async-done | bytes 786464 | tf_op jit(solution)/shard_map/all_to_all | solution.py:735
  99.8 8.6 %collective-permute-done.8 = bf16[512,1152]{1,0:T(8,128)(2,1)} collective-permute-done((bf16[512,1152]{1,0:T(8,128)(2,1)}, bf16[512,1152]{1,0:T(8,128)(2,1)}, u32[]{:S(2)}, u32[]{:S(2)}) %collective-permute-start.8) | collective-permute-done | bytes 1179680 | tf_op jit(solution)/shard_map/ppermute | solution.py:29
  116.7 4.2 shard_map.206
  128.3 7.8 %shard_map.207.mixed_ref = bf16[1024,256]{1,0:T(8,128)(2,1)S(1)} custom-call(s32[16]{0:T(128)S(1)} %pad_add_fusion.place, bf16[1024,768]{1,0:T(8,128)(2,1)S(1)} %fusion.7.q_ref.k_ref.v_ref.kp_ref.vp_ref, bf16[1024,768]{1,0:T(8,128)(2,1)S(1)} %fusion.7.q_ref.k_ref.v_ref.kp_ref.vp_ref, bf16[1024,768]{1,0:T(8,128)(2,1)S(1)} %fusion.7.q_ref.k_ref.v_ref.kp_ref.vp_ref, ...), custom_call_target="tpu_custom_call" | custom-call | flops 1 | bytes 1 | tf_op jit(solution)/shard_map/pallas_call | solution.py:488
  148.4 9.2 %collective-permute-done.15.refs_1_ = bf16[128,2048]{1,0:T(8,128)(2,1)S(1)} collective-permute-done((bf16[128,2048]{1,0:T(8,128)(2,1)S(1)}, bf16[128,2048]{1,0:T(8,128)(2,1)S(1)}, u32[]{:S(2)}, u32[]{:S(2)}) %collective-permute-start.15) | collective-permute-done | bytes 524320 | tf_op jit(solution)/shard_map/ppermute | solution.py:29
  157.6 12.4 %collective-permute-done.16.refs_2_ = bf16[128,2048]{1,0:T(8,128)(2,1)S(1)} collective-permute-done((bf16[128,2048]{1,0:T(8,128)(2,1)S(1)}, bf16[128,2048]{1,0:T(8,128)(2,1)S(1)}, u32[]{:S(2)}, u32[]{:S(2)}) %collective-permute-start.16) | collective-permute-done | bytes 524320 | tf_op jit(solution)/shard_map/ppermute | solution.py:29
  178.1 22.4 %collective-permute-done.24.refs_3_ = bf16[128,2048]{1,0:T(8,128)(2,1)S(1)} collective-permute-done((bf16[128,2048]{1,0:T(8,128)(2,1)S(1)}, bf16[128,2048]{1,0:T(8,128)(2,1)S(1)}, u32[]{:S(2)}, u32[]{:S(2)}) %collective-permute-start.24) | collective-permute-done | bytes 524320 | tf_op jit(solution)/shard_map/ppermute | solution.py:29
  214.6 7.5 %shard_map.213 = (bf16[512,768]{1,0:T(8,128)(2,1)S(1)}, bf16[512,768]{1,0:T(8,128)(2,1)S(1)}, bf16[512,768]{1,0:T(8,128)(2,1)S(1)}, bf16[512,2048]{1,0:T(8,128)(2,1)S(1)}, bf16[512,2048]{1,0:T(8,128)(2,1)S(1)}) custom-call(bf16[128,2048]{1,0:T(8,128)(2,1)S(1)} %copy-done.60, bf16[128,2048]{1,0:T(8,128)(2,1)S(1)} %copy-done.64, ...), custom_call_target="tpu_custom_call" | custom-call | flops 1 | bytes 1 | tf_op jit(solution)/shard_map/pallas_call | solution.py:200
  222.1 4.2 shard_map.214
  226.4 8.0 %shard_map.211 = (bf16[512,768]{1,0:T(8,128)(2,1)S(1)}, bf16[512,768]{1,0:T(8,128)(2,1)S(1)}, bf16[512,768]{1,0:T(8,128)(2,1)S(1)}, bf16[512,2048]{1,0:T(8,128)(2,1)S(1)}, bf16[512,2048]{1,0:T(8,128)(2,1)S(1)}) custom-call(bf16[128,2048]{1,0:T(8,128)(2,1)S(1)} %copy-done.52, bf16[128,2048]{1,0:T(8,128)(2,1)S(1)} %copy-done.58, ...), custom_call_target="tpu_custom_call" | custom-call | flops 1 | bytes 1 | tf_op jit(solution)/shard_map/pallas_call | solution.py:200
  234.4 4.3 shard_map.212.here_ref
  244.3 13.5 %shard_map.216 = bf16[2,8,192,1536]{3,2,1,0:T(8,128)(2,1)} custom-call(bf16[512,2048]{1,0:T(8,128)(2,1)S(1)} %get-tuple-element.257.x0_ref, bf16[512,2048]{1,0:T(8,128)(2,1)S(1)} %get-tuple-element.258.x1_ref, bf16[512,2048]{1,0:T(8,128)(2,1)S(1)} %get-tuple-element.259.dy0_ref, bf16[512,2048]{1,0:T(8,128)(2,1)S(1)} %get-tuple-element.260.dy1_ref, ...), custom_call_target="tpu_custom_call" | custom-call | flops 10000000000 | bytes 20000000 | tf_op jit(solution)/shard_map/pallas_call | solution.py:339
  261.5 13.5 %collective-permute-done.32.refs_2_ = bf16[128,2048]{1,0:T(8,128)(2,1)S(1)} collective-permute-done((bf16[128,2048]{1,0:T(8,128)(2,1)}, bf16[128,2048]{1,0:T(8,128)(2,1)S(1)}, u32[]{:S(2)}, u32[]{:S(2)}) %collective-permute-start.32) | collective-permute-done | bytes 524320 | tf_op jit(solution)/shard_map/ppermute | solution.py:29
  288.4 4.6 %shard_map.218 = (f32[512,2048]{1,0:T(8,128)S(1)}, bf16[512,2048]{1,0:T(8,128)(2,1)S(1)}) custom-call(bf16[512,768]{1,0:T(8,128)(2,1)S(1)} %copy-done.39, bf16[512,768]{1,0:T(8,128)(2,1)S(1)} %copy-done.37, bf16[768,2048]{1,0:T(8,128)(2,1)S(1)} %copy-done.1), custom_call_target="tpu_custom_call" | custom-call | flops 1 | bytes 1 | tf_op jit(solution)/shard_map/pallas_call | solution.py:361
  293.0 5.8 %collective-permute-done.35.refs_3_ = bf16[128,2048]{1,0:T(8,128)(2,1)S(1)} collective-permute-done((bf16[128,2048]{1,0:T(8,128)(2,1)S(1)}, bf16[128,2048]{1,0:T(8,128)(2,1)S(1)}, u32[]{:S(2)}, u32[]{:S(2)}) %collective-permute-start.35) | collective-permute-done | bytes 524320 | tf_op jit(solution)/shard_map/ppermute | solution.py:29
  298.8 9.3 %collective-permute-done.34.refs_2_ = bf16[128,2048]{1,0:T(8,128)(2,1)S(1)} collective-permute-done((bf16[128,2048]{1,0:T(8,128)(2,1)S(1)}, bf16[128,2048]{1,0:T(8,128)(2,1)S(1)}, u32[]{:S(2)}, u32[]{:S(2)}) %collective-permute-start.34) | collective-permute-done | bytes 524320 | tf_op jit(solution)/shard_map/ppermute | solution.py:29
  328.9 11.9 %shard_map.220 = (bf16[1024,768]{1,0:T(8,128)(2,1)S(1)}, f32[64,512]{1,0:T(8,128)S(1)}) custom-call(s32[16]{0:T(128)S(1)} %pad_add_fusion.place, bf16[1024,768]{1,0:T(8,128)(2,1)S(1)} %fusion.7.q_ref.k_ref.v_ref.kp_ref.vp_ref, bf16[1024,768]{1,0:T(8,128)(2,1)S(1)} %fusion.7.q_ref.k_ref.v_ref.kp_ref.vp_ref, ...), custom_call_target="tpu_custom_call" | custom-call | flops 1 | bytes 1 | tf_op jit(solution)/shard_map/pallas_call | solution.py:507
  341.7 8.1 %shard_map.222 = bf16[2048,1024]{1,0:T(8,128)(2,1)} custom-call(bf16[1024,2048]{1,0:T(8,128)(2,1)S(1)} %copy-done.11, bf16[1024,768]{1,0:T(8,128)(2,1)S(1)} %fusion.30.grad_ref, bf16[1024,256]{1,0:T(8,128)(2,1)S(1)} %copy-done.7, bf16[512,2048]{1,0:T(8,128)(2,1)S(1)} %copy-done.4, bf16[512,2048]{1,0:T(8,128)(2,1)S(1)} %copy-done.16), custom_call_target="tpu_custom_call" | custom-call | flops 1 | bytes 1 | tf_op jit(solution)/shard_map/pallas_call | solution.py:548
  369.0 7.9 %all-to-all-done.3.here_ref = bf16[8,16,1536]{2,1,0:T(8,128)(2,1)S(1)} async-done(((bf16[8,16,1536]{2,1,0:T(8,128)(2,1)}), bf16[8,16,1536]{2,1,0:T(8,128)(2,1)S(1)}, u32[]{:S(2)}, u32[]{:S(2)}) %all-to-all-start.3) | async-done | bytes 393248 | tf_op jit(solution)/shard_map/all_to_all | solution.py:808
  387.5 13.8 %reduce-scatter.5.cloned.1.call-done = bf16[256,1024]{1,0:T(8,128)(2,1)} async-done(((bf16[2048,1024]{1,0:T(8,128)(2,1)}), bf16[256,1024]{1,0:T(8,128)(2,1)}) %reduce-scatter.5.cloned.1.call-update) | async-done | bytes 524304 | tf_op jit(solution)/shard_map/reduce_scatter | solution.py:802
  401.2 13.0 %collective-permute-done.47 = bf16[48,2048]{1,0:T(8,128)(2,1)S(1)} collective-permute-done((bf16[48,2048]{1,0:T(8,128)(2,1)S(1)}, bf16[48,2048]{1,0:T(8,128)(2,1)S(1)}, u32[]{:S(2)}, u32[]{:S(2)}) %collective-permute-start.47) | collective-permute-done | bytes 196640 | tf_op jit(solution)/shard_map/ppermute | solution.py:29
  416.3 5.4 %all-to-all-start.4 = ((bf16[16,32,768]{2,1,0:T(8,128)(2,1)}), bf16[16,32,768]{2,1,0:T(8,128)(2,1)S(1)}, u32[]{:S(2)}, u32[]{:S(2)}) async-start(bf16[16,32,768]{2,1,0:T(8,128)(2,1)} %pad_maximum_fusion.1), calls=%async_computation.6 | async-start | bytes 1572864 | tf_op jit(solution)/shard_map/all_to_all | solution.py:816
  423.2 4.3 collective-permute-start.49
  427.6 4.5 collective-permute-start.48
  441.9 4.1 collective-permute-done.49.out1_ref
  (329 shorter events, 174.8 us)
Async XLA Ops:
  7.2 28.0 %collective-permute-start.2 = (bf16[128,2048]{1,0:T(8,128)(2,1)}, bf16[128,2048]{1,0:T(8,128)(2,1)S(1)}, u32[]{:S(2)}, u32[]{:S(2)}) collective-permute-start(bf16[128,2048]{1,0:T(8,128)(2,1)} %refs_4_.4), channel_id=1, source_target_pairs={{6,0},{0,2},{2,4},{4,6},{7,1},{1,3},{3,5},{5,7},{14,8},{8,10},{10,... | collective-permute-start | bytes 1572872 | tf_op jit(solution)/shard_map/ppermute | solution.py:29
  9.2 26.1 %collective-permute-start.1 = (bf16[128,2048]{1,0:T(8,128)(2,1)}, bf16[128,2048]{1,0:T(8,128)(2,1)}, u32[]{:S(2)}, u32[]{:S(2)}) collective-permute-start(bf16[128,2048]{1,0:T(8,128)(2,1)} %refs_4_.4), channel_id=1, source_target_pairs={{2,0},{4,2},{6,4},{0,6},{3,1},{5,3},{7,5},{1,7},{10,8},{12,10},{14... | collective-permute-start | bytes 1572872 | tf_op jit(solution)/shard_map/ppermute | solution.py:29
  16.6 18.7 %all-to-all-start = ((bf16[8,32,896]{2,1,0:T(8,128)(2,1)}), bf16[8,32,896]{2,1,0:T(8,128)(2,1)S(1)}, u32[]{:S(2)}, u32[]{:S(2)}) async-start(bf16[8,32,896]{2,1,0:T(8,128)(2,1)} %shard_map.203), calls=%async_computation | async-start | bytes 917504 | tf_op jit(solution)/shard_map/all_to_all | solution.py:715
  36.9 33.9 %all-to-all-start.1 = ((bf16[4,256,1152]{2,1,0:T(8,128)(2,1)}), bf16[4,256,1152]{2,1,0:T(8,128)(2,1)}, u32[]{:S(2)}, u32[]{:S(2)}) async-start(bf16[4,256,1152]{2,1,0:T(8,128)(2,1)} %broadcast_in_dim.19), calls=%async_computation.1 | async-start | bytes 4718592 | tf_op jit(solution)/shard_map/all_to_all | solution.py:723
  74.1 34.3 %collective-permute-start.8 = (bf16[512,1152]{1,0:T(8,128)(2,1)}, bf16[512,1152]{1,0:T(8,128)(2,1)}, u32[]{:S(2)}, u32[]{:S(2)}) collective-permute-start(bf16[512,1152]{1,0:T(8,128)(2,1)} %get-tuple-element.329), channel_id=1, source_target_pairs={{96,0},{0,32},{32,64},{64,96},{97,1},{1,33},{33,65},{65,97},{98,2}... | collective-permute-start | bytes 3538952 | tf_op jit(solution)/shard_map/ppermute | solution.py:29
  74.1 34.3 %collective-permute-start.7 = (bf16[512,1152]{1,0:T(8,128)(2,1)}, bf16[512,1152]{1,0:T(8,128)(2,1)}, u32[]{:S(2)}, u32[]{:S(2)}) collective-permute-start(bf16[512,1152]{1,0:T(8,128)(2,1)} %get-tuple-element.330), channel_id=1, source_target_pairs={{32,0},{64,32},{96,64},{0,96},{33,1},{65,33},{97,65},{1,97},{34,2}... | collective-permute-start | bytes 3538952 | tf_op jit(solution)/shard_map/ppermute | solution.py:29
  79.3 20.4 %all-to-all-start.2 = ((bf16[8,32,1536]{2,1,0:T(8,128)(2,1)}), bf16[8,32,1536]{2,1,0:T(8,128)(2,1)}, u32[]{:S(2)}, u32[]{:S(2)}) async-start(bf16[8,32,1536]{2,1,0:T(8,128)(2,1)} %shard_map.204), calls=%async_computation.2 | async-start | bytes 1572864 | tf_op jit(solution)/shard_map/all_to_all | solution.py:735
  83.5 124.5 %all-gather.3.cloned.1.call-start = ((), (), s32[]{:S(2)}) async-start(), calls=%async_computation.9 | async-start | bytes 10616832 | tf_op jit(solution)/shard_map/all_gather | solution.py:742
  110.6 252.1 %reduce-scatter.3.cloned.1.call-start = ((), (), s32[]{:S(2)}) async-start(), calls=%async_computation.7 | async-start | bytes 10027008 | tf_op jit(solution)/shard_map/reduce_scatter | solution.py:783
  110.6 17.6 %collective-permute-start.13 = (bf16[128,2048]{1,0:T(8,128)(2,1)}, bf16[128,2048]{1,0:T(8,128)(2,1)S(1)}, u32[]{:S(2)}, u32[]{:S(2)}) collective-permute-start(bf16[128,2048]{1,0:T(8,128)(2,1)} %refs_5_.1), channel_id=1, source_target_pairs={{4,0},{6,2},{0,4},{2,6},{5,1},{7,3},{1,5},{3,7},{12,8},{14,10},{8,... | collective-permute-start | bytes 1572872 | tf_op jit(solution)/shard_map/ppermute | solution.py:29
  142.7 27.2 %collective-permute-start.16 = (bf16[128,2048]{1,0:T(8,128)(2,1)S(1)}, bf16[128,2048]{1,0:T(8,128)(2,1)S(1)}, u32[]{:S(2)}, u32[]{:S(2)}) collective-permute-start(bf16[128,2048]{1,0:T(8,128)(2,1)S(1)} %get-tuple-element.216), channel_id=1, source_target_pairs={{4,0},{6,2},{0,4},{2,6},{5,1},{7,3},{1,5},{3,7},{12,8},{14,10},{8,... | collective-permute-start | bytes 1572872 | tf_op jit(solution)/shard_map/ppermute | solution.py:29
  146.8 23.3 %collective-permute-start.17 = (bf16[128,2048]{1,0:T(8,128)(2,1)S(1)}, bf16[128,2048]{1,0:T(8,128)(2,1)S(1)}, u32[]{:S(2)}, u32[]{:S(2)}) collective-permute-start(bf16[128,2048]{1,0:T(8,128)(2,1)S(1)} %get-tuple-element.217), channel_id=1, source_target_pairs={{2,0},{4,2},{6,4},{0,6},{3,1},{5,3},{7,5},{1,7},{10,8},{12,10},{14... | collective-permute-start | bytes 1572872 | tf_op jit(solution)/shard_map/ppermute | solution.py:29
  147.8 22.3 %collective-permute-start.18 = (bf16[128,2048]{1,0:T(8,128)(2,1)}, bf16[128,2048]{1,0:T(8,128)(2,1)S(1)}, u32[]{:S(2)}, u32[]{:S(2)}) collective-permute-start(bf16[128,2048]{1,0:T(8,128)(2,1)} %refs_5_.1), channel_id=1, source_target_pairs={{1,0},{0,1},{3,2},{2,3},{5,4},{4,5},{7,6},{6,7},{9,8},{8,9},{11,10... | collective-permute-start | bytes 1572872 | tf_op jit(solution)/shard_map/ppermute | solution.py:29
  147.8 22.3 %collective-permute-start.19 = (bf16[128,2048]{1,0:T(8,128)(2,1)}, bf16[128,2048]{1,0:T(8,128)(2,1)S(1)}, u32[]{:S(2)}, u32[]{:S(2)}) collective-permute-start(bf16[128,2048]{1,0:T(8,128)(2,1)} %collective-permute-done.11.refs_5_), channel_id=1, source_target_pairs={{1,0},{0,1},{3,2},{2,3},{5,4},{4,5},{7,6},{6,7},{9,8},{8,9},{11,10... | collective-permute-start | bytes 1572872 | tf_op jit(solution)/shard_map/ppermute | solution.py:29
  174.0 26.4 %collective-permute-start.24 = (bf16[128,2048]{1,0:T(8,128)(2,1)S(1)}, bf16[128,2048]{1,0:T(8,128)(2,1)S(1)}, u32[]{:S(2)}, u32[]{:S(2)}) collective-permute-start(bf16[128,2048]{1,0:T(8,128)(2,1)S(1)} %get-tuple-element.227.refs_0_), channel_id=1, source_target_pairs={{6,0},{0,2},{2,4},{4,6},{7,1},{1,3},{3,5},{5,7},{14,8},{8,10},{10,... | collective-permute-start | bytes 1572872 | tf_op jit(solution)/shard_map/ppermute | solution.py:29
  174.0 27.2 %collective-permute-start.22 = (bf16[128,2048]{1,0:T(8,128)(2,1)S(1)}, bf16[128,2048]{1,0:T(8,128)(2,1)S(1)}, u32[]{:S(2)}, u32[]{:S(2)}) collective-permute-start(bf16[128,2048]{1,0:T(8,128)(2,1)S(1)} %get-tuple-element.227.refs_0_), channel_id=1, source_target_pairs={{2,0},{4,2},{6,4},{0,6},{3,1},{5,3},{7,5},{1,7},{10,8},{12,10},{14... | collective-permute-start | bytes 1572872 | tf_op jit(solution)/shard_map/ppermute | solution.py:29
  177.3 25.3 %collective-permute-start.25 = (bf16[128,2048]{1,0:T(8,128)(2,1)S(1)}, bf16[128,2048]{1,0:T(8,128)(2,1)S(1)}, u32[]{:S(2)}, u32[]{:S(2)}) collective-permute-start(bf16[128,2048]{1,0:T(8,128)(2,1)S(1)} %get-tuple-element.227.refs_0_), channel_id=1, source_target_pairs={{1,0},{0,1},{3,2},{2,3},{5,4},{4,5},{7,6},{6,7},{9,8},{8,9},{11,10... | collective-permute-start | bytes 1572872 | tf_op jit(solution)/shard_map/ppermute | solution.py:29
  177.3 26.1 %collective-permute-start.23 = (bf16[128,2048]{1,0:T(8,128)(2,1)S(1)}, bf16[128,2048]{1,0:T(8,128)(2,1)}, u32[]{:S(2)}, u32[]{:S(2)}) collective-permute-start(bf16[128,2048]{1,0:T(8,128)(2,1)S(1)} %get-tuple-element.227.refs_0_), channel_id=1, source_target_pairs={{4,0},{6,2},{0,4},{2,6},{5,1},{7,3},{1,5},{3,7},{12,8},{14,10},{8,... | collective-permute-start | bytes 1572872 | tf_op jit(solution)/shard_map/ppermute | solution.py:29
  259.4 141.8 %reduce-scatter.5.cloned.1.call-start = ((), (), s32[]{:S(2)}) async-start(), calls=%async_computation.8 | async-start | bytes 4718592 | tf_op jit(solution)/shard_map/reduce_scatter | solution.py:802
  283.0 25.0 %collective-permute-start.34 = (bf16[128,2048]{1,0:T(8,128)(2,1)S(1)}, bf16[128,2048]{1,0:T(8,128)(2,1)S(1)}, u32[]{:S(2)}, u32[]{:S(2)}) collective-permute-start(bf16[128,2048]{1,0:T(8,128)(2,1)S(1)} %get-tuple-element.276.refs_0_), channel_id=1, source_target_pairs={{4,0},{6,2},{0,4},{2,6},{5,1},{7,3},{1,5},{3,7},{12,8},{14,10},{8,... | collective-permute-start | bytes 1572872 | tf_op jit(solution)/shard_map/ppermute | solution.py:29
  285.8 22.8 %collective-permute-start.33 = (bf16[128,2048]{1,0:T(8,128)(2,1)S(1)}, bf16[128,2048]{1,0:T(8,128)(2,1)S(1)}, u32[]{:S(2)}, u32[]{:S(2)}) collective-permute-start(bf16[128,2048]{1,0:T(8,128)(2,1)S(1)} %get-tuple-element.276.refs_0_), channel_id=1, source_target_pairs={{2,0},{4,2},{6,4},{0,6},{3,1},{5,3},{7,5},{1,7},{10,8},{12,10},{14... | collective-permute-start | bytes 1572872 | tf_op jit(solution)/shard_map/ppermute | solution.py:29
  315.1 35.9 %collective-permute-start.39 = (bf16[128,2048]{1,0:T(8,128)(2,1)}, bf16[128,2048]{1,0:T(8,128)(2,1)}, u32[]{:S(2)}, u32[]{:S(2)}) collective-permute-start(bf16[128,2048]{1,0:T(8,128)(2,1)} %get-tuple-element.285), channel_id=1, source_target_pairs={{6,0},{0,2},{2,4},{4,6},{7,1},{1,3},{3,5},{5,7},{14,8},{8,10},{10,... | collective-permute-start | bytes 1572872 | tf_op jit(solution)/shard_map/ppermute | solution.py:29
  316.5 34.5 %collective-permute-start.40 = (bf16[128,2048]{1,0:T(8,128)(2,1)}, bf16[128,2048]{1,0:T(8,128)(2,1)}, u32[]{:S(2)}, u32[]{:S(2)}) collective-permute-start(bf16[128,2048]{1,0:T(8,128)(2,1)} %get-tuple-element.286), channel_id=1, source_target_pairs={{4,0},{6,2},{0,4},{2,6},{5,1},{7,3},{1,5},{3,7},{12,8},{14,10},{8,... | collective-permute-start | bytes 1572872 | tf_op jit(solution)/shard_map/ppermute | solution.py:29
  319.2 31.8 %collective-permute-start.41 = (bf16[128,2048]{1,0:T(8,128)(2,1)}, bf16[128,2048]{1,0:T(8,128)(2,1)}, u32[]{:S(2)}, u32[]{:S(2)}) collective-permute-start(bf16[128,2048]{1,0:T(8,128)(2,1)} %get-tuple-element.287), channel_id=1, source_target_pairs={{2,0},{4,2},{6,4},{0,6},{3,1},{5,3},{7,5},{1,7},{10,8},{12,10},{14... | collective-permute-start | bytes 1572872 | tf_op jit(solution)/shard_map/ppermute | solution.py:29
  376.9 37.4 %collective-permute-start.43 = (bf16[128,2048]{1,0:T(8,128)(2,1)}, bf16[128,2048]{1,0:T(8,128)(2,1)S(1)}, u32[]{:S(2)}, u32[]{:S(2)}) collective-permute-start(bf16[128,2048]{1,0:T(8,128)(2,1)} %get-tuple-element.295), channel_id=1, source_target_pairs={{6,0},{0,2},{2,4},{4,6},{7,1},{1,3},{3,5},{5,7},{14,8},{8,10},{10,... | collective-permute-start | bytes 1572872 | tf_op jit(solution)/shard_map/ppermute | solution.py:29
  377.5 36.8 %collective-permute-start.44 = (bf16[128,2048]{1,0:T(8,128)(2,1)}, bf16[128,2048]{1,0:T(8,128)(2,1)}, u32[]{:S(2)}, u32[]{:S(2)}) collective-permute-start(bf16[128,2048]{1,0:T(8,128)(2,1)} %get-tuple-element.296), channel_id=1, source_target_pairs={{4,0},{6,2},{0,4},{2,6},{5,1},{7,3},{1,5},{3,7},{12,8},{14,10},{8,... | collective-permute-start | bytes 1572872 | tf_op jit(solution)/shard_map/ppermute | solution.py:29
  379.5 34.7 %collective-permute-start.45 = (bf16[128,2048]{1,0:T(8,128)(2,1)}, bf16[128,2048]{1,0:T(8,128)(2,1)}, u32[]{:S(2)}, u32[]{:S(2)}) collective-permute-start(bf16[128,2048]{1,0:T(8,128)(2,1)} %get-tuple-element.297), channel_id=1, source_target_pairs={{2,0},{4,2},{6,4},{0,6},{3,1},{5,3},{7,5},{1,7},{10,8},{12,10},{14... | collective-permute-start | bytes 1572872 | tf_op jit(solution)/shard_map/ppermute | solution.py:29
  380.2 34.1 %collective-permute-start.46 = (bf16[8,16,1536]{2,1,0:T(8,128)(2,1)S(1)}, bf16[8,16,1536]{2,1,0:T(8,128)(2,1)}, u32[]{:S(2)}, u32[]{:S(2)}) collective-permute-start(bf16[8,16,1536]{2,1,0:T(8,128)(2,1)S(1)} %all-to-all-done.3.here_ref), channel_id=1, source_target_pairs={{64,0},{0,64},{65,1},{1,65},{66,2},{2,66},{67,3},{3,67},{68,4},{4,... | collective-permute-start | bytes 1179656 | tf_op jit(solution)/shard_map/ppermute | solution.py:29
  382.2 32.0 %collective-permute-start.47 = (bf16[48,2048]{1,0:T(8,128)(2,1)S(1)}, bf16[48,2048]{1,0:T(8,128)(2,1)S(1)}, u32[]{:S(2)}, u32[]{:S(2)}) collective-permute-start(bf16[48,2048]{1,0:T(8,128)(2,1)S(1)} %maximum_maximum_fusion), channel_id=1, source_target_pairs={{64,0},{0,64},{65,1},{1,65},{66,2},{2,66},{67,3},{3,67},{68,4},{4,... | collective-permute-start | bytes 589832 | tf_op jit(solution)/shard_map/ppermute | solution.py:29
  416.3 29.7 %all-to-all-start.4 = ((bf16[16,32,768]{2,1,0:T(8,128)(2,1)}), bf16[16,32,768]{2,1,0:T(8,128)(2,1)S(1)}, u32[]{:S(2)}, u32[]{:S(2)}) async-start(bf16[16,32,768]{2,1,0:T(8,128)(2,1)} %pad_maximum_fusion.1), calls=%async_computation.6 | async-start | bytes 1572864 | tf_op jit(solution)/shard_map/all_to_all | solution.py:816
  423.2 22.8 %collective-permute-start.49 = (bf16[8,32,256]{2,1,0:T(8,128)(2,1)}, bf16[8,32,256]{2,1,0:T(8,128)(2,1)S(1)}, u32[]{:S(2)}, u32[]{:S(2)}) collective-permute-start(bf16[8,32,256]{2,1,0:T(8,128)(2,1)} %bitcast.16), channel_id=1, source_target_pairs={{0,64},{1,72},{2,80},{3,88},{4,96},{5,104},{6,112},{7,120},{8,65},... | collective-permute-start | bytes 393224 | tf_op jit(solution)/shard_map/ppermute | solution.py:41
  427.6 18.4 %collective-permute-start.48 = (bf16[8,32,256]{2,1,0:T(8,128)(2,1)}, bf16[8,32,256]{2,1,0:T(8,128)(2,1)}, u32[]{:S(2)}, u32[]{:S(2)}) collective-permute-start(bf16[8,32,256]{2,1,0:T(8,128)(2,1)} %bitcast.16), channel_id=1, source_target_pairs={{0,0},{1,8},{2,16},{3,24},{4,32},{5,40},{6,48},{7,56},{8,1},{9,9},... | collective-permute-start | bytes 393224 | tf_op jit(solution)/shard_map/ppermute | solution.py:41
  (107 other events, 743.4 us)
Sparse Core Ops, SparseCore 0:
  110.7 97.3 all-gather.2
  259.5 85.5 reduce-scatter.2
  351.1 50.0 reduce-scatter.4

commit v4 on v3

--- a/solution.py
+++ b/solution.py
@@ -70,12 +70,76 @@
     return lax.dot_general(left, right, (((1,), (1,)), ((), ())), preferred_element_type=full)
 
 
-def attn_cut_kernel(q_ref, k_ref, v_ref, gain_ref, out_ref):
-    wide = q_ref.shape[1] // N_TEAM
+def attn_cut_kernel(gain_ref, mlp_gain_ref, *refs):
+    sources, out_ref, held, rows, arrived = refs[:3], refs[3], refs[4:7], refs[7], refs[8]
+    copies = [pltpu.make_async_copy(sources[i], held[i], arrived.at[i]) for i in range(3)]
+    for copy in copies:
+        copy.start()
+    shard, width = sources[0].shape
+    wide = width // N_TEAM
+    rows[...] = jnp.zeros_like(rows)
+    rows[0:1, :shard] = gain_ref[...].astype(full)
+    rows[1:2, :shard] = mlp_gain_ref[...].astype(full)
+    gains = rows[...].T[:shard].astype(low)
+    out_ref[:, :, 3 * wide :] = jnp.zeros((N_TEAM, shard, out_ref.shape[2] - 3 * wide), low)
+    for copy in copies:
+        copy.wait()
     for t in range(N_TEAM):
-        for i, ref in enumerate((q_ref, k_ref, v_ref)):
+        for i, ref in enumerate(held):
             out_ref[t, :, i * wide : (i + 1) * wide] = ref[:, t * wide : (t + 1) * wide]
-        out_ref[t, :, 3 * wide :] = gain_ref[...]
+        out_ref[t, :, 3 * wide : 3 * wide + 8] = gains
+
+
+def attn_cut(w_query, w_key, w_value, norm_gain, mlp_gain):
+    shard, width = w_query.shape
+    vmem = pl.BlockSpec(memory_space=pltpu.VMEM)
+    return pl.pallas_call(
+        attn_cut_kernel,
+        in_specs=[vmem] * 2 + [pl.BlockSpec(memory_space=pl.ANY)] * 3,
+        out_shape=jax.ShapeDtypeStruct((N_TEAM, shard, 3 * width // N_TEAM + 128), low),
+        scratch_shapes=[pltpu.VMEM((shard, width), low)] * 3
+        + [pltpu.VMEM((8, 128), full), pltpu.SemaphoreType.DMA((3,))],
+        compiler_params=pltpu.CompilerParams(vmem_limit_bytes=8 << 20),
+    )(norm_gain[None], mlp_gain[None], w_query, w_key, w_value)
+
+
+def assemble_kernel(at, own_ref, low_ref, high_ref, *refs):
+    *pair_refs, qkv_ref, out_ref, gain_ref = refs
+    yl, x = at[0], at[1]
+    rows = own_ref.shape[0]
+    qkv_ref[pl.ds(pl.multiple_of(yl * rows, 256), rows)] = own_ref[...]
+    there = (1 - yl) * rows
+    qkv_ref[pl.ds(pl.multiple_of(there, 256), rows // 2)] = low_ref[...]
+    qkv_ref[pl.ds(pl.multiple_of(there + rows // 2, 256), rows // 2)] = high_ref[...]
+    block, wide = pair_refs[0].shape[0] // 2, pair_refs[0].shape[1] - 128
+    shard = block // N_TEAM
+    for k, pair_ref in enumerate(pair_refs):
+        for side in range(2):
+            fleet = (yl + side) % 2 * N_X + (x + k) % N_X
+            piece = slice(side * block, (side + 1) * block)
+            gains = pair_ref[piece, :128].astype(full).T[: gain_ref.shape[0]]
+            gain_ref[:, pl.ds(pl.multiple_of(fleet * block, 256), block)] = gains
+            to = pl.ds(pl.multiple_of(fleet * shard, 32), shard)
+            for t in range(N_TEAM):
+                first = side * block + t * shard
+                out_ref[to, t * wide : (t + 1) * wide] = pair_ref[first : first + shard, 128:]
+
+
+def assemble(at, own, there, pairs):
+    width, wide = 2 * own.shape[0], pairs[0].shape[1] - 128
+    vmem = pl.BlockSpec(memory_space=pltpu.VMEM)
+    return pl.pallas_call(
+        assemble_kernel,
+        in_specs=[pl.BlockSpec(memory_space=pltpu.SMEM)] + [vmem] * (3 + N_X),
+        out_specs=[vmem] * 3,
+        out_shape=[
+            jax.ShapeDtypeStruct((width, own.shape[1]), low),
+            jax.ShapeDtypeStruct((wide, width), low),
+            jax.ShapeDtypeStruct((8, width), full),
+        ],
+        compiler_params=pltpu.CompilerParams(vmem_limit_bytes=16 << 20),
+        cost_estimate=FILLS,
+    )(at, own, *there, *pairs)
 
 
 def feed_cut_kernel(unit_rows, gate_ref, up_ref, out_ref):
@@ -90,15 +154,6 @@
                 out_ref[t, :, at : at + unit_rows] = ref[:, first : first + unit_rows]
 
 
-def attn_cut(w_query, w_key, w_value, gains):
-    shard, width = w_query.shape
-    return pl.pallas_call(
-        attn_cut_kernel,
-        out_shape=jax.ShapeDtypeStruct((N_TEAM, shard, 3 * width // N_TEAM + gains.shape[1]), low),
-        compiler_params=pltpu.CompilerParams(vmem_limit_bytes=8 << 20),
-    )(w_query, w_key, w_value, gains)
-
-
 def feed_cut(w_gate, w_up, unit_rows, units):
     return pl.pallas_call(
         functools.partial(feed_cut_kernel, unit_rows),
@@ -142,9 +197,8 @@
 
 
 def norm_kernel(*refs):
-    *block_refs, gain_ref, out_ref, rows_ref = refs
-    rows_ref[...] = gain_ref[...].astype(full).T[: rows_ref.shape[0]]
-    gain = rows_ref[:1]
+    *block_refs, gain_ref, out_ref = refs
+    gain = gain_ref[:1]
     at = 0
     for ref in block_refs:
         for first in range(0, ref.shape[0], 16):
@@ -153,15 +207,14 @@
         at += ref.shape[0]
 
 
-def normalised(blocks, gain_columns):
+def normalised(blocks, gain_rows):
     rows = sum(block.shape[0] for block in blocks)
-    width = blocks[0].shape[1]
     return pl.pallas_call(
         norm_kernel,
-        out_shape=[jax.ShapeDtypeStruct((rows, width), low), jax.ShapeDtypeStruct((8, width), full)],
+        out_shape=jax.ShapeDtypeStruct((rows, blocks[0].shape[1]), low),
         compiler_params=pltpu.CompilerParams(vmem_limit_bytes=14 << 20),
         cost_estimate=FILLS,
-    )(*blocks, gain_columns)
+    )(*blocks, gain_rows)
 
 
 TILE = 256
@@ -708,52 +761,48 @@
     mask = (distance >= 0) & (distance < WIN) & (query_segs[:, :, None] == key_segs[:, None, :])
     mask = mask.astype(full)
 
-    gains = jnp.concatenate([norm_gain[:, None], mlp_gain[:, None], jnp.zeros((shard, 126), low)], axis=1)
     out_there = swapped(w_out)
     x_mine = [tokens, from_ahead(tokens, "z", 1), None, from_ahead(tokens, "z", 3)]
-    cut = attn_cut(w_query, w_key, w_value, gains)
+    cut = attn_cut(w_query, w_key, w_value, norm_gain, mlp_gain)
     cut = lax.all_to_all(cut, TEAM, 0, 0, tiled=True).reshape(N_TEAM * shard, -1)
     out_cut = out_there.reshape(shard, N_TEAM, team_wide).transpose(1, 0, 2)
     out_cut = out_cut.reshape(N_TEAM * shard, team_wide)
     cut, out_cut, x_mine, w_gate_later, dy = lax.optimization_barrier((cut, out_cut, x_mine, w_gate, cotangent))
-    at_out = cut.shape[1]
-    attn_piece = jnp.concatenate([cut, out_cut], axis=1)
+    qkv_piece, rest = cut[:, : 3 * team_wide], jnp.concatenate([cut[:, 3 * team_wide :], out_cut], axis=1)
     along_y = lambda value, by: from_ahead(value, ("g", "yl"), by)
     other = lambda block: from_ahead(block, "c", 1)
-    attn = lax.all_to_all(jnp.broadcast_to(attn_piece, (N_X, *attn_piece.shape)), "x", 0, 0, tiled=True)
-    attn = attn.reshape(N_X * N_TEAM * shard, -1)
+    attn = lax.all_to_all(jnp.broadcast_to(qkv_piece, (N_X, *qkv_piece.shape)), "x", 0, 0, tiled=True)
+    attn = attn.reshape(width // 2, -1)
+    half_rest = rest.shape[0] // 2
+    rest_there = along_y(rest[:half_rest], 1), along_y(rest[half_rest:], -1)
     x_mine[2] = from_ahead(x_mine[0], "z", 2)
     x_other = [other(x_mine[0]), other(x_mine[1]), None, other(x_mine[3])]
     gate_up = feed_cut(w_gate_later, w_up, unit_rows, units)
     down_piece = pack(w_down, unit_pad, 2 * units)
-    attn, x_mine, x_other, dy, gate_up, down_piece, place, mask = lax.optimization_barrier(
-        (attn, x_mine, x_other, dy, gate_up, down_piece, place, mask)
-    )
+    attn, rest_there, x_mine, x_other, dy, gate_up, down_piece, place, mask = lax.optimization_barrier(
+        (attn, rest_there, x_mine, x_other, dy, gate_up, down_piece, place, mask)
+    )
+    pair = jnp.concatenate([rest, *rest_there], axis=0)
+    pairs = [pair] + [from_ahead(pair, "x", k) for k in (1, 2, 3)]
     x_other[2] = other(x_mine[2])
+    gate_up_piece = lax.all_to_all(gate_up, TEAM, 0, 0, tiled=True).reshape(N_TEAM * shard, -1)
+    attn_there = along_y(attn[: width // 4], 1), along_y(attn[width // 4 :], -1)
+    attn, attn_there, pairs, x_mine, x_other, dy, gate_up_piece = lax.optimization_barrier(
+        (attn, attn_there, pairs, x_mine, x_other, dy, gate_up_piece)
+    )
+    dy_mine = [dy, from_ahead(dy, "z", 1), None, from_ahead(dy, "z", 3)]
     x_blocks = x_mine + x_other
     halo = along_line(lax.select_n(last_spot, *[block[BLOCK - WIN :] for block in x_blocks]), 1)
-    gate_up_piece = lax.all_to_all(gate_up, TEAM, 0, 0, tiled=True).reshape(N_TEAM * shard, -1)
-    attn_there = along_y(attn[: width // 4], 1), along_y(attn[width // 4 :], -1)
-    dy_mine = [dy, from_ahead(dy, "z", 1), None, from_ahead(dy, "z", 3)]
-    attn, attn_there, x_blocks, halo, dy_mine, gate_up_piece = lax.optimization_barrier(
-        (attn, attn_there, x_blocks, halo, dy_mine, gate_up_piece)
-    )
     feed_piece = jnp.concatenate([gate_up_piece, down_piece], axis=0)
     w_feed = lax.all_gather(feed_piece, FLEET, axis=0, tiled=False)
-    dy_mine[2] = from_ahead(dy_mine[0], "z", 2)
 
     half = N_Z * BLOCK
-    whole = jnp.zeros((width, attn.shape[1]), low)
-    whole = lax.dynamic_update_slice(whole, attn, (yl * (width // 2), 0))
-    whole = lax.dynamic_update_slice(whole, attn_there[0], ((1 - yl) * (width // 2), 0))
-    attn = lax.dynamic_update_slice(whole, attn_there[1], ((1 - yl) * (width // 2) + width // 4, 0))
-    w_qkv = attn[:, : 3 * team_wide]
-    w_out_team = attn[:, at_out:].reshape(N_FLEET, N_TEAM, shard, team_wide)
-    w_out_team = w_out_team.transpose(0, 2, 1, 3).reshape(N_FLEET * shard, width)
-    normed, gain_rows = normalised(x_blocks, attn[:, 3 * team_wide : at_out])
+    w_qkv, w_out_team, gain_rows = assemble(jnp.stack([yl, x]).astype(jnp.int32), attn, attn_there, pairs)
+    normed = normalised(x_blocks, gain_rows)
     gain_one, gain_two = gain_rows[:1], gain_rows[1:2]
     qkv = matmul(normed, w_qkv).astype(low)
-    qkv, dy_mine = lax.optimization_barrier((qkv, dy_mine))
+    qkv, dy_mine, halo = lax.optimization_barrier((qkv, dy_mine, halo))
+    dy_mine[2] = from_ahead(dy_mine[0], "z", 2)
     halo = halo.astype(full)
     halo = matmul((halo * inverse_rms(halo) * gain_one).astype(low), w_qkv[:, team_wide:]).astype(low)
     mixed = attend(place, qkv, halo, mask)

time: 464 us -> 457 us (0.985)
  the two profiles are of different devices: /device:TPU:8 before, /device:TPU:14 now
where the time goes in v4:
time: 457 us; the launch traced here: 449 us
  waiting for transfers between devices  173 us (38%)
  Pallas kernels  94.4 us (21%)
  starting transfers between devices  87.2 us (19%)
  local copies, waits for them, and re-layouts  54.5 us (12%)
  between operations  15.2 us (3%)
  matrix products  12.6 us (3%)
  other arithmetic  12 us (3%)
    ppermute x50, waiting for transfers between devices, from_ahead(): return lax.ppermute(value, axis, [((i + by) % n, i) for i in range(n)])  130 us
    ppermute x50, starting transfers between devices, from_ahead(): return lax.ppermute(value, axis, [((i + by) % n, i) for i in range(n)])  47.8 us
    unnamed x210, local copies, waits for them, and re-layouts  44.8 us
    reduce_scatter x1, waiting for transfers between devices, body(): lax.psum_scatter(attn_term, FLEET, scatter_dimension=0, tiled=True)  17.2 us
    pallas_call x2, Pallas kernels, feed(): pl.pallas_call(feed_kernel, grid=(tiles,), in_specs=[pl.BlockSpec(memory_...  14.8 us
    pallas_call x1, Pallas kernels, feed_terms(): pl.pallas_call(terms_kernel, grid=(N_FLEET,), in_specs=[cut] * 2 + [whole...  13.4 us
    ppermute x3, starting transfers between devices, swapped(): lax.ppermute(value, ALL, [(g * n + a, (g ^ across) * n + b) for g in rang...  12.9 us
    pallas_call x1, Pallas kernels, attend_back(): pl.pallas_call(attend_back_kernel, grid_spec=pltpu.PrefetchScalarGridSpec...  11.9 us
  transfers between devices with their start and end apart: 63, of which 24 were waited for; matrix products, arithmetic and copies ran while one was open for 6% of the time, Pallas kernels for 18%

profile of v4, /device:TPU:14, one launch (start us, length us, event | category | flops | bytes accessed | tf_op | source)
XLA Modules:
  0.0 449.3 jit_solution(4316178444465016047)
XLA Ops:
  24.5 8.0 %all-to-all-done = bf16[8,32,896]{2,1,0:T(8,128)(2,1)S(1)} async-done(((bf16[8,32,896]{2,1,0:T(8,128)(2,1)}), bf16[8,32,896]{2,1,0:T(8,128)(2,1)S(1)}, u32[]{:S(2)}, u32[]{:S(2)}) %all-to-all-start) | async-done | bytes 458784 | tf_op jit(solution)/shard_map/all_to_all | solution.py:767
  34.7 6.8 %all-to-all-start.1 = ((bf16[4,256,768]{2,1,0:T(8,128)(2,1)}), bf16[4,256,768]{2,1,0:T(8,128)(2,1)S(1)}, u32[]{:S(2)}, u32[]{:S(2)}) async-start(bf16[4,256,768]{2,1,0:T(8,128)(2,1)} %broadcast_in_dim.18), calls=%async_computation.1 | async-start | bytes 3145728 | tf_op jit(solution)/shard_map/all_to_all | solution.py:774
  67.2 4.2 all-to-all-start.2
  73.2 12.1 %collective-permute-done.12.refs_2_ = bf16[512,384]{1,0:T(8,128)(2,1)S(1)} collective-permute-done((bf16[512,384]{1,0:T(8,128)(2,1)S(1)}, bf16[512,384]{1,0:T(8,128)(2,1)S(1)}, u32[]{:S(2)}, u32[]{:S(2)}) %collective-permute-start.12) | collective-permute-done | bytes 393248 | tf_op jit(solution)/shard_map/ppermute | solution.py:29
  86.0 6.7 %collective-permute-done.11.refs_1_ = bf16[512,384]{1,0:T(8,128)(2,1)S(1)} collective-permute-done((bf16[512,384]{1,0:T(8,128)(2,1)S(1)}, bf16[512,384]{1,0:T(8,128)(2,1)S(1)}, u32[]{:S(2)}, u32[]{:S(2)}) %collective-permute-start.11) | collective-permute-done | bytes 393248 | tf_op jit(solution)/shard_map/ppermute | solution.py:29
  104.4 3.6 shard_map.207.normed_ref
  111.5 3.6 collective-permute-done.17
  115.8 7.8 %shard_map.208.mixed_ref = bf16[1024,256]{1,0:T(8,128)(2,1)S(1)} custom-call(s32[16]{0:T(128)S(1)} %pad_add_fusion.place, bf16[1024,768]{1,0:T(8,128)(2,1)S(1)} %convolution_convert_fusion.2.q_ref.k_ref.v_ref.kp_ref.vp_ref, bf16[1024,768]{1,0:T(8,128)(2,1)S(1)} %convolution_convert_fusion.2.q_ref.k_ref.v_ref.kp_ref.vp_ref, ...), custom_call_target="tpu_custom_call" | custom-call | flops 1 | bytes 1 | tf_op jit(solution)/shard_map/pallas_call | solution.py:541
  129.0 11.3 %collective-permute-done.19.refs_6_ = bf16[128,2048]{1,0:T(8,128)(2,1)S(1)} collective-permute-done((bf16[128,2048]{1,0:T(8,128)(2,1)S(1)}, bf16[128,2048]{1,0:T(8,128)(2,1)S(1)}, u32[]{:S(2)}, u32[]{:S(2)}) %collective-permute-start.19) | collective-permute-done | bytes 524320 | tf_op jit(solution)/shard_map/ppermute | solution.py:29
  144.1 21.8 %collective-permute-done.20.refs_1_ = bf16[128,2048]{1,0:T(8,128)(2,1)S(1)} collective-permute-done((bf16[128,2048]{1,0:T(8,128)(2,1)S(1)}, bf16[128,2048]{1,0:T(8,128)(2,1)S(1)}, u32[]{:S(2)}, u32[]{:S(2)}) %collective-permute-start.20) | collective-permute-done | bytes 524320 | tf_op jit(solution)/shard_map/ppermute | solution.py:29
  174.3 22.4 %collective-permute-done.29.refs_3_ = bf16[128,2048]{1,0:T(8,128)(2,1)S(1)} collective-permute-done((bf16[128,2048]{1,0:T(8,128)(2,1)S(1)}, bf16[128,2048]{1,0:T(8,128)(2,1)S(1)}, u32[]{:S(2)}, u32[]{:S(2)}) %collective-permute-start.29) | collective-permute-done | bytes 524320 | tf_op jit(solution)/shard_map/ppermute | solution.py:29
  201.6 3.7 copy-done.4
  208.0 7.4 %shard_map.214 = (bf16[512,768]{1,0:T(8,128)(2,1)S(1)}, bf16[512,768]{1,0:T(8,128)(2,1)S(1)}, bf16[512,768]{1,0:T(8,128)(2,1)S(1)}, bf16[512,2048]{1,0:T(8,128)(2,1)S(1)}, bf16[512,2048]{1,0:T(8,128)(2,1)S(1)}) custom-call(bf16[128,2048]{1,0:T(8,128)(2,1)S(1)} %copy-done.73, bf16[128,2048]{1,0:T(8,128)(2,1)S(1)} %copy-done.77, ...), custom_call_target="tpu_custom_call" | custom-call | flops 1 | bytes 1 | tf_op jit(solution)/shard_map/pallas_call | solution.py:253
  215.5 4.2 shard_map.215
  220.3 7.4 %shard_map.212 = (bf16[512,768]{1,0:T(8,128)(2,1)S(1)}, bf16[512,768]{1,0:T(8,128)(2,1)S(1)}, bf16[512,768]{1,0:T(8,128)(2,1)S(1)}, bf16[512,2048]{1,0:T(8,128)(2,1)S(1)}, bf16[512,2048]{1,0:T(8,128)(2,1)S(1)}) custom-call(bf16[128,2048]{1,0:T(8,128)(2,1)S(1)} %copy-done.65, bf16[128,2048]{1,0:T(8,128)(2,1)S(1)} %copy-done.71, ...), custom_call_target="tpu_custom_call" | custom-call | flops 1 | bytes 1 | tf_op jit(solution)/shard_map/pallas_call | solution.py:253
  227.7 4.3 shard_map.213.here_ref
  237.4 13.4 %shard_map.217 = bf16[2,8,192,1536]{3,2,1,0:T(8,128)(2,1)} custom-call(bf16[512,2048]{1,0:T(8,128)(2,1)S(1)} %get-tuple-element.265.x0_ref, bf16[512,2048]{1,0:T(8,128)(2,1)S(1)} %get-tuple-element.266.x1_ref, bf16[512,2048]{1,0:T(8,128)(2,1)S(1)} %get-tuple-element.267.dy0_ref, bf16[512,2048]{1,0:T(8,128)(2,1)S(1)} %get-tuple-element.268.dy1_ref, ...), custom_call_target="tpu_custom_call" | custom-call | flops 10000000000 | bytes 20000000 | tf_op jit(solution)/shard_map/pallas_call | solution.py:392
  252.5 15.0 %collective-permute-done.37.refs_2_ = bf16[128,2048]{1,0:T(8,128)(2,1)S(1)} collective-permute-done((bf16[128,2048]{1,0:T(8,128)(2,1)}, bf16[128,2048]{1,0:T(8,128)(2,1)S(1)}, u32[]{:S(2)}, u32[]{:S(2)}) %collective-permute-start.37) | collective-permute-done | bytes 524320 | tf_op jit(solution)/shard_map/ppermute | solution.py:29
  279.9 4.6 %shard_map.219 = (f32[512,2048]{1,0:T(8,128)S(1)}, bf16[512,2048]{1,0:T(8,128)(2,1)S(1)}) custom-call(bf16[512,768]{1,0:T(8,128)(2,1)S(1)} %copy-done.51, bf16[512,768]{1,0:T(8,128)(2,1)S(1)} %copy-done.49, bf16[768,2048]{1,0:T(8,128)(2,1)S(1)} %copy-done.1), custom_call_target="tpu_custom_call" | custom-call | flops 1 | bytes 1 | tf_op jit(solution)/shard_map/pallas_call | solution.py:414
  284.5 15.8 %collective-permute-done.40.refs_3_ = bf16[128,2048]{1,0:T(8,128)(2,1)S(1)} collective-permute-done((bf16[128,2048]{1,0:T(8,128)(2,1)S(1)}, bf16[128,2048]{1,0:T(8,128)(2,1)S(1)}, u32[]{:S(2)}, u32[]{:S(2)}) %collective-permute-start.40) | collective-permute-done | bytes 524320 | tf_op jit(solution)/shard_map/ppermute | solution.py:29
  307.6 3.6 collective-permute-start.45
  316.7 11.9 %shard_map.221 = (bf16[1024,768]{1,0:T(8,128)(2,1)S(1)}, f32[64,512]{1,0:T(8,128)S(1)}) custom-call(s32[16]{0:T(128)S(1)} %pad_add_fusion.place, bf16[1024,768]{1,0:T(8,128)(2,1)S(1)} %convolution_convert_fusion.2.q_ref.k_ref.v_ref.kp_ref.vp_ref, bf16[1024,768]{1,0:T(8,128)(2,1)S(1)} %convolution_convert_fusion.2.q_ref.k_ref.v_ref.kp_ref.vp_ref, ...), custom_call_target="tpu_custom_call" | custom-call | flops 1 | bytes 1 | tf_op jit(solution)/shard_map/pallas_call | solution.py:560
  328.6 8.0 %shard_map.223 = bf16[2048,1024]{1,0:T(8,128)(2,1)} custom-call(bf16[1024,2048]{1,0:T(8,128)(2,1)S(1)} %copy-done.3, bf16[1024,768]{1,0:T(8,128)(2,1)S(1)} %fusion.22.grad_ref, bf16[1024,256]{1,0:T(8,128)(2,1)S(1)} %copy-done.9, bf16[512,2048]{1,0:T(8,128)(2,1)S(1)} %copy-done.6, bf16[512,2048]{1,0:T(8,128)(2,1)S(1)} %copy-done.19), custom_call_target="tpu_custom_call" | custom-call | flops 1 | bytes 1 | tf_op jit(solution)/shard_map/pallas_call | solution.py:601
  339.2 3.9 convolution_convert_fusion.1
  351.6 3.6 all-to-all-start.3
  356.1 8.0 %all-to-all-done.3.here_ref = bf16[8,16,1536]{2,1,0:T(8,128)(2,1)S(1)} async-done(((bf16[8,16,1536]{2,1,0:T(8,128)(2,1)}), bf16[8,16,1536]{2,1,0:T(8,128)(2,1)S(1)}, u32[]{:S(2)}, u32[]{:S(2)}) %all-to-all-start.3) | async-done | bytes 393248 | tf_op jit(solution)/shard_map/all_to_all | solution.py:857
  375.0 17.2 %reduce-scatter.5.cloned.1.call-done = bf16[256,1024]{1,0:T(8,128)(2,1)} async-done(((bf16[2048,1024]{1,0:T(8,128)(2,1)}), bf16[256,1024]{1,0:T(8,128)(2,1)}) %reduce-scatter.5.cloned.1.call-update) | async-done | bytes 524304 | tf_op jit(solution)/shard_map/reduce_scatter | solution.py:851
  392.3 12.5 %collective-permute-done.52 = bf16[48,2048]{1,0:T(8,128)(2,1)} collective-permute-done((bf16[48,2048]{1,0:T(8,128)(2,1)S(1)}, bf16[48,2048]{1,0:T(8,128)(2,1)}, u32[]{:S(2)}, u32[]{:S(2)}) %collective-permute-start.52) | collective-permute-done | bytes 196640 | tf_op jit(solution)/shard_map/ppermute | solution.py:29
  406.8 5.2 %all-to-all-start.4 = ((bf16[16,32,768]{2,1,0:T(8,128)(2,1)}), bf16[16,32,768]{2,1,0:T(8,128)(2,1)S(1)}, u32[]{:S(2)}, u32[]{:S(2)}) async-start(bf16[16,32,768]{2,1,0:T(8,128)(2,1)} %pad_maximum_fusion.1), calls=%async_computation.6 | async-start | bytes 1572864 | tf_op jit(solution)/shard_map/all_to_all | solution.py:865
  413.8 5.9 %collective-permute-start.54 = (bf16[8,32,256]{2,1,0:T(8,128)(2,1)}, bf16[8,32,256]{2,1,0:T(8,128)(2,1)S(1)}, u32[]{:S(2)}, u32[]{:S(2)}) collective-permute-start(bf16[8,32,256]{2,1,0:T(8,128)(2,1)} %bitcast.16), channel_id=1, source_target_pairs={{0,64},{1,72},{2,80},{3,88},{4,96},{5,104},{6,112},{7,120},{8,65},... | collective-permute-start | bytes 393224 | tf_op jit(solution)/shard_map/ppermute | solution.py:41
  419.7 4.5 %collective-permute-start.53 = (bf16[8,32,256]{2,1,0:T(8,128)(2,1)}, bf16[8,32,256]{2,1,0:T(8,128)(2,1)}, u32[]{:S(2)}, u32[]{:S(2)}) collective-permute-start(bf16[8,32,256]{2,1,0:T(8,128)(2,1)} %bitcast.16), channel_id=1, source_target_pairs={{0,0},{1,8},{2,16},{3,24},{4,32},{5,40},{6,48},{7,56},{8,1},{9,9},... | collective-permute-start | bytes 393224 | tf_op jit(solution)/shard_map/ppermute | solution.py:41
  435.1 4.8 %all-to-all-done.4.sums_ref = bf16[16,32,768]{2,1,0:T(8,128)(2,1)S(1)} async-done(((bf16[16,32,768]{2,1,0:T(8,128)(2,1)}), bf16[16,32,768]{2,1,0:T(8,128)(2,1)S(1)}, u32[]{:S(2)}, u32[]{:S(2)}) %all-to-all-start.4) | async-done | bytes 786464 | tf_op jit(solution)/shard_map/all_to_all | solution.py:865
  (380 shorter events, 161.1 us)
Async XLA Ops:
  7.2 25.3 %collective-permute-start.2 = (bf16[128,2048]{1,0:T(8,128)(2,1)}, bf16[128,2048]{1,0:T(8,128)(2,1)S(1)}, u32[]{:S(2)}, u32[]{:S(2)}) collective-permute-start(bf16[128,2048]{1,0:T(8,128)(2,1)} %refs_4_.4), channel_id=1, source_target_pairs={{6,0},{0,2},{2,4},{4,6},{7,1},{1,3},{3,5},{5,7},{14,8},{8,10},{10,... | collective-permute-start | bytes 1572872 | tf_op jit(solution)/shard_map/ppermute | solution.py:29
  9.2 23.3 %collective-permute-start.1 = (bf16[128,2048]{1,0:T(8,128)(2,1)}, bf16[128,2048]{1,0:T(8,128)(2,1)S(1)}, u32[]{:S(2)}, u32[]{:S(2)}) collective-permute-start(bf16[128,2048]{1,0:T(8,128)(2,1)} %refs_4_.4), channel_id=1, source_target_pairs={{2,0},{4,2},{6,4},{0,6},{3,1},{5,3},{7,5},{1,7},{10,8},{12,10},{14... | collective-permute-start | bytes 1572872 | tf_op jit(solution)/shard_map/ppermute | solution.py:29
  34.7 25.1 %all-to-all-start.1 = ((bf16[4,256,768]{2,1,0:T(8,128)(2,1)}), bf16[4,256,768]{2,1,0:T(8,128)(2,1)S(1)}, u32[]{:S(2)}, u32[]{:S(2)}) async-start(bf16[4,256,768]{2,1,0:T(8,128)(2,1)} %broadcast_in_dim.18), calls=%async_computation.1 | async-start | bytes 3145728 | tf_op jit(solution)/shard_map/all_to_all | solution.py:774
  64.2 29.2 %collective-permute-start.10 = (bf16[512,768]{1,0:T(8,128)(2,1)}, bf16[512,768]{1,0:T(8,128)(2,1)}, u32[]{:S(2)}, u32[]{:S(2)}) collective-permute-start(bf16[512,768]{1,0:T(8,128)(2,1)} %get-tuple-element.337), channel_id=1, source_target_pairs={{96,0},{0,32},{32,64},{64,96},{97,1},{1,33},{33,65},{65,97},{98,2}... | collective-permute-start | bytes 2359304 | tf_op jit(solution)/shard_map/ppermute | solution.py:29
  67.2 26.3 %collective-permute-start.9 = (bf16[512,768]{1,0:T(8,128)(2,1)}, bf16[512,768]{1,0:T(8,128)(2,1)}, u32[]{:S(2)}, u32[]{:S(2)}) collective-permute-start(bf16[512,768]{1,0:T(8,128)(2,1)} %get-tuple-element.338), channel_id=1, source_target_pairs={{32,0},{64,32},{96,64},{0,96},{33,1},{65,33},{97,65},{1,97},{34,2}... | collective-permute-start | bytes 2359304 | tf_op jit(solution)/shard_map/ppermute | solution.py:29
  67.2 26.3 %all-to-all-start.2 = ((bf16[8,32,1536]{2,1,0:T(8,128)(2,1)}), bf16[8,32,1536]{2,1,0:T(8,128)(2,1)}, u32[]{:S(2)}, u32[]{:S(2)}) async-start(bf16[8,32,1536]{2,1,0:T(8,128)(2,1)} %copy-done.17), calls=%async_computation.2 | async-start | bytes 1572864 | tf_op jit(solution)/shard_map/all_to_all | solution.py:788
  71.4 130.2 %all-gather.3.cloned.1.call-start = ((), (), s32[]{:S(2)}) async-start(), calls=%async_computation.9 | async-start | bytes 10616832 | tf_op jit(solution)/shard_map/all_gather | solution.py:797
  71.4 22.0 %collective-permute-start.14 = (bf16[128,2048]{1,0:T(8,128)(2,1)}, bf16[128,2048]{1,0:T(8,128)(2,1)}, u32[]{:S(2)}, u32[]{:S(2)}) collective-permute-start(bf16[128,2048]{1,0:T(8,128)(2,1)} %collective-permute-done.5.refs_2_), channel_id=1, source_target_pairs={{1,0},{0,1},{3,2},{2,3},{5,4},{4,5},{7,6},{6,7},{9,8},{8,9},{11,10... | collective-permute-start | bytes 1572872 | tf_op jit(solution)/shard_map/ppermute | solution.py:29
  95.8 253.8 %reduce-scatter.3.cloned.1.call-start = ((), (), s32[]{:S(2)}) async-start(), calls=%async_computation.7 | async-start | bytes 10027008 | tf_op jit(solution)/shard_map/reduce_scatter | solution.py:832
  140.2 25.6 %collective-permute-start.20 = (bf16[128,2048]{1,0:T(8,128)(2,1)S(1)}, bf16[128,2048]{1,0:T(8,128)(2,1)S(1)}, u32[]{:S(2)}, u32[]{:S(2)}) collective-permute-start(bf16[128,2048]{1,0:T(8,128)(2,1)S(1)} %get-tuple-element.223), channel_id=1, source_target_pairs={{6,0},{0,2},{2,4},{4,6},{7,1},{1,3},{3,5},{5,7},{14,8},{8,10},{10,... | collective-permute-start | bytes 1572872 | tf_op jit(solution)/shard_map/ppermute | solution.py:29
  140.2 25.6 %collective-permute-start.21 = (bf16[128,2048]{1,0:T(8,128)(2,1)S(1)}, bf16[128,2048]{1,0:T(8,128)(2,1)S(1)}, u32[]{:S(2)}, u32[]{:S(2)}) collective-permute-start(bf16[128,2048]{1,0:T(8,128)(2,1)S(1)} %get-tuple-element.224), channel_id=1, source_target_pairs={{4,0},{6,2},{0,4},{2,6},{5,1},{7,3},{1,5},{3,7},{12,8},{14,10},{8,... | collective-permute-start | bytes 1572872 | tf_op jit(solution)/shard_map/ppermute | solution.py:29
  141.9 24.6 %collective-permute-start.22 = (bf16[128,2048]{1,0:T(8,128)(2,1)S(1)}, bf16[128,2048]{1,0:T(8,128)(2,1)S(1)}, u32[]{:S(2)}, u32[]{:S(2)}) collective-permute-start(bf16[128,2048]{1,0:T(8,128)(2,1)S(1)} %get-tuple-element.225), channel_id=1, source_target_pairs={{2,0},{4,2},{6,4},{0,6},{3,1},{5,3},{7,5},{1,7},{10,8},{12,10},{14... | collective-permute-start | bytes 1572872 | tf_op jit(solution)/shard_map/ppermute | solution.py:29
  143.5 22.9 %collective-permute-start.23 = (bf16[128,2048]{1,0:T(8,128)(2,1)S(1)}, bf16[128,2048]{1,0:T(8,128)(2,1)S(1)}, u32[]{:S(2)}, u32[]{:S(2)}) collective-permute-start(bf16[128,2048]{1,0:T(8,128)(2,1)S(1)} %copy-done.20), channel_id=1, source_target_pairs={{1,0},{0,1},{3,2},{2,3},{5,4},{4,5},{7,6},{6,7},{9,8},{8,9},{11,10... | collective-permute-start | bytes 1572872 | tf_op jit(solution)/shard_map/ppermute | solution.py:29
  143.5 22.9 %collective-permute-start.24 = (bf16[128,2048]{1,0:T(8,128)(2,1)S(1)}, bf16[128,2048]{1,0:T(8,128)(2,1)S(1)}, u32[]{:S(2)}, u32[]{:S(2)}) collective-permute-start(bf16[128,2048]{1,0:T(8,128)(2,1)S(1)} %collective-permute-done.15.refs_5_), channel_id=1, source_target_pairs={{1,0},{0,1},{3,2},{2,3},{5,4},{4,5},{7,6},{6,7},{9,8},{8,9},{11,10... | collective-permute-start | bytes 1572872 | tf_op jit(solution)/shard_map/ppermute | solution.py:29
  170.2 26.4 %collective-permute-start.29 = (bf16[128,2048]{1,0:T(8,128)(2,1)S(1)}, bf16[128,2048]{1,0:T(8,128)(2,1)S(1)}, u32[]{:S(2)}, u32[]{:S(2)}) collective-permute-start(bf16[128,2048]{1,0:T(8,128)(2,1)S(1)} %get-tuple-element.235.refs_0_), channel_id=1, source_target_pairs={{6,0},{0,2},{2,4},{4,6},{7,1},{1,3},{3,5},{5,7},{14,8},{8,10},{10,... | collective-permute-start | bytes 1572872 | tf_op jit(solution)/shard_map/ppermute | solution.py:29
  170.3 27.6 %collective-permute-start.27 = (bf16[128,2048]{1,0:T(8,128)(2,1)S(1)}, bf16[128,2048]{1,0:T(8,128)(2,1)S(1)}, u32[]{:S(2)}, u32[]{:S(2)}) collective-permute-start(bf16[128,2048]{1,0:T(8,128)(2,1)S(1)} %get-tuple-element.235.refs_0_), channel_id=1, source_target_pairs={{2,0},{4,2},{6,4},{0,6},{3,1},{5,3},{7,5},{1,7},{10,8},{12,10},{14... | collective-permute-start | bytes 1572872 | tf_op jit(solution)/shard_map/ppermute | solution.py:29
  173.5 25.7 %collective-permute-start.30 = (bf16[128,2048]{1,0:T(8,128)(2,1)S(1)}, bf16[128,2048]{1,0:T(8,128)(2,1)S(1)}, u32[]{:S(2)}, u32[]{:S(2)}) collective-permute-start(bf16[128,2048]{1,0:T(8,128)(2,1)S(1)} %get-tuple-element.235.refs_0_), channel_id=1, source_target_pairs={{1,0},{0,1},{3,2},{2,3},{5,4},{4,5},{7,6},{6,7},{9,8},{8,9},{11,10... | collective-permute-start | bytes 1572872 | tf_op jit(solution)/shard_map/ppermute | solution.py:29
  173.5 26.5 %collective-permute-start.28 = (bf16[128,2048]{1,0:T(8,128)(2,1)S(1)}, bf16[128,2048]{1,0:T(8,128)(2,1)}, u32[]{:S(2)}, u32[]{:S(2)}) collective-permute-start(bf16[128,2048]{1,0:T(8,128)(2,1)S(1)} %get-tuple-element.235.refs_0_), channel_id=1, source_target_pairs={{4,0},{6,2},{0,4},{2,6},{5,1},{7,3},{1,5},{3,7},{12,8},{14,10},{8,... | collective-permute-start | bytes 1572872 | tf_op jit(solution)/shard_map/ppermute | solution.py:29
  252.4 139.9 %reduce-scatter.5.cloned.1.call-start = ((), (), s32[]{:S(2)}) async-start(), calls=%async_computation.8 | async-start | bytes 4718592 | tf_op jit(solution)/shard_map/reduce_scatter | solution.py:851
  275.3 25.0 %collective-permute-start.40 = (bf16[128,2048]{1,0:T(8,128)(2,1)S(1)}, bf16[128,2048]{1,0:T(8,128)(2,1)S(1)}, u32[]{:S(2)}, u32[]{:S(2)}) collective-permute-start(bf16[128,2048]{1,0:T(8,128)(2,1)S(1)} %get-tuple-element.284.refs_0_), channel_id=1, source_target_pairs={{6,0},{0,2},{2,4},{4,6},{7,1},{1,3},{3,5},{5,7},{14,8},{8,10},{10,... | collective-permute-start | bytes 1572872 | tf_op jit(solution)/shard_map/ppermute | solution.py:29
  275.5 24.8 %collective-permute-start.39 = (bf16[128,2048]{1,0:T(8,128)(2,1)S(1)}, bf16[128,2048]{1,0:T(8,128)(2,1)S(1)}, u32[]{:S(2)}, u32[]{:S(2)}) collective-permute-start(bf16[128,2048]{1,0:T(8,128)(2,1)S(1)} %get-tuple-element.284.refs_0_), channel_id=1, source_target_pairs={{4,0},{6,2},{0,4},{2,6},{5,1},{7,3},{1,5},{3,7},{12,8},{14,10},{8,... | collective-permute-start | bytes 1572872 | tf_op jit(solution)/shard_map/ppermute | solution.py:29
  277.5 23.4 %collective-permute-start.38 = (bf16[128,2048]{1,0:T(8,128)(2,1)S(1)}, bf16[128,2048]{1,0:T(8,128)(2,1)S(1)}, u32[]{:S(2)}, u32[]{:S(2)}) collective-permute-start(bf16[128,2048]{1,0:T(8,128)(2,1)S(1)} %get-tuple-element.284.refs_0_), channel_id=1, source_target_pairs={{2,0},{4,2},{6,4},{0,6},{3,1},{5,3},{7,5},{1,7},{10,8},{12,10},{14... | collective-permute-start | bytes 1572872 | tf_op jit(solution)/shard_map/ppermute | solution.py:29
  307.4 30.4 %collective-permute-start.44 = (bf16[128,2048]{1,0:T(8,128)(2,1)}, bf16[128,2048]{1,0:T(8,128)(2,1)}, u32[]{:S(2)}, u32[]{:S(2)}) collective-permute-start(bf16[128,2048]{1,0:T(8,128)(2,1)} %get-tuple-element.293), channel_id=1, source_target_pairs={{6,0},{0,2},{2,4},{4,6},{7,1},{1,3},{3,5},{5,7},{14,8},{8,10},{10,... | collective-permute-start | bytes 1572872 | tf_op jit(solution)/shard_map/ppermute | solution.py:29
  307.6 30.2 %collective-permute-start.45 = (bf16[128,2048]{1,0:T(8,128)(2,1)}, bf16[128,2048]{1,0:T(8,128)(2,1)}, u32[]{:S(2)}, u32[]{:S(2)}) collective-permute-start(bf16[128,2048]{1,0:T(8,128)(2,1)} %get-tuple-element.294), channel_id=1, source_target_pairs={{4,0},{6,2},{0,4},{2,6},{5,1},{7,3},{1,5},{3,7},{12,8},{14,10},{8,... | collective-permute-start | bytes 1572872 | tf_op jit(solution)/shard_map/ppermute | solution.py:29
  311.2 26.6 %collective-permute-start.46 = (bf16[128,2048]{1,0:T(8,128)(2,1)}, bf16[128,2048]{1,0:T(8,128)(2,1)}, u32[]{:S(2)}, u32[]{:S(2)}) collective-permute-start(bf16[128,2048]{1,0:T(8,128)(2,1)} %get-tuple-element.295), channel_id=1, source_target_pairs={{2,0},{4,2},{6,4},{0,6},{3,1},{5,3},{7,5},{1,7},{10,8},{12,10},{14... | collective-permute-start | bytes 1572872 | tf_op jit(solution)/shard_map/ppermute | solution.py:29
  364.1 40.7 %collective-permute-start.48 = (bf16[128,2048]{1,0:T(8,128)(2,1)}, bf16[128,2048]{1,0:T(8,128)(2,1)S(1)}, u32[]{:S(2)}, u32[]{:S(2)}) collective-permute-start(bf16[128,2048]{1,0:T(8,128)(2,1)} %get-tuple-element.303), channel_id=1, source_target_pairs={{6,0},{0,2},{2,4},{4,6},{7,1},{1,3},{3,5},{5,7},{14,8},{8,10},{10,... | collective-permute-start | bytes 1572872 | tf_op jit(solution)/shard_map/ppermute | solution.py:29
  364.7 40.1 %collective-permute-start.49 = (bf16[128,2048]{1,0:T(8,128)(2,1)}, bf16[128,2048]{1,0:T(8,128)(2,1)}, u32[]{:S(2)}, u32[]{:S(2)}) collective-permute-start(bf16[128,2048]{1,0:T(8,128)(2,1)} %get-tuple-element.304), channel_id=1, source_target_pairs={{4,0},{6,2},{0,4},{2,6},{5,1},{7,3},{1,5},{3,7},{12,8},{14,10},{8,... | collective-permute-start | bytes 1572872 | tf_op jit(solution)/shard_map/ppermute | solution.py:29
  367.0 37.8 %collective-permute-start.50 = (bf16[128,2048]{1,0:T(8,128)(2,1)}, bf16[128,2048]{1,0:T(8,128)(2,1)}, u32[]{:S(2)}, u32[]{:S(2)}) collective-permute-start(bf16[128,2048]{1,0:T(8,128)(2,1)} %get-tuple-element.305), channel_id=1, source_target_pairs={{2,0},{4,2},{6,4},{0,6},{3,1},{5,3},{7,5},{1,7},{10,8},{12,10},{14... | collective-permute-start | bytes 1572872 | tf_op jit(solution)/shard_map/ppermute | solution.py:29
  367.6 37.1 %collective-permute-start.51 = (bf16[8,16,1536]{2,1,0:T(8,128)(2,1)S(1)}, bf16[8,16,1536]{2,1,0:T(8,128)(2,1)}, u32[]{:S(2)}, u32[]{:S(2)}) collective-permute-start(bf16[8,16,1536]{2,1,0:T(8,128)(2,1)S(1)} %all-to-all-done.3.here_ref), channel_id=1, source_target_pairs={{64,0},{0,64},{65,1},{1,65},{66,2},{2,66},{67,3},{3,67},{68,4},{4,... | collective-permute-start | bytes 1179656 | tf_op jit(solution)/shard_map/ppermute | solution.py:29
  368.3 36.5 %collective-permute-start.52 = (bf16[48,2048]{1,0:T(8,128)(2,1)S(1)}, bf16[48,2048]{1,0:T(8,128)(2,1)}, u32[]{:S(2)}, u32[]{:S(2)}) collective-permute-start(bf16[48,2048]{1,0:T(8,128)(2,1)S(1)} %maximum_maximum_fusion), channel_id=1, source_target_pairs={{64,0},{0,64},{65,1},{1,65},{66,2},{2,66},{67,3},{3,67},{68,4},{4,... | collective-permute-start | bytes 589832 | tf_op jit(solution)/shard_map/ppermute | solution.py:29
  406.8 33.1 %all-to-all-start.4 = ((bf16[16,32,768]{2,1,0:T(8,128)(2,1)}), bf16[16,32,768]{2,1,0:T(8,128)(2,1)S(1)}, u32[]{:S(2)}, u32[]{:S(2)}) async-start(bf16[16,32,768]{2,1,0:T(8,128)(2,1)} %pad_maximum_fusion.1), calls=%async_computation.6 | async-start | bytes 1572864 | tf_op jit(solution)/shard_map/all_to_all | solution.py:865
  413.8 21.2 %collective-permute-start.54 = (bf16[8,32,256]{2,1,0:T(8,128)(2,1)}, bf16[8,32,256]{2,1,0:T(8,128)(2,1)S(1)}, u32[]{:S(2)}, u32[]{:S(2)}) collective-permute-start(bf16[8,32,256]{2,1,0:T(8,128)(2,1)} %bitcast.16), channel_id=1, source_target_pairs={{0,64},{1,72},{2,80},{3,88},{4,96},{5,104},{6,112},{7,120},{8,65},... | collective-permute-start | bytes 393224 | tf_op jit(solution)/shard_map/ppermute | solution.py:41
  (136 other events, 1063.5 us)
Sparse Core Ops, SparseCore 0:
  96.0 103.5 all-gather.2
  252.5 85.2 reduce-scatter.2
  340.3 51.9 reduce-scatter.4

commit v5 on v4

--- a/solution.py
+++ b/solution.py
@@ -790,7 +790,7 @@
     attn, attn_there, pairs, x_mine, x_other, dy, gate_up_piece = lax.optimization_barrier(
         (attn, attn_there, pairs, x_mine, x_other, dy, gate_up_piece)
     )
-    dy_mine = [dy, from_ahead(dy, "z", 1), None, from_ahead(dy, "z", 3)]
+    dy_mine = z_gather(dy)
     x_blocks = x_mine + x_other
     halo = along_line(lax.select_n(last_spot, *[block[BLOCK - WIN :] for block in x_blocks]), 1)
     feed_piece = jnp.concatenate([gate_up_piece, down_piece], axis=0)
@@ -801,8 +801,7 @@
     normed = normalised(x_blocks, gain_rows)
     gain_one, gain_two = gain_rows[:1], gain_rows[1:2]
     qkv = matmul(normed, w_qkv).astype(low)
-    qkv, dy_mine, halo = lax.optimization_barrier((qkv, dy_mine, halo))
-    dy_mine[2] = from_ahead(dy_mine[0], "z", 2)
+    qkv, halo = lax.optimization_barrier((qkv, halo))
     halo = halo.astype(full)
     halo = matmul((halo * inverse_rms(halo) * gain_one).astype(low), w_qkv[:, team_wide:]).astype(low)
     mixed = attend(place, qkv, halo, mask)

time: 457 us -> 464 us (1.015)
  the two profiles are of different devices: /device:TPU:14 before, /device:TPU:8 now
where the time goes in v5:
time: 464 us; the launch traced here: 456 us
  waiting for transfers between devices  169 us (36%)
  starting transfers between devices  95.8 us (21%)
  Pallas kernels  94.4 us (20%)
  local copies, waits for them, and re-layouts  56.7 us (12%)
  between operations  15.4 us (3%)
  matrix products  12.5 us (3%)
  other arithmetic  12 us (3%)
    ppermute x50, waiting for transfers between devices, from_ahead(): return lax.ppermute(value, axis, [((i + by) % n, i) for i in range(n)])  131 us
    ppermute x50, starting transfers between devices, from_ahead(): return lax.ppermute(value, axis, [((i + by) % n, i) for i in range(n)])  54.4 us
    unnamed x210, local copies, waits for them, and re-layouts  47.1 us
    pallas_call x2, Pallas kernels, feed(): pl.pallas_call(feed_kernel, grid=(tiles,), in_specs=[pl.BlockSpec(memory_...  14.8 us
    pallas_call x1, Pallas kernels, feed_terms(): pl.pallas_call(terms_kernel, grid=(N_FLEET,), in_specs=[cut] * 2 + [whole...  13.4 us
    ppermute x3, starting transfers between devices, swapped(): lax.ppermute(value, ALL, [(g * n + a, (g ^ across) * n + b) for g in rang...  12.5 us
    reduce_scatter x1, waiting for transfers between devices, body(): lax.psum_scatter(attn_term, FLEET, scatter_dimension=0, tiled=True)  11.9 us
    pallas_call x1, Pallas kernels, attend_back(): pl.pallas_call(attend_back_kernel, grid_spec=pltpu.PrefetchScalarGridSpec...  11.9 us
  transfers between devices with their start and end apart: 63, of which 24 were waited for; matrix products, arithmetic and copies ran while one was open for 6% of the time, Pallas kernels for 18%

profile of v5, /device:TPU:8, one launch (start us, length us, event | category | flops | bytes accessed | tf_op | source)
XLA Modules:
  0.0 455.8 jit_solution(18063653713723390888)
XLA Ops:
  20.4 4.4 all-to-all-start
  26.4 8.7 %all-to-all-done = bf16[8,32,896]{2,1,0:T(8,128)(2,1)S(1)} async-done(((bf16[8,32,896]{2,1,0:T(8,128)(2,1)}), bf16[8,32,896]{2,1,0:T(8,128)(2,1)S(1)}, u32[]{:S(2)}, u32[]{:S(2)}) %all-to-all-start) | async-done | bytes 458784 | tf_op jit(solution)/shard_map/all_to_all | solution.py:767
  37.3 3.7 all-to-all-start.1
  67.2 4.2 all-to-all-start.2
  74.5 10.1 %collective-permute-done.12.refs_2_ = bf16[512,384]{1,0:T(8,128)(2,1)S(1)} collective-permute-done((bf16[512,384]{1,0:T(8,128)(2,1)S(1)}, bf16[512,384]{1,0:T(8,128)(2,1)S(1)}, u32[]{:S(2)}, u32[]{:S(2)}) %collective-permute-start.12) | collective-permute-done | bytes 393248 | tf_op jit(solution)/shard_map/ppermute | solution.py:29
  85.4 7.7 %collective-permute-done.11.refs_1_ = bf16[512,384]{1,0:T(8,128)(2,1)S(1)} collective-permute-done((bf16[512,384]{1,0:T(8,128)(2,1)S(1)}, bf16[512,384]{1,0:T(8,128)(2,1)S(1)}, u32[]{:S(2)}, u32[]{:S(2)}) %collective-permute-start.11) | collective-permute-done | bytes 393248 | tf_op jit(solution)/shard_map/ppermute | solution.py:29
  113.1 7.8 %shard_map.208.mixed_ref = bf16[1024,256]{1,0:T(8,128)(2,1)S(1)} custom-call(s32[16]{0:T(128)S(1)} %pad_add_fusion.place, bf16[1024,768]{1,0:T(8,128)(2,1)S(1)} %convolution_convert_fusion.2.q_ref.k_ref.v_ref.kp_ref.vp_ref, bf16[1024,768]{1,0:T(8,128)(2,1)S(1)} %convolution_convert_fusion.2.q_ref.k_ref.v_ref.kp_ref.vp_ref, ...), custom_call_target="tpu_custom_call" | custom-call | flops 1 | bytes 1 | tf_op jit(solution)/shard_map/pallas_call | solution.py:541
  129.4 8.0 %collective-permute-done.19.refs_7_ = bf16[128,2048]{1,0:T(8,128)(2,1)S(1)} collective-permute-done((bf16[128,2048]{1,0:T(8,128)(2,1)S(1)}, bf16[128,2048]{1,0:T(8,128)(2,1)S(1)}, u32[]{:S(2)}, u32[]{:S(2)}) %collective-permute-start.19) | collective-permute-done | bytes 524320 | tf_op jit(solution)/shard_map/ppermute | solution.py:29
  137.4 12.4 %collective-permute-done.18.refs_6_ = bf16[128,2048]{1,0:T(8,128)(2,1)S(1)} collective-permute-done((bf16[128,2048]{1,0:T(8,128)(2,1)S(1)}, bf16[128,2048]{1,0:T(8,128)(2,1)S(1)}, u32[]{:S(2)}, u32[]{:S(2)}) %collective-permute-start.18) | collective-permute-done | bytes 524320 | tf_op jit(solution)/shard_map/ppermute | solution.py:29
  155.7 8.6 %collective-permute-done.20.refs_1_ = bf16[128,2048]{1,0:T(8,128)(2,1)S(1)} collective-permute-done((bf16[128,2048]{1,0:T(8,128)(2,1)S(1)}, bf16[128,2048]{1,0:T(8,128)(2,1)S(1)}, u32[]{:S(2)}, u32[]{:S(2)}) %collective-permute-start.20) | collective-permute-done | bytes 524320 | tf_op jit(solution)/shard_map/ppermute | solution.py:29
  164.3 12.2 %collective-permute-done.21.refs_2_ = bf16[128,2048]{1,0:T(8,128)(2,1)S(1)} collective-permute-done((bf16[128,2048]{1,0:T(8,128)(2,1)S(1)}, bf16[128,2048]{1,0:T(8,128)(2,1)S(1)}, u32[]{:S(2)}, u32[]{:S(2)}) %collective-permute-start.21) | collective-permute-done | bytes 524320 | tf_op jit(solution)/shard_map/ppermute | solution.py:29
  185.7 11.3 %collective-permute-done.29.refs_3_ = bf16[128,2048]{1,0:T(8,128)(2,1)S(1)} collective-permute-done((bf16[128,2048]{1,0:T(8,128)(2,1)S(1)}, bf16[128,2048]{1,0:T(8,128)(2,1)S(1)}, u32[]{:S(2)}, u32[]{:S(2)}) %collective-permute-start.29) | collective-permute-done | bytes 524320 | tf_op jit(solution)/shard_map/ppermute | solution.py:29
  197.8 9.1 %collective-permute-done.27.refs_1_ = bf16[128,2048]{1,0:T(8,128)(2,1)S(1)} collective-permute-done((bf16[128,2048]{1,0:T(8,128)(2,1)S(1)}, bf16[128,2048]{1,0:T(8,128)(2,1)S(1)}, u32[]{:S(2)}, u32[]{:S(2)}) %collective-permute-start.27) | collective-permute-done | bytes 524320 | tf_op jit(solution)/shard_map/ppermute | solution.py:29
  210.7 3.7 copy-done.4
  217.1 7.4 %shard_map.214 = (bf16[512,768]{1,0:T(8,128)(2,1)S(1)}, bf16[512,768]{1,0:T(8,128)(2,1)S(1)}, bf16[512,768]{1,0:T(8,128)(2,1)S(1)}, bf16[512,2048]{1,0:T(8,128)(2,1)S(1)}, bf16[512,2048]{1,0:T(8,128)(2,1)S(1)}) custom-call(bf16[128,2048]{1,0:T(8,128)(2,1)S(1)} %copy-done.73, bf16[128,2048]{1,0:T(8,128)(2,1)S(1)} %copy-done.77, ...), custom_call_target="tpu_custom_call" | custom-call | flops 1 | bytes 1 | tf_op jit(solution)/shard_map/pallas_call | solution.py:253
  224.6 4.2 shard_map.215
  228.9 7.4 %shard_map.212 = (bf16[512,768]{1,0:T(8,128)(2,1)S(1)}, bf16[512,768]{1,0:T(8,128)(2,1)S(1)}, bf16[512,768]{1,0:T(8,128)(2,1)S(1)}, bf16[512,2048]{1,0:T(8,128)(2,1)S(1)}, bf16[512,2048]{1,0:T(8,128)(2,1)S(1)}) custom-call(bf16[128,2048]{1,0:T(8,128)(2,1)S(1)} %copy-done.65, bf16[128,2048]{1,0:T(8,128)(2,1)S(1)} %copy-done.71, ...), custom_call_target="tpu_custom_call" | custom-call | flops 1 | bytes 1 | tf_op jit(solution)/shard_map/pallas_call | solution.py:253
  236.4 4.3 shard_map.213.here_ref
  246.5 13.4 %shard_map.217 = bf16[2,8,192,1536]{3,2,1,0:T(8,128)(2,1)} custom-call(bf16[512,2048]{1,0:T(8,128)(2,1)S(1)} %get-tuple-element.259.x0_ref, bf16[512,2048]{1,0:T(8,128)(2,1)S(1)} %get-tuple-element.260.x1_ref, bf16[512,2048]{1,0:T(8,128)(2,1)S(1)} %get-tuple-element.261.dy0_ref, bf16[512,2048]{1,0:T(8,128)(2,1)S(1)} %get-tuple-element.262.dy1_ref, ...), custom_call_target="tpu_custom_call" | custom-call | flops 10000000000 | bytes 20000000 | tf_op jit(solution)/shard_map/pallas_call | solution.py:392
  263.3 14.2 %collective-permute-done.37.refs_2_ = bf16[128,2048]{1,0:T(8,128)(2,1)S(1)} collective-permute-done((bf16[128,2048]{1,0:T(8,128)(2,1)}, bf16[128,2048]{1,0:T(8,128)(2,1)S(1)}, u32[]{:S(2)}, u32[]{:S(2)}) %collective-permute-start.37) | collective-permute-done | bytes 524320 | tf_op jit(solution)/shard_map/ppermute | solution.py:29
  290.6 4.6 %shard_map.219 = (f32[512,2048]{1,0:T(8,128)S(1)}, bf16[512,2048]{1,0:T(8,128)(2,1)S(1)}) custom-call(bf16[512,768]{1,0:T(8,128)(2,1)S(1)} %copy-done.51, bf16[512,768]{1,0:T(8,128)(2,1)S(1)} %copy-done.49, bf16[768,2048]{1,0:T(8,128)(2,1)S(1)} %copy-done.1), custom_call_target="tpu_custom_call" | custom-call | flops 1 | bytes 1 | tf_op jit(solution)/shard_map/pallas_call | solution.py:414
  295.1 15.9 %collective-permute-done.40.refs_3_ = bf16[128,2048]{1,0:T(8,128)(2,1)S(1)} collective-permute-done((bf16[128,2048]{1,0:T(8,128)(2,1)S(1)}, bf16[128,2048]{1,0:T(8,128)(2,1)S(1)}, u32[]{:S(2)}, u32[]{:S(2)}) %collective-permute-start.40) | collective-permute-done | bytes 524320 | tf_op jit(solution)/shard_map/ppermute | solution.py:29
  325.3 4.9 %collective-permute-start.42 = (bf16[64,512]{1,0:T(8,128)(2,1)S(1)}, bf16[64,512]{1,0:T(8,128)(2,1)S(1)}, u32[]{:S(2)}, u32[]{:S(2)}) collective-permute-start(bf16[64,512]{1,0:T(8,128)(2,1)S(1)} %shard_map.222), channel_id=1, source_target_pairs={{8,0},{16,8},{24,16},{32,24},{40,32},{48,40},{56,48},{9,1},{17,9},... | collective-permute-start | bytes 196616 | tf_op jit(solution)/shard_map/ppermute | solution.py:33
  331.3 11.9 %shard_map.221 = (bf16[1024,768]{1,0:T(8,128)(2,1)S(1)}, f32[64,512]{1,0:T(8,128)S(1)}) custom-call(s32[16]{0:T(128)S(1)} %pad_add_fusion.place, bf16[1024,768]{1,0:T(8,128)(2,1)S(1)} %convolution_convert_fusion.2.q_ref.k_ref.v_ref.kp_ref.vp_ref, bf16[1024,768]{1,0:T(8,128)(2,1)S(1)} %convolution_convert_fusion.2.q_ref.k_ref.v_ref.kp_ref.vp_ref, ...), custom_call_target="tpu_custom_call" | custom-call | flops 1 | bytes 1 | tf_op jit(solution)/shard_map/pallas_call | solution.py:560
  343.2 8.0 %shard_map.223 = bf16[2048,1024]{1,0:T(8,128)(2,1)} custom-call(bf16[1024,2048]{1,0:T(8,128)(2,1)S(1)} %copy-done.3, bf16[1024,768]{1,0:T(8,128)(2,1)S(1)} %fusion.22.grad_ref, bf16[1024,256]{1,0:T(8,128)(2,1)S(1)} %copy-done.9, bf16[512,2048]{1,0:T(8,128)(2,1)S(1)} %copy-done.6, bf16[512,2048]{1,0:T(8,128)(2,1)S(1)} %copy-done.19), custom_call_target="tpu_custom_call" | custom-call | flops 1 | bytes 1 | tf_op jit(solution)/shard_map/pallas_call | solution.py:601
  353.8 3.9 convolution_convert_fusion.1
  370.8 7.9 %all-to-all-done.3.here_ref = bf16[8,16,1536]{2,1,0:T(8,128)(2,1)S(1)} async-done(((bf16[8,16,1536]{2,1,0:T(8,128)(2,1)}), bf16[8,16,1536]{2,1,0:T(8,128)(2,1)S(1)}, u32[]{:S(2)}, u32[]{:S(2)}) %all-to-all-start.3) | async-done | bytes 393248 | tf_op jit(solution)/shard_map/all_to_all | solution.py:856
  389.4 11.9 %reduce-scatter.5.cloned.1.call-done = bf16[256,1024]{1,0:T(8,128)(2,1)} async-done(((bf16[2048,1024]{1,0:T(8,128)(2,1)}), bf16[256,1024]{1,0:T(8,128)(2,1)}) %reduce-scatter.5.cloned.1.call-update) | async-done | bytes 524304 | tf_op jit(solution)/shard_map/reduce_scatter | solution.py:850
  401.3 13.1 %collective-permute-done.52 = bf16[48,2048]{1,0:T(8,128)(2,1)} collective-permute-done((bf16[48,2048]{1,0:T(8,128)(2,1)S(1)}, bf16[48,2048]{1,0:T(8,128)(2,1)}, u32[]{:S(2)}, u32[]{:S(2)}) %collective-permute-start.52) | collective-permute-done | bytes 196640 | tf_op jit(solution)/shard_map/ppermute | solution.py:29
  416.4 5.4 %all-to-all-start.4 = ((bf16[16,32,768]{2,1,0:T(8,128)(2,1)}), bf16[16,32,768]{2,1,0:T(8,128)(2,1)S(1)}, u32[]{:S(2)}, u32[]{:S(2)}) async-start(bf16[16,32,768]{2,1,0:T(8,128)(2,1)} %pad_maximum_fusion.1), calls=%async_computation.6 | async-start | bytes 1572864 | tf_op jit(solution)/shard_map/all_to_all | solution.py:864
  423.6 4.3 collective-permute-start.54
  428.0 4.5 collective-permute-start.53
  (380 shorter events, 181.3 us)
Async XLA Ops:
  7.2 28.0 %collective-permute-start.2 = (bf16[128,2048]{1,0:T(8,128)(2,1)}, bf16[128,2048]{1,0:T(8,128)(2,1)S(1)}, u32[]{:S(2)}, u32[]{:S(2)}) collective-permute-start(bf16[128,2048]{1,0:T(8,128)(2,1)} %refs_4_.4), channel_id=1, source_target_pairs={{6,0},{0,2},{2,4},{4,6},{7,1},{1,3},{3,5},{5,7},{14,8},{8,10},{10,... | collective-permute-start | bytes 1572872 | tf_op jit(solution)/shard_map/ppermute | solution.py:29
  9.2 26.0 %collective-permute-start.1 = (bf16[128,2048]{1,0:T(8,128)(2,1)}, bf16[128,2048]{1,0:T(8,128)(2,1)S(1)}, u32[]{:S(2)}, u32[]{:S(2)}) collective-permute-start(bf16[128,2048]{1,0:T(8,128)(2,1)} %refs_4_.4), channel_id=1, source_target_pairs={{2,0},{4,2},{6,4},{0,6},{3,1},{5,3},{7,5},{1,7},{10,8},{12,10},{14... | collective-permute-start | bytes 1572872 | tf_op jit(solution)/shard_map/ppermute | solution.py:29
  37.3 24.0 %all-to-all-start.1 = ((bf16[4,256,768]{2,1,0:T(8,128)(2,1)}), bf16[4,256,768]{2,1,0:T(8,128)(2,1)S(1)}, u32[]{:S(2)}, u32[]{:S(2)}) async-start(bf16[4,256,768]{2,1,0:T(8,128)(2,1)} %broadcast_in_dim.18), calls=%async_computation.1 | async-start | bytes 3145728 | tf_op jit(solution)/shard_map/all_to_all | solution.py:774
  64.3 29.6 %collective-permute-start.10 = (bf16[512,768]{1,0:T(8,128)(2,1)}, bf16[512,768]{1,0:T(8,128)(2,1)}, u32[]{:S(2)}, u32[]{:S(2)}) collective-permute-start(bf16[512,768]{1,0:T(8,128)(2,1)} %get-tuple-element.331), channel_id=1, source_target_pairs={{96,0},{0,32},{32,64},{64,96},{97,1},{1,33},{33,65},{65,97},{98,2}... | collective-permute-start | bytes 2359304 | tf_op jit(solution)/shard_map/ppermute | solution.py:29
  67.2 26.6 %collective-permute-start.9 = (bf16[512,768]{1,0:T(8,128)(2,1)}, bf16[512,768]{1,0:T(8,128)(2,1)}, u32[]{:S(2)}, u32[]{:S(2)}) collective-permute-start(bf16[512,768]{1,0:T(8,128)(2,1)} %get-tuple-element.332), channel_id=1, source_target_pairs={{32,0},{64,32},{96,64},{0,96},{33,1},{65,33},{97,65},{1,97},{34,2}... | collective-permute-start | bytes 2359304 | tf_op jit(solution)/shard_map/ppermute | solution.py:29
  67.2 26.6 %all-to-all-start.2 = ((bf16[8,32,1536]{2,1,0:T(8,128)(2,1)}), bf16[8,32,1536]{2,1,0:T(8,128)(2,1)}, u32[]{:S(2)}, u32[]{:S(2)}) async-start(bf16[8,32,1536]{2,1,0:T(8,128)(2,1)} %copy-done.17), calls=%async_computation.2 | async-start | bytes 1572864 | tf_op jit(solution)/shard_map/all_to_all | solution.py:788
  71.5 139.2 %all-gather.3.cloned.1.call-start = ((), (), s32[]{:S(2)}) async-start(), calls=%async_computation.9 | async-start | bytes 10616832 | tf_op jit(solution)/shard_map/all_gather | solution.py:797
  71.5 22.4 %collective-permute-start.14 = (bf16[128,2048]{1,0:T(8,128)(2,1)}, bf16[128,2048]{1,0:T(8,128)(2,1)}, u32[]{:S(2)}, u32[]{:S(2)}) collective-permute-start(bf16[128,2048]{1,0:T(8,128)(2,1)} %collective-permute-done.5.refs_2_), channel_id=1, source_target_pairs={{1,0},{0,1},{3,2},{2,3},{5,4},{4,5},{7,6},{6,7},{9,8},{8,9},{11,10... | collective-permute-start | bytes 1572872 | tf_op jit(solution)/shard_map/ppermute | solution.py:29
  96.3 268.2 %reduce-scatter.3.cloned.1.call-start = ((), (), s32[]{:S(2)}) async-start(), calls=%async_computation.7 | async-start | bytes 10027008 | tf_op jit(solution)/shard_map/reduce_scatter | solution.py:831
  124.2 25.7 %collective-permute-start.18 = (bf16[128,2048]{1,0:T(8,128)(2,1)S(1)}, bf16[128,2048]{1,0:T(8,128)(2,1)S(1)}, u32[]{:S(2)}, u32[]{:S(2)}) collective-permute-start(bf16[128,2048]{1,0:T(8,128)(2,1)S(1)} %copy-done.20), channel_id=1, source_target_pairs={{4,0},{6,2},{0,4},{2,6},{5,1},{7,3},{1,5},{3,7},{12,8},{14,10},{8,... | collective-permute-start | bytes 1572872 | tf_op jit(solution)/shard_map/ppermute | solution.py:29
  126.7 23.1 %collective-permute-start.17 = (bf16[128,2048]{1,0:T(8,128)(2,1)S(1)}, bf16[128,2048]{1,0:T(8,128)(2,1)S(1)}, u32[]{:S(2)}, u32[]{:S(2)}) collective-permute-start(bf16[128,2048]{1,0:T(8,128)(2,1)S(1)} %copy-done.20), channel_id=1, source_target_pairs={{2,0},{4,2},{6,4},{0,6},{3,1},{5,3},{7,5},{1,7},{10,8},{12,10},{14... | collective-permute-start | bytes 1572872 | tf_op jit(solution)/shard_map/ppermute | solution.py:29
  151.0 25.5 %collective-permute-start.21 = (bf16[128,2048]{1,0:T(8,128)(2,1)S(1)}, bf16[128,2048]{1,0:T(8,128)(2,1)S(1)}, u32[]{:S(2)}, u32[]{:S(2)}) collective-permute-start(bf16[128,2048]{1,0:T(8,128)(2,1)S(1)} %get-tuple-element.218), channel_id=1, source_target_pairs={{4,0},{6,2},{0,4},{2,6},{5,1},{7,3},{1,5},{3,7},{12,8},{14,10},{8,... | collective-permute-start | bytes 1572872 | tf_op jit(solution)/shard_map/ppermute | solution.py:29
  153.4 23.2 %collective-permute-start.22 = (bf16[128,2048]{1,0:T(8,128)(2,1)S(1)}, bf16[128,2048]{1,0:T(8,128)(2,1)S(1)}, u32[]{:S(2)}, u32[]{:S(2)}) collective-permute-start(bf16[128,2048]{1,0:T(8,128)(2,1)S(1)} %get-tuple-element.219), channel_id=1, source_target_pairs={{2,0},{4,2},{6,4},{0,6},{3,1},{5,3},{7,5},{1,7},{10,8},{12,10},{14... | collective-permute-start | bytes 1572872 | tf_op jit(solution)/shard_map/ppermute | solution.py:29
  155.2 21.3 %collective-permute-start.23 = (bf16[128,2048]{1,0:T(8,128)(2,1)S(1)}, bf16[128,2048]{1,0:T(8,128)(2,1)S(1)}, u32[]{:S(2)}, u32[]{:S(2)}) collective-permute-start(bf16[128,2048]{1,0:T(8,128)(2,1)S(1)} %copy-done.20), channel_id=1, source_target_pairs={{1,0},{0,1},{3,2},{2,3},{5,4},{4,5},{7,6},{6,7},{9,8},{8,9},{11,10... | collective-permute-start | bytes 1572872 | tf_op jit(solution)/shard_map/ppermute | solution.py:29
  155.2 21.3 %collective-permute-start.24 = (bf16[128,2048]{1,0:T(8,128)(2,1)S(1)}, bf16[128,2048]{1,0:T(8,128)(2,1)S(1)}, u32[]{:S(2)}, u32[]{:S(2)}) collective-permute-start(bf16[128,2048]{1,0:T(8,128)(2,1)S(1)} %collective-permute-done.17.refs_5_), channel_id=1, source_target_pairs={{1,0},{0,1},{3,2},{2,3},{5,4},{4,5},{7,6},{6,7},{9,8},{8,9},{11,10... | collective-permute-start | bytes 1572872 | tf_op jit(solution)/shard_map/ppermute | solution.py:29
  182.0 24.9 %collective-permute-start.27 = (bf16[128,2048]{1,0:T(8,128)(2,1)S(1)}, bf16[128,2048]{1,0:T(8,128)(2,1)S(1)}, u32[]{:S(2)}, u32[]{:S(2)}) collective-permute-start(bf16[128,2048]{1,0:T(8,128)(2,1)S(1)} %get-tuple-element.229.refs_0_), channel_id=1, source_target_pairs={{2,0},{4,2},{6,4},{0,6},{3,1},{5,3},{7,5},{1,7},{10,8},{12,10},{14... | collective-permute-start | bytes 1572872 | tf_op jit(solution)/shard_map/ppermute | solution.py:29
  184.4 23.4 %collective-permute-start.30 = (bf16[128,2048]{1,0:T(8,128)(2,1)S(1)}, bf16[128,2048]{1,0:T(8,128)(2,1)S(1)}, u32[]{:S(2)}, u32[]{:S(2)}) collective-permute-start(bf16[128,2048]{1,0:T(8,128)(2,1)S(1)} %get-tuple-element.229.refs_0_), channel_id=1, source_target_pairs={{1,0},{0,1},{3,2},{2,3},{5,4},{4,5},{7,6},{6,7},{9,8},{8,9},{11,10... | collective-permute-start | bytes 1572872 | tf_op jit(solution)/shard_map/ppermute | solution.py:29
  184.4 24.2 %collective-permute-start.28 = (bf16[128,2048]{1,0:T(8,128)(2,1)S(1)}, bf16[128,2048]{1,0:T(8,128)(2,1)}, u32[]{:S(2)}, u32[]{:S(2)}) collective-permute-start(bf16[128,2048]{1,0:T(8,128)(2,1)S(1)} %get-tuple-element.229.refs_0_), channel_id=1, source_target_pairs={{4,0},{6,2},{0,4},{2,6},{5,1},{7,3},{1,5},{3,7},{12,8},{14,10},{8,... | collective-permute-start | bytes 1572872 | tf_op jit(solution)/shard_map/ppermute | solution.py:29
  261.4 139.8 %reduce-scatter.5.cloned.1.call-start = ((), (), s32[]{:S(2)}) async-start(), calls=%async_computation.8 | async-start | bytes 4718592 | tf_op jit(solution)/shard_map/reduce_scatter | solution.py:850
  285.3 25.7 %collective-permute-start.40 = (bf16[128,2048]{1,0:T(8,128)(2,1)S(1)}, bf16[128,2048]{1,0:T(8,128)(2,1)S(1)}, u32[]{:S(2)}, u32[]{:S(2)}) collective-permute-start(bf16[128,2048]{1,0:T(8,128)(2,1)S(1)} %get-tuple-element.278.refs_0_), channel_id=1, source_target_pairs={{6,0},{0,2},{2,4},{4,6},{7,1},{1,3},{3,5},{5,7},{14,8},{8,10},{10,... | collective-permute-start | bytes 1572872 | tf_op jit(solution)/shard_map/ppermute | solution.py:29
  285.3 25.7 %collective-permute-start.39 = (bf16[128,2048]{1,0:T(8,128)(2,1)S(1)}, bf16[128,2048]{1,0:T(8,128)(2,1)S(1)}, u32[]{:S(2)}, u32[]{:S(2)}) collective-permute-start(bf16[128,2048]{1,0:T(8,128)(2,1)S(1)} %get-tuple-element.278.refs_0_), channel_id=1, source_target_pairs={{4,0},{6,2},{0,4},{2,6},{5,1},{7,3},{1,5},{3,7},{12,8},{14,10},{8,... | collective-permute-start | bytes 1572872 | tf_op jit(solution)/shard_map/ppermute | solution.py:29
  288.5 23.1 %collective-permute-start.38 = (bf16[128,2048]{1,0:T(8,128)(2,1)S(1)}, bf16[128,2048]{1,0:T(8,128)(2,1)S(1)}, u32[]{:S(2)}, u32[]{:S(2)}) collective-permute-start(bf16[128,2048]{1,0:T(8,128)(2,1)S(1)} %get-tuple-element.278.refs_0_), channel_id=1, source_target_pairs={{2,0},{4,2},{6,4},{0,6},{3,1},{5,3},{7,5},{1,7},{10,8},{12,10},{14... | collective-permute-start | bytes 1572872 | tf_op jit(solution)/shard_map/ppermute | solution.py:29
  318.1 34.3 %collective-permute-start.44 = (bf16[128,2048]{1,0:T(8,128)(2,1)}, bf16[128,2048]{1,0:T(8,128)(2,1)}, u32[]{:S(2)}, u32[]{:S(2)}) collective-permute-start(bf16[128,2048]{1,0:T(8,128)(2,1)} %get-tuple-element.287), channel_id=1, source_target_pairs={{6,0},{0,2},{2,4},{4,6},{7,1},{1,3},{3,5},{5,7},{14,8},{8,10},{10,... | collective-permute-start | bytes 1572872 | tf_op jit(solution)/shard_map/ppermute | solution.py:29
  319.0 33.5 %collective-permute-start.45 = (bf16[128,2048]{1,0:T(8,128)(2,1)}, bf16[128,2048]{1,0:T(8,128)(2,1)}, u32[]{:S(2)}, u32[]{:S(2)}) collective-permute-start(bf16[128,2048]{1,0:T(8,128)(2,1)} %get-tuple-element.288), channel_id=1, source_target_pairs={{4,0},{6,2},{0,4},{2,6},{5,1},{7,3},{1,5},{3,7},{12,8},{14,10},{8,... | collective-permute-start | bytes 1572872 | tf_op jit(solution)/shard_map/ppermute | solution.py:29
  322.2 30.2 %collective-permute-start.46 = (bf16[128,2048]{1,0:T(8,128)(2,1)}, bf16[128,2048]{1,0:T(8,128)(2,1)}, u32[]{:S(2)}, u32[]{:S(2)}) collective-permute-start(bf16[128,2048]{1,0:T(8,128)(2,1)} %get-tuple-element.289), channel_id=1, source_target_pairs={{2,0},{4,2},{6,4},{0,6},{3,1},{5,3},{7,5},{1,7},{10,8},{12,10},{14... | collective-permute-start | bytes 1572872 | tf_op jit(solution)/shard_map/ppermute | solution.py:29
  378.7 35.7 %collective-permute-start.48 = (bf16[128,2048]{1,0:T(8,128)(2,1)}, bf16[128,2048]{1,0:T(8,128)(2,1)S(1)}, u32[]{:S(2)}, u32[]{:S(2)}) collective-permute-start(bf16[128,2048]{1,0:T(8,128)(2,1)} %get-tuple-element.297), channel_id=1, source_target_pairs={{6,0},{0,2},{2,4},{4,6},{7,1},{1,3},{3,5},{5,7},{14,8},{8,10},{10,... | collective-permute-start | bytes 1572872 | tf_op jit(solution)/shard_map/ppermute | solution.py:29
  379.3 35.1 %collective-permute-start.49 = (bf16[128,2048]{1,0:T(8,128)(2,1)}, bf16[128,2048]{1,0:T(8,128)(2,1)}, u32[]{:S(2)}, u32[]{:S(2)}) collective-permute-start(bf16[128,2048]{1,0:T(8,128)(2,1)} %get-tuple-element.298), channel_id=1, source_target_pairs={{4,0},{6,2},{0,4},{2,6},{5,1},{7,3},{1,5},{3,7},{12,8},{14,10},{8,... | collective-permute-start | bytes 1572872 | tf_op jit(solution)/shard_map/ppermute | solution.py:29
  381.3 33.1 %collective-permute-start.50 = (bf16[128,2048]{1,0:T(8,128)(2,1)}, bf16[128,2048]{1,0:T(8,128)(2,1)}, u32[]{:S(2)}, u32[]{:S(2)}) collective-permute-start(bf16[128,2048]{1,0:T(8,128)(2,1)} %get-tuple-element.299), channel_id=1, source_target_pairs={{2,0},{4,2},{6,4},{0,6},{3,1},{5,3},{7,5},{1,7},{10,8},{12,10},{14... | collective-permute-start | bytes 1572872 | tf_op jit(solution)/shard_map/ppermute | solution.py:29
  382.0 32.5 %collective-permute-start.51 = (bf16[8,16,1536]{2,1,0:T(8,128)(2,1)S(1)}, bf16[8,16,1536]{2,1,0:T(8,128)(2,1)}, u32[]{:S(2)}, u32[]{:S(2)}) collective-permute-start(bf16[8,16,1536]{2,1,0:T(8,128)(2,1)S(1)} %all-to-all-done.3.here_ref), channel_id=1, source_target_pairs={{64,0},{0,64},{65,1},{1,65},{66,2},{2,66},{67,3},{3,67},{68,4},{4,... | collective-permute-start | bytes 1179656 | tf_op jit(solution)/shard_map/ppermute | solution.py:29
  382.0 32.5 %collective-permute-start.52 = (bf16[48,2048]{1,0:T(8,128)(2,1)S(1)}, bf16[48,2048]{1,0:T(8,128)(2,1)}, u32[]{:S(2)}, u32[]{:S(2)}) collective-permute-start(bf16[48,2048]{1,0:T(8,128)(2,1)S(1)} %maximum_maximum_fusion), channel_id=1, source_target_pairs={{64,0},{0,64},{65,1},{1,65},{66,2},{2,66},{67,3},{3,67},{68,4},{4,... | collective-permute-start | bytes 589832 | tf_op jit(solution)/shard_map/ppermute | solution.py:29
  416.4 29.8 %all-to-all-start.4 = ((bf16[16,32,768]{2,1,0:T(8,128)(2,1)}), bf16[16,32,768]{2,1,0:T(8,128)(2,1)S(1)}, u32[]{:S(2)}, u32[]{:S(2)}) async-start(bf16[16,32,768]{2,1,0:T(8,128)(2,1)} %pad_maximum_fusion.1), calls=%async_computation.6 | async-start | bytes 1572864 | tf_op jit(solution)/shard_map/all_to_all | solution.py:864
  423.6 22.6 %collective-permute-start.54 = (bf16[8,32,256]{2,1,0:T(8,128)(2,1)}, bf16[8,32,256]{2,1,0:T(8,128)(2,1)S(1)}, u32[]{:S(2)}, u32[]{:S(2)}) collective-permute-start(bf16[8,32,256]{2,1,0:T(8,128)(2,1)} %bitcast.16), channel_id=1, source_target_pairs={{0,64},{1,72},{2,80},{3,88},{4,96},{5,104},{6,112},{7,120},{8,65},... | collective-permute-start | bytes 393224 | tf_op jit(solution)/shard_map/ppermute | solution.py:41
  (136 other events, 1026.8 us)
Sparse Core Ops, SparseCore 0:
  96.4 103.1 all-gather.2
  261.6 85.4 reduce-scatter.2
  352.6 48.6 reduce-scatter.4
